TPU v7x, 32 devices: a whole 2x2x4 slice. The times are simulated.
32 devices in a mesh: row: 4 (over y, core), col: 8 (over z, x).
Axes of the slice: x: 2, y: 2, z: 4, core: 2. Of those that a mesh axis runs over, the one named last changes fastest.
Arguments:
- jac_tiles: bfloat16 [4096, 128, 128], P(('row', 'col')), may hold values from -0.0625 to 0.0625
- tile_pose: int32 [4096], P(('row', 'col')), may hold values from 0 to 63, as said below
- tile_point: int32 [4096], P(('row', 'col')), may hold values from 0 to 15
- tile_valid: int32 [4096], P(('row', 'col')), may hold values 0 or 1
- prior_weight: float32 [64, 128], P(('row', 'col')), may hold values from 0.1 to 1
- right_side: float32 [64, 128, 128], P(('row', 'col')), may hold values from -6 to 6
Outputs:
- solution: float32 [64, 128, 128], P(('row', 'col'))
- residual: float32 [64, 128, 128], P(('row', 'col'))
Inputs may be any that keep to these rules, and one draw needn't show every extreme that they name: `tile_pose`: entry t belongs to device t // 128; pose block (a multi-camera rig's poses at one time step) k is held by device k // 2. On each device, all entries that name blocks of one holding device name the same one of its two blocks.
All inputs are finite; a program needn't handle non-finite values. No bound on the sum of `tile_valid` on one device may be relied on, other than what follows from the above.
Results may differ from a plain program's by a relative error of at most 0.0055.
Values may be sent and summed in bfloat16 or wider, within the bound.
No kernel may reach another device: no remote copies, remote signals or barrier semaphores. Data moves between devices by JAX's collectives and lax.ppermute only.
A program may use at most 128 MiB of HBM per device.

v0:
```python
import functools
import math

import jax
import jax.numpy as jnp
from jax import lax
from jax.experimental import pallas as pl
from jax.experimental.pallas import tpu as pltpu
from jax.sharding import PartitionSpec as P

PT_DEV = 16
ITERS = 3
CORES = 2
UNROLL = 8
AREAS = 2
NEAR = 2 * AREAS

damping = 0.5
lowest = 0.5
highest = 8.0
BOTH = ("row", "col")
ONE, TWO, BOTH_AXES = ("x", "y"), ("y", "x"), "x y"


class Grid:
    def __init__(self):
        rows = lax.axis_size("row")
        cols = lax.axis_size("col")
        self.sizes = {"y": rows // CORES, "core": CORES, "z": cols // 2, "x": 2}
        self.count = rows * cols
        self.plane = self.sizes["z"] * CORES * 2

    def coords(self, device):
        cols = self.sizes["z"] * 2
        if isinstance(device, int):
            row, col = device // cols, device % cols
            return {"y": row // 2, "core": row % 2, "z": col // 2, "x": col % 2}
        row, col = lax.div(device, cols), lax.rem(device, cols)
        return {"y": lax.div(row, 2), "core": lax.rem(row, 2), "z": lax.div(col, 2), "x": lax.rem(col, 2)}

    def device(self, at):
        row = at["y"] * 2 + at["core"]
        col = at["z"] * 2 + at["x"]
        return row * self.sizes["z"] * 2 + col

    def spot(self, pose, home):
        at, base = self.coords(lax.div(pose, 2)), self.coords(home)
        away = {a: lax.rem(at[a] - base[a] + n, n) for a, n in self.sizes.items()}
        x, y, z = away["x"], away["y"], at["z"] ^ base["z"]
        if self.sizes["y"] == 2:
            swap = base["core"] == 1
            x, y = jnp.where(swap, y, x), jnp.where(swap, x, y)
        z = jnp.where(z == 0, 0, self.sizes["z"] - z)
        chip = (y * 2 + x) * self.sizes["z"] + z
        spot = (chip * CORES + at["core"]) * 2 + lax.rem(pose, 2)
        area = jnp.where(spot < self.plane, 0, 1)
        return area, spot - area * self.plane

    def send(self, block, axes, distance):
        route = []
        for source in range(self.count):
            at = self.coords(source)
            names = axes if isinstance(axes, str) else axes[at["core"]]
            for name in names.split():
                moved = (at[name] + distance) % self.sizes[name]
                at[name] = at[name] ^ distance if name == "z" else moved
            route.append((source, self.device(at)))
        return lax.ppermute(block, BOTH, route)

    def fetch(self, block, axes, distance):
        return self.send(block, axes, -distance)

    def swap(self, block):
        return self.send(block, "core", 1)


def along_z(grid, block):
    depth = grid.sizes["z"]
    moved = [grid.send(block, "z", r) for r in range(1, depth)]
    return jnp.concatenate([block] + moved[::-1])


def gather_field(grid, low, plan, load):
    wide = grid.sizes["y"]
    base = along_z(grid, low)
    if wide == 2:
        corner = grid.send(low, BOTH_AXES, 1)
        base, corner, plan = lax.optimization_barrier((base, corner, plan))
        tiles = load()
        sums = base_product(plan, tiles, base)
        over = [grid.send(base, axes, 1) for axes in (ONE, TWO)]
        far = along_z(grid, corner)
        far, *sums = lax.optimization_barrier((far, *sums))
        pieces = [*over, far]
    else:
        base, plan = lax.optimization_barrier((base, plan))
        tiles = load()
        sums = base_product(plan, tiles, base)
        lines = [base] + [grid.fetch(base, "y", r) for r in range(1, wide)]
        pieces = []
        for line in lines:
            pieces += [line, grid.fetch(line, "x", 1)]
        pieces = pieces[1:]
    return sums, pieces, plan, tiles


def scatter_sum(grid, plan, tiles, rest, low):
    depth, wide = grid.sizes["z"], grid.sizes["y"]
    order = range(depth - 1, 0, -1)
    shape = (depth, 2 * CORES, low.shape[1], tiles.shape[2])

    def narrow(v):
        return v.astype(jnp.bfloat16)

    def widen(v):
        return v.astype(jnp.float32)

    diagonal = 0.0
    if wide == 2:
        one, two, here, *parts = rest
        one, two, *parts = lax.optimization_barrier((one, two, *parts))
        one, two = grid.send(one, ONE, 1), grid.send(two, TWO, 1)
        parts = [grid.send(parts[depth - r - 1], "z", r) for r in order]
        parts[0], low = lax.optimization_barrier((parts[0], low))
        base = base_return(grid, plan, tiles, low)
        *parts, one, two, base = lax.optimization_barrier((*parts, one, two, base))
        base = (base + widen(one) + widen(two)).reshape(shape)
        corner = narrow(here + sum(widen(part) for part in parts))
    else:
        total = jnp.concatenate([base_return(grid, plan, tiles, low), rest[0]])
        total = total.reshape((wide, 2) + shape)
        total = total[:, 0] + widen(grid.send(narrow(total[:, 1]), "x", 1))
        base = total[0]
        for r in range(1, wide):
            base = base + widen(grid.send(narrow(total[r]), "y", r))
        corner = None
    parts = [narrow(base[depth - r]) for r in order]
    if corner is not None:
        *parts, corner = lax.optimization_barrier((*parts, corner))
        diagonal = widen(grid.send(corner, BOTH_AXES, 1))
    gram = base[0] + diagonal
    for r, part in zip(order, parts):
        gram = gram + widen(grid.send(part, "z", r))
    return gram


def plan_kernel(near, area, pose, point, valid, out):
    tiles, slots = area.shape[1], out.shape[1]
    row_id = lax.broadcasted_iota(jnp.int32, (tiles, tiles), 0)
    col_id = lax.broadcasted_iota(jnp.int32, (tiles, tiles), 1)
    lane = lax.broadcasted_iota(jnp.int32, (tiles, slots), 1)

    def column(row):
        return jnp.sum(jnp.where(row_id == col_id, row, 0.0), axis=1, keepdims=True)

    def half_up(v, unit):
        whole = v.astype(jnp.int32) + (unit - 1)
        return (whole & ~(unit - 1)).astype(jnp.float32)

    def arrange(key, phase):
        key_col, phase_col = column(key), column(phase)
        same = jnp.where((key_col == key) & (real_col > 0.0) & (real > 0.0), 1.0, 0.0)
        count = jnp.sum(same, axis=0, keepdims=True)
        rank = jnp.sum(jnp.where(row_id < col_id, same, 0.0), axis=0, keepdims=True)
        rank_col = jnp.sum(jnp.where(col_id < row_id, same, 0.0), axis=1, keepdims=True)
        room = jnp.where((rank == 0.0) & (real > 0.0), half_up(count, 2), 0.0)
        place = jnp.sum(jnp.where(key < key_col, room, 0.0), axis=1, keepdims=True) + rank_col
        end, gap, bounds = 0.0, 0.0, []
        for k in range(AREAS):
            used = jnp.sum(jnp.where(phase == k, room, 0.0), axis=1, keepdims=True)
            place = place + jnp.where(phase_col == k, gap, 0.0)
            padded = half_up(used, 2 * UNROLL)
            end, gap = end + padded, gap + padded - used
            bounds.append(end)
        place = jnp.where(real_col > 0.0, place, -1.0)
        return jnp.where(place.astype(jnp.int32) == lane, 1.0, 0.0), bounds

    def pick(hit, values):
        return jnp.sum(hit * values, axis=0, keepdims=True)

    real = valid[...].astype(jnp.float32)
    real_col = column(real)
    area_row = area[...].astype(jnp.float32)
    pose_row = pose[...].astype(jnp.float32)
    point_row = point[...].astype(jnp.float32)
    pose_col, point_col = column(pose_row), column(point_row)
    tile_col = column(col_id[:1].astype(jnp.float32))
    points = CORES * PT_DEV
    hit, ends = arrange(area_row * points + point_row, area_row)
    rows = [
        pick(hit, tile_col),
        pick(hit, pose_col),
        pick(hit, jnp.ones_like(tile_col)),
        pick(hit, point_col),
    ]
    turned = AREAS - 1.0 - area_row
    hit, bounds = arrange(turned * 65536.0 + pose_row, turned)
    rows += [
        pick(hit, tile_col),
        pick(hit, point_col - points) + points,
        pick(hit, pose_col),
    ]
    ends += bounds
    spot = lane[:1]
    tail = jnp.zeros_like(rows[0])
    for k, end in enumerate(ends):
        tail = jnp.where(spot == k, end * (0.5 / UNROLL), tail)
    for k in range(near.shape[0]):
        tail = jnp.where(spot == NEAR + k, near[k].astype(jnp.float32), tail)
    for k, row in enumerate(rows + [tail]):
        out[k : k + 1] = row.astype(jnp.int32)


def make_plan(grid, place, near, indices):
    pose, point, valid = indices
    tiles = pose.shape[0]
    area, pose = grid.spot(pose, place)
    slots = tiles + max(AREAS * CORES * PT_DEV, min(tiles, 2 * grid.count)) + 2 * AREAS * UNROLL
    slots = -(-slots // 128) * 128
    rows = [v.reshape(1, tiles) for v in (area, pose, point, valid)]
    vmem = pl.BlockSpec(memory_space=pltpu.VMEM)
    return pl.pallas_call(
        plan_kernel,
        out_shape=jax.ShapeDtypeStruct((8, slots), jnp.int32),
        in_specs=[pl.BlockSpec(memory_space=pltpu.SMEM)] + [vmem] * 4,
        out_specs=vmem,
        compiler_params=pltpu.CompilerParams(vmem_limit_bytes=32 * tiles * slots + 2 * 1024 * 1024),
    )(near, *rows)


def join_kernel(first, second, out, sems):
    half = first.shape[0]
    copies = [
        pltpu.make_async_copy(first, out.at[pl.ds(0, half)], sems.at[0]),
        pltpu.make_async_copy(second, out.at[pl.ds(half, half)], sems.at[1]),
    ]
    for copy in copies:
        copy.start()
    for copy in copies:
        copy.wait()


def join_tiles(first, second):
    shape = (2 * first.shape[0], *first.shape[1:])
    return pl.pallas_call(
        join_kernel,
        out_shape=jax.ShapeDtypeStruct(shape, first.dtype),
        in_specs=[pl.BlockSpec(memory_space=pl.ANY)] * 2,
        out_specs=pl.BlockSpec(memory_space=pltpu.VMEM),
        scratch_shapes=[pltpu.SemaphoreType.DMA((2,))],
        compiler_params=pltpu.CompilerParams(vmem_limit_bytes=2 * 1024 * 1024),
    )(first, second)


NT = (((1,), (1,)), ((), ()))
NN = (((1,), (0,)), ((), ()))
F_TILE, F_POSE, F_REAL, F_POINT, B_TILE, B_POINT, B_POSE, ENDS = range(8)


def forward(plan, tiles, field, acc, begin, end):
    def body(i, _):
        for u in range(UNROLL):
            j = 2 * (i * UNROLL + u)
            block = [
                field[plan[F_POSE, j + h], : acc.shape[1]]
                * plan[F_REAL, j + h].astype(jnp.float32).astype(jnp.bfloat16)
                for h in range(2)
            ]
            tile = [tiles[plan[F_TILE, j + h]] for h in range(2)]
            acc[plan[F_POINT, j]] += lax.dot_general(
                jnp.concatenate(block, axis=1),
                jnp.concatenate(tile, axis=1),
                NT,
                preferred_element_type=jnp.float32,
            )
        return 0

    lax.fori_loop(begin, end, body, 0)


def backward(plan, tiles, low, total, begin, end):
    def body(i, _):
        for u in range(UNROLL):
            j = 2 * (i * UNROLL + u)
            block = [low[plan[B_POINT, j + h]] for h in range(2)]
            tile = [tiles[plan[B_TILE, j + h]] for h in range(2)]
            total[plan[B_POSE, j]] += lax.dot_general(
                jnp.concatenate(block, axis=1),
                jnp.concatenate(tile, axis=0),
                NN,
                preferred_element_type=jnp.float32,
            )
        return 0

    lax.fori_loop(begin, end, body, 0)


def assemble(pieces, field):
    start = 0
    for piece in pieces:
        field[start : start + piece.shape[0]] = piece[...]
        start += piece.shape[0]


def near_side(plan, field, sides, area):
    for side in range(sides.shape[0]):
        spot = NEAR + 2 * side

        @pl.when(plan[ENDS, spot] == area)
        def _():
            sides[side] = field[pl.ds(plan[ENDS, spot + 1], 2)]


def base_forward(plan_in, tiles, field, acc, sides, plan, sem):
    copy = pltpu.make_async_copy(plan_in, plan, sem)
    copy.start()
    acc[...] = jnp.zeros_like(acc)
    sides[...] = jnp.zeros_like(sides)
    copy.wait()
    near_side(plan, field, sides, 0)
    forward(plan, tiles, field, acc, 0, plan[ENDS, 0])


def rest_both(cuts, plan_in, tiles, part, sides_in, *refs):
    pieces, refs = refs[: -len(cuts) - 7], refs[-len(cuts) - 7 :]
    (acc, sides, low), outs, (field, total, plan, sem) = refs[:3], refs[3:-4], refs[-4:]
    copy = pltpu.make_async_copy(plan_in, plan, sem)
    copy.start()
    assemble(pieces, field)
    total[...] = jnp.zeros_like(total)
    points = acc.shape[0]
    low[points] = jnp.zeros(low.shape[1:], jnp.bfloat16)
    copy.wait()
    near_side(plan, field, sides, 1)
    forward(plan, tiles, field, acc, plan[ENDS, 0], plan[ENDS, 1])
    low[:points] = acc[...].astype(jnp.bfloat16)
    backward(plan, tiles, low, total, 0, plan[ENDS, AREAS])
    start = 0
    for size, out in zip(cuts, outs):
        out[...] = total[start : start + size].astype(out.dtype)
        start += size


def base_backward(plan_in, tiles, low, base, plan, sem):
    copy = pltpu.make_async_copy(plan_in, plan, sem)
    copy.start()
    base[...] = jnp.zeros_like(base)
    copy.wait()
    backward(plan, tiles, low, base, plan[ENDS, AREAS], plan[ENDS, AREAS + 1])


def call(kernel, outs, scratch, args, kinds, tiles, share, aliases={}):
    place = {
        "a": pl.BlockSpec(memory_space=pl.ANY),
        "v": pl.BlockSpec(memory_space=pltpu.VMEM),
    }
    size = sum(math.prod(v.shape) * jnp.dtype(v.dtype).itemsize for v in scratch)
    scratch = scratch + [pltpu.SMEM(args[0].shape, jnp.int32), pltpu.SemaphoreType.DMA]
    return pl.pallas_call(
        kernel,
        out_shape=outs,
        in_specs=[place[kind] for kind in kinds],
        out_specs=[place["v"]] * len(outs),
        scratch_shapes=scratch,
        input_output_aliases=aliases,
        compiler_params=pltpu.CompilerParams(vmem_limit_bytes=size + 3 * 1024 * 1024),
        cost_estimate=pl.CostEstimate(
            flops=int(share * 4 * tiles.size * 128),
            bytes_accessed=tiles.size * 2,
            transcendentals=0,
        ),
    )(*args)


def array(lead, like, kind):
    return jax.ShapeDtypeStruct((lead, *like[1:]), kind)


def base_product(plan, tiles, base):
    rows = tiles.shape[1] // CORES
    acc = (0, rows, tiles.shape[1])
    return call(
        base_forward,
        [
            array(CORES * PT_DEV, acc, jnp.float32),
            jax.ShapeDtypeStruct((2 * CORES, 2, *base.shape[1:]), jnp.bfloat16),
        ],
        [],
        [plan, tiles, base],
        "avv",
        tiles,
        0.125,
    )


def rest_product(grid, plan, tiles, sums, pieces):
    plane = grid.plane
    rest = 2 * grid.count - plane
    if grid.sizes["y"] == 2:
        group = 2 * CORES
        cuts = [plane, plane, group] + [group] * (grid.sizes["z"] - 1)
        kinds = [jnp.bfloat16, jnp.bfloat16, jnp.float32] + [jnp.bfloat16] * (grid.sizes["z"] - 1)
    else:
        cuts, kinds = [rest], [jnp.float32]
    rows, points = sums[0].shape[1:]
    like = (0, rows, tiles.shape[2])
    _, sides, low, *outs = call(
        functools.partial(rest_both, cuts),
        [
            *[jax.ShapeDtypeStruct(v.shape, v.dtype) for v in sums],
            array(CORES * PT_DEV + 1, (0, rows, points), jnp.bfloat16),
            *[array(cut, like, kind) for cut, kind in zip(cuts, kinds)],
        ],
        [pltpu.VMEM((rest, *pieces[0].shape[1:]), jnp.bfloat16), pltpu.VMEM((rest, *like[1:]), jnp.float32)],
        [plan, tiles, *sums, *pieces],
        "avvv" + "v" * len(pieces),
        tiles,
        0.75,
        {2: 0, 3: 1},
    )
    return outs, low, sides


def base_return(grid, plan, tiles, low):
    (base,) = call(
        base_backward,
        [array(grid.plane, (0, low.shape[1], tiles.shape[2]), jnp.float32)],
        [],
        [plan, tiles, low],
        "avv",
        tiles,
        0.125,
    )
    return base


def in_order(core, mine, theirs, axis):
    low, high = jnp.where(core == 0, mine, theirs), jnp.where(core == 0, theirs, mine)
    return jnp.concatenate([low, high], axis=axis)


def on_device(jac_tiles, tile_pose, tile_point, tile_valid, prior_weight, right_side):
    grid = Grid()
    place = lax.axis_index(BOTH)
    at = grid.coords(place)
    core = at["core"]
    homes = [grid.device(at | {"core": c}) for c in range(CORES)]
    params, rhs = right_side.shape[1:]
    rows = rhs // CORES

    def half(v, which):
        return lax.dynamic_slice_in_dim(v, which * rows, rows, 1)

    def whole(*values):
        v = jnp.stack(values).reshape((-1, CORES, 2) + values[0].shape[1:])
        mine = lax.dynamic_index_in_dim(v, core, 1, keepdims=False)
        theirs = grid.swap(lax.dynamic_index_in_dim(v, 1 - core, 1, keepdims=False))
        return tuple(jnp.swapaxes(in_order(core, mine, theirs, 2), 2, 3))

    turned = jnp.swapaxes(right_side, 1, 2)
    names = jnp.stack([tile_pose, tile_point, tile_valid]).astype(jnp.float32)
    width = -(-names.shape[1] // params)
    names = jnp.pad(names, ((0, 0), (0, width * params - names.shape[1])))
    extra = jnp.concatenate([prior_weight, names.reshape(3 * width, params)])
    extra = jnp.pad(extra, ((0, -extra.shape[0] % 16), (0, 0))).reshape(2, -1, params)
    pack = jnp.concatenate([half(turned, 1 - core), extra], axis=1)
    other_tiles = grid.swap(jac_tiles)
    theirs = grid.swap(pack)
    right_side = in_order(core, half(turned, core), theirs[:, :rows], 0)
    theirs = theirs[:, rows:].reshape(-1, params)
    weights = in_order(core, prior_weight, theirs[:2], 0)
    names = theirs[2 : 2 + 3 * width].reshape(3, -1)[:, : tile_pose.shape[0]].astype(jnp.int32)
    indices = jnp.stack([tile_pose, tile_point, tile_valid])
    shift = jnp.array([[0], [PT_DEV], [0]], jnp.int32)
    indices = jnp.concatenate([indices, names + shift], axis=1)
    near = []
    for home in homes:
        near += grid.spot(2 * jnp.maximum(home - 1, 0), place)
        near += grid.spot(2 * jnp.minimum(home + 1, grid.count - 1), place)
    plan = make_plan(grid, place, jnp.stack(near), indices)
    tiles = None

    def load():
        return join_tiles(jac_tiles, other_tiles) if tiles is None else tiles

    zero = jnp.zeros((params,), jnp.float32)
    theta = (highest + lowest) / 2.0
    delta = (highest - lowest) / 2.0
    sigma = theta / delta
    ratio = 1.0 / sigma
    step = right_side / theta
    solution = jnp.zeros(right_side.shape, jnp.float32)
    residual = right_side
    for turn in range(ITERS):
        if turn > 0:
            new_ratio = 1.0 / (2.0 * sigma - ratio)
            step = new_ratio * ratio * step + 2.0 * new_ratio / delta * residual
            ratio = new_ratio
        solution = solution + step
        low = step.astype(jnp.bfloat16)
        if turn == 0:
            extra = jnp.broadcast_to(weights[:, None, :], (2 * CORES, 16, params))
            low = jnp.concatenate([low, extra.astype(jnp.bfloat16)], axis=1)
        sums, pieces, plan, tiles = gather_field(grid, low, plan, load)
        rest, point_sums, sides = rest_product(grid, plan, tiles, sums, pieces)
        gram = scatter_sum(grid, plan, tiles, rest, point_sums)
        sides = sides.astype(jnp.float32)
        if turn == 0:
            w_left, w_right = [], []
            for c, home in enumerate(homes):
                first, last = home == 0, home == grid.count - 1
                left, right = sides[2 * c, :, rows], sides[2 * c + 1, :, rows]
                one, two = weights[2 * c], weights[2 * c + 1]
                w_left += [jnp.where(first, zero, left[0]), jnp.where(first, zero, two)]
                w_right += [one, jnp.where(last, one, right[1])]
            w_left = jnp.stack(w_left)[:, None, :]
            w_right = jnp.stack(w_right)[:, None, :]
        left = jnp.concatenate([sides[2 * c, :, :rows] for c in range(CORES)])
        right = []
        for c, home in enumerate(homes):
            turned = step[2 * c : 2 * c + 2][::-1]
            right.append(jnp.where(home == grid.count - 1, turned, sides[2 * c + 1, :, :rows]))
        prior = w_left * (step - left) + w_right * (step - jnp.concatenate(right))
        residual = residual - (gram + prior + damping * step)
    return whole(solution, residual)


def solution(mesh):
    return jax.shard_map(
        on_device,
        mesh=mesh,
        in_specs=(
            P(BOTH, None, None),
            P(BOTH),
            P(BOTH),
            P(BOTH),
            P(BOTH, None),
            P(BOTH, None, None),
        ),
        out_specs=(P(BOTH, None, None), P(BOTH, None, None)),
        check_vma=False,
    )
```

profile of v0, /device:TPU:0, one launch (start us, length us, event | category | flops | bytes accessed | tf_op | source)
XLA Modules:
  0.0 161.7 jit_solution(8995342378611692643)
XLA Ops:
  4.4 3.6 %collective-permute-done = f32[2,72,128]{2,1,0:T(8,128)S(1)} collective-permute-done((f32[2,72,128]{2,1,0:T(8,128)S(1)}, f32[2,72,128]{2,1,0:T(8,128)S(1)}, u32[]{:S(2)}, u32[]{:S(2)}) %collective-permute-start) | collective-permute-done | bytes 73760 | tf_op jit(solution)/shard_map/ppermute | solution.py:68
  8.8 5.0 %collective-permute-start.1 = (bf16[4,80,128]{2,1,0:T(8,128)(2,1)S(1)}, bf16[4,80,128]{2,1,0:T(8,128)(2,1)S(1)}, u32[]{:S(2)}, u32[]{:S(2)}) collective-permute-start(bf16[4,80,128]{2,1,0:T(8,128)(2,1)S(1)} %pad_maximum_fusion.7), channel_id=1, source_target_pairs={{0,6},{1,7},{2,4},{3,5},{4,2},{5,3},{6,0},{7,1},{8,14},{9,15},{10,... | collective-permute-start | bytes 245768 | tf_op jit(solution)/shard_map/ppermute | solution.py:68
  14.5 2.6 %collective-permute-start.4 = (bf16[4,80,128]{2,1,0:T(8,128)(2,1)S(1)}, bf16[4,80,128]{2,1,0:T(8,128)(2,1)S(1)}, u32[]{:S(2)}, u32[]{:S(2)}) collective-permute-start(bf16[4,80,128]{2,1,0:T(8,128)(2,1)S(1)} %pad_maximum_fusion.7), channel_id=1, source_target_pairs={{0,17},{1,16},{2,19},{3,18},{4,21},{5,20},{6,23},{7,22},{8,25},{9,... | collective-permute-start | bytes 245768 | tf_op jit(solution)/shard_map/ppermute | solution.py:68
  21.1 3.4 %collective-permute-start.6 = (bf16[4,80,128]{2,1,0:T(8,128)(2,1)S(1)}, bf16[4,80,128]{2,1,0:T(8,128)(2,1)S(1)}, u32[]{:S(2)}, u32[]{:S(2)}) collective-permute-start(bf16[4,80,128]{2,1,0:T(8,128)(2,1)S(1)} %collective-permute-done.4), channel_id=1, source_target_pairs={{0,6},{1,7},{2,4},{3,5},{4,2},{5,3},{6,0},{7,1},{8,14},{9,15},{10,... | collective-permute-start | bytes 245768 | tf_op jit(solution)/shard_map/ppermute | solution.py:68
  25.5 1.5 collective-permute-start.10
  27.6 1.5 collective-permute-start.9
  29.1 1.9 %collective-permute-done.7 = bf16[4,80,128]{2,1,0:T(8,128)(2,1)S(1)} collective-permute-done((bf16[4,80,128]{2,1,0:T(8,128)(2,1)S(1)}, bf16[4,80,128]{2,1,0:T(8,128)(2,1)S(1)}, u32[]{:S(2)}, u32[]{:S(2)}) %collective-permute-start.7) | collective-permute-done | bytes 81952 | tf_op jit(solution)/shard_map/ppermute | solution.py:68
  31.0 2.2 %copy-done.3 = bf16[128,128,128]{2,1,0:T(8,128)(2,1)S(1)} copy-done((bf16[128,128,128]{2,1,0:T(8,128)(2,1)S(1)}, bf16[128,128,128]{2,1,0:T(8,128)(2,1)}, u32[]{:S(2)}) %copy-start.3) | copy-done | bytes 4194328
  33.2 2.5 %shard_map.87.tiles = bf16[256,128,128]{2,1,0:T(8,128)(2,1)S(1)} custom-call(bf16[128,128,128]{2,1,0:T(8,128)(2,1)S(1)} %copy-done.3, bf16[128,128,128]{2,1,0:T(8,128)(2,1)} %collective-permute-done.5.second), custom_call_target="tpu_custom_call" | custom-call | tf_op jit(solution)/shard_map/pallas_call | solution.py:245
  35.7 2.1 %shard_map.88 = (f32[32,64,128]{2,1,0:T(8,128)S(1)}, bf16[4,2,80,128]{3,2,1,0:T(8,128)(2,1)S(1)}) custom-call(s32[8,384]{1,0:T(8,128)S(1)} %shard_map.86.plan_in, bf16[256,128,128]{2,1,0:T(8,128)(2,1)S(1)} %shard_map.87.tiles, bf16[16,80,128]{2,1,0:T(8,128)(2,1)S(1)} %pad_maximum_fusion.field), custom_call_target="tpu_custom_call" | custom-call | flops 268435456 | bytes 8388608 | tf_op jit(solution)/shard_map/pallas_call | solution.py:359
  37.8 5.9 %shard_map.89 = (f32[32,64,128]{2,1,0:T(8,128)S(1)}, bf16[4,2,80,128]{3,2,1,0:T(8,128)(2,1)S(1)}, bf16[33,64,128]{2,1,0:T(8,128)(2,1)S(1)}, bf16[16,64,128]{2,1,...) custom-call(s32[8,384]{1,0:T(8,128)S(1)} %shard_map.86.plan_in, ...), custom_call_target="tpu_custom_call", output_to_operand_aliasing={{0}: (2, {}), {1}: (3, {})} | custom-call | flops 1610612736 | bytes 8388608 | tf_op jit(solution)/shard_map/pallas_call | solution.py:359
  43.7 2.1 %collective-permute-start.11 = (bf16[4,64,128]{2,1,0:T(8,128)(2,1)S(1)}, bf16[4,64,128]{2,1,0:T(8,128)(2,1)S(1)}, u32[]{:S(2)}, u32[]{:S(2)}) collective-permute-start(bf16[4,64,128]{2,1,0:T(8,128)(2,1)S(1)} %get-tuple-element.114), channel_id=1, source_target_pairs={{0,6},{1,7},{2,4},{3,5},{4,2},{5,3},{6,0},{7,1},{8,14},{9,15},{10,... | collective-permute-start | bytes 196616 | tf_op jit(solution)/shard_map/ppermute | solution.py:68
  46.5 1.8 %collective-permute-start.15 = (bf16[16,64,128]{2,1,0:T(8,128)(2,1)S(1)}, bf16[16,64,128]{2,1,0:T(8,128)(2,1)S(1)}, u32[]{:S(2)}, u32[]{:S(2)}) collective-permute-start(bf16[16,64,128]{2,1,0:T(8,128)(2,1)S(1)} %get-tuple-element.120), channel_id=1, source_target_pairs={{0,16},{1,17},{2,18},{3,19},{4,20},{5,21},{6,22},{7,23},{8,9},{9,8... | collective-permute-start | bytes 786440 | tf_op jit(solution)/shard_map/ppermute | solution.py:68
  48.4 3.0 %collective-permute-start.13 = (bf16[4,64,128]{2,1,0:T(8,128)(2,1)S(1)}, bf16[4,64,128]{2,1,0:T(8,128)(2,1)S(1)}, u32[]{:S(2)}, u32[]{:S(2)}) collective-permute-start(bf16[4,64,128]{2,1,0:T(8,128)(2,1)S(1)} %get-tuple-element.118), channel_id=1, source_target_pairs={{0,2},{1,3},{2,0},{3,1},{4,6},{5,7},{6,4},{7,5},{8,10},{9,11},{10,... | collective-permute-start | bytes 196616 | tf_op jit(solution)/shard_map/ppermute | solution.py:68
  51.5 1.5 shard_map.90
  55.9 2.4 %collective-permute-start.17 = (bf16[4,64,128]{2,1,0:T(8,128)(2,1)S(1)}, bf16[4,64,128]{2,1,0:T(8,128)(2,1)S(1)}, u32[]{:S(2)}, u32[]{:S(2)}) collective-permute-start(bf16[4,64,128]{2,1,0:T(8,128)(2,1)S(1)} %get-tuple-element.130), channel_id=1, source_target_pairs={{0,6},{1,7},{2,4},{3,5},{4,2},{5,3},{6,0},{7,1},{8,14},{9,15},{10,... | collective-permute-start | bytes 196616 | tf_op jit(solution)/shard_map/ppermute | solution.py:68
  58.3 1.9 %collective-permute-start.19 = (bf16[4,64,128]{2,1,0:T(8,128)(2,1)S(1)}, bf16[4,64,128]{2,1,0:T(8,128)(2,1)S(1)}, u32[]{:S(2)}, u32[]{:S(2)}) collective-permute-start(bf16[4,64,128]{2,1,0:T(8,128)(2,1)S(1)} %get-tuple-element.132), channel_id=1, source_target_pairs={{0,2},{1,3},{2,0},{3,1},{4,6},{5,7},{6,4},{7,5},{8,10},{9,11},{10,... | collective-permute-start | bytes 196616 | tf_op jit(solution)/shard_map/ppermute | solution.py:68
  60.3 2.4 %collective-permute-done.17 = bf16[4,64,128]{2,1,0:T(8,128)(2,1)S(1)} collective-permute-done((bf16[4,64,128]{2,1,0:T(8,128)(2,1)S(1)}, bf16[4,64,128]{2,1,0:T(8,128)(2,1)S(1)}, u32[]{:S(2)}, u32[]{:S(2)}) %collective-permute-start.17) | collective-permute-done | bytes 65568 | tf_op jit(solution)/shard_map/ppermute | solution.py:68
  62.7 1.4 collective-permute-done.18
  64.2 2.0 %collective-permute-start.20 = (bf16[4,64,128]{2,1,0:T(8,128)(2,1)S(1)}, bf16[4,64,128]{2,1,0:T(8,128)(2,1)S(1)}, u32[]{:S(2)}, u32[]{:S(2)}) collective-permute-start(bf16[4,64,128]{2,1,0:T(8,128)(2,1)S(1)} %get-tuple-element.207), channel_id=1, source_target_pairs={{0,6},{1,7},{2,4},{3,5},{4,2},{5,3},{6,0},{7,1},{8,14},{9,15},{10,... | collective-permute-start | bytes 196616 | tf_op jit(solution)/shard_map/ppermute | solution.py:68
  66.2 2.4 %collective-permute-start.22 = (bf16[4,64,128]{2,1,0:T(8,128)(2,1)S(1)}, bf16[4,64,128]{2,1,0:T(8,128)(2,1)S(1)}, u32[]{:S(2)}, u32[]{:S(2)}) collective-permute-start(bf16[4,64,128]{2,1,0:T(8,128)(2,1)S(1)} %get-tuple-element.207), channel_id=1, source_target_pairs={{0,2},{1,3},{2,0},{3,1},{4,6},{5,7},{6,4},{7,5},{8,10},{9,11},{10,... | collective-permute-start | bytes 196616 | tf_op jit(solution)/shard_map/ppermute | solution.py:68
  68.7 2.4 %collective-permute-start.23 = (bf16[4,64,128]{2,1,0:T(8,128)(2,1)S(1)}, bf16[4,64,128]{2,1,0:T(8,128)(2,1)S(1)}, u32[]{:S(2)}, u32[]{:S(2)}) collective-permute-start(bf16[4,64,128]{2,1,0:T(8,128)(2,1)S(1)} %get-tuple-element.207), channel_id=1, source_target_pairs={{0,17},{1,16},{2,19},{3,18},{4,21},{5,20},{6,23},{7,22},{8,25},{9,... | collective-permute-start | bytes 196616 | tf_op jit(solution)/shard_map/ppermute | solution.py:68
  71.1 1.5 collective-permute-done.21
  74.9 2.0 %collective-permute-start.28 = (bf16[16,64,128]{2,1,0:T(8,128)(2,1)S(1)}, bf16[16,64,128]{2,1,0:T(8,128)(2,1)S(1)}, u32[]{:S(2)}, u32[]{:S(2)}) collective-permute-start(bf16[16,64,128]{2,1,0:T(8,128)(2,1)S(1)} %pad_maximum_fusion.2.field), channel_id=1, source_target_pairs={{0,16},{1,17},{2,18},{3,19},{4,20},{5,21},{6,22},{7,23},{8,9},{9,8... | collective-permute-start | bytes 786440 | tf_op jit(solution)/shard_map/ppermute | solution.py:68
  78.3 2.9 %collective-permute-start.26 = (bf16[4,64,128]{2,1,0:T(8,128)(2,1)S(1)}, bf16[4,64,128]{2,1,0:T(8,128)(2,1)S(1)}, u32[]{:S(2)}, u32[]{:S(2)}) collective-permute-start(bf16[4,64,128]{2,1,0:T(8,128)(2,1)S(1)} %collective-permute-done.23), channel_id=1, source_target_pairs={{0,2},{1,3},{2,0},{3,1},{4,6},{5,7},{6,4},{7,5},{8,10},{9,11},{10,... | collective-permute-start | bytes 196616 | tf_op jit(solution)/shard_map/ppermute | solution.py:68
  81.2 2.0 %shard_map.91 = (f32[32,64,128]{2,1,0:T(8,128)S(1)}, bf16[4,2,64,128]{3,2,1,0:T(8,128)(2,1)S(1)}) custom-call(s32[8,384]{1,0:T(8,128)S(1)} %shard_map.86.plan_in, bf16[256,128,128]{2,1,0:T(8,128)(2,1)S(1)} %shard_map.87.tiles, bf16[16,64,128]{2,1,0:T(8,128)(2,1)S(1)} %pad_maximum_fusion.2.field), custom_call_target="tpu_custom_call" | custom-call | flops 268435456 | bytes 8388608 | tf_op jit(solution)/shard_map/pallas_call | solution.py:359
  84.4 5.9 %shard_map.92 = (f32[32,64,128]{2,1,0:T(8,128)S(1)}, bf16[4,2,64,128]{3,2,1,0:T(8,128)(2,1)S(1)}, bf16[33,64,128]{2,1,0:T(8,128)(2,1)S(1)}, bf16[16,64,128]{2,1,...) custom-call(s32[8,384]{1,0:T(8,128)S(1)} %shard_map.86.plan_in, ...), custom_call_target="tpu_custom_call", output_to_operand_aliasing={{0}: (2, {}), {1}: (3, {})} | custom-call | flops 1610612736 | bytes 8388608 | tf_op jit(solution)/shard_map/pallas_call | solution.py:359
  91.9 1.5 collective-permute-start.29
  94.1 2.3 %collective-permute-start.31 = (bf16[4,64,128]{2,1,0:T(8,128)(2,1)S(1)}, bf16[4,64,128]{2,1,0:T(8,128)(2,1)S(1)}, u32[]{:S(2)}, u32[]{:S(2)}) collective-permute-start(bf16[4,64,128]{2,1,0:T(8,128)(2,1)S(1)} %get-tuple-element.151), channel_id=1, source_target_pairs={{0,2},{1,3},{2,0},{3,1},{4,6},{5,7},{6,4},{7,5},{8,10},{9,11},{10,... | collective-permute-start | bytes 196616 | tf_op jit(solution)/shard_map/ppermute | solution.py:68
  96.4 1.7 %collective-permute-done.29 = bf16[4,64,128]{2,1,0:T(8,128)(2,1)S(1)} collective-permute-done((bf16[4,64,128]{2,1,0:T(8,128)(2,1)S(1)}, bf16[4,64,128]{2,1,0:T(8,128)(2,1)S(1)}, u32[]{:S(2)}, u32[]{:S(2)}) %collective-permute-start.29) | collective-permute-done | bytes 65568 | tf_op jit(solution)/shard_map/ppermute | solution.py:68
  98.1 1.5 shard_map.93
  99.8 2.0 %collective-permute-start.34 = (bf16[4,64,128]{2,1,0:T(8,128)(2,1)S(1)}, bf16[4,64,128]{2,1,0:T(8,128)(2,1)S(1)}, u32[]{:S(2)}, u32[]{:S(2)}) collective-permute-start(bf16[4,64,128]{2,1,0:T(8,128)(2,1)S(1)} %add_convert_fusion.1), channel_id=1, source_target_pairs={{0,17},{1,16},{2,19},{3,18},{4,21},{5,20},{6,23},{7,22},{8,25},{9,... | collective-permute-start | bytes 196616 | tf_op jit(solution)/shard_map/ppermute | solution.py:68
  104.3 1.9 %collective-permute-start.37 = (bf16[4,64,128]{2,1,0:T(8,128)(2,1)S(1)}, bf16[4,64,128]{2,1,0:T(8,128)(2,1)S(1)}, u32[]{:S(2)}, u32[]{:S(2)}) collective-permute-start(bf16[4,64,128]{2,1,0:T(8,128)(2,1)S(1)} %get-tuple-element.165), channel_id=1, source_target_pairs={{0,2},{1,3},{2,0},{3,1},{4,6},{5,7},{6,4},{7,5},{8,10},{9,11},{10,... | collective-permute-start | bytes 196616 | tf_op jit(solution)/shard_map/ppermute | solution.py:68
  106.2 2.0 %collective-permute-done.35 = bf16[4,64,128]{2,1,0:T(8,128)(2,1)S(1)} collective-permute-done((bf16[4,64,128]{2,1,0:T(8,128)(2,1)S(1)}, bf16[4,64,128]{2,1,0:T(8,128)(2,1)S(1)}, u32[]{:S(2)}, u32[]{:S(2)}) %collective-permute-start.35) | collective-permute-done | bytes 65568 | tf_op jit(solution)/shard_map/ppermute | solution.py:68
  108.2 3.2 %collective-permute-done.36 = bf16[4,64,128]{2,1,0:T(8,128)(2,1)S(1)} collective-permute-done((bf16[4,64,128]{2,1,0:T(8,128)(2,1)S(1)}, bf16[4,64,128]{2,1,0:T(8,128)(2,1)S(1)}, u32[]{:S(2)}, u32[]{:S(2)}) %collective-permute-start.36) | collective-permute-done | bytes 65568 | tf_op jit(solution)/shard_map/ppermute | solution.py:68
  112.9 3.1 %collective-permute-start.40 = (bf16[4,64,128]{2,1,0:T(8,128)(2,1)S(1)}, bf16[4,64,128]{2,1,0:T(8,128)(2,1)S(1)}, u32[]{:S(2)}, u32[]{:S(2)}) collective-permute-start(bf16[4,64,128]{2,1,0:T(8,128)(2,1)S(1)} %get-tuple-element.202), channel_id=1, source_target_pairs={{0,2},{1,3},{2,0},{3,1},{4,6},{5,7},{6,4},{7,5},{8,10},{9,11},{10,... | collective-permute-start | bytes 196616 | tf_op jit(solution)/shard_map/ppermute | solution.py:68
  118.3 2.8 %collective-permute-done.39 = bf16[4,64,128]{2,1,0:T(8,128)(2,1)S(1)} collective-permute-done((bf16[4,64,128]{2,1,0:T(8,128)(2,1)S(1)}, bf16[4,64,128]{2,1,0:T(8,128)(2,1)S(1)}, u32[]{:S(2)}, u32[]{:S(2)}) %collective-permute-start.39) | collective-permute-done | bytes 65568 | tf_op jit(solution)/shard_map/ppermute | solution.py:68
  123.0 1.8 %collective-permute-start.42 = (bf16[4,64,128]{2,1,0:T(8,128)(2,1)S(1)}, bf16[4,64,128]{2,1,0:T(8,128)(2,1)S(1)}, u32[]{:S(2)}, u32[]{:S(2)}) collective-permute-start(bf16[4,64,128]{2,1,0:T(8,128)(2,1)S(1)} %collective-permute-done.41), channel_id=1, source_target_pairs={{0,6},{1,7},{2,4},{3,5},{4,2},{5,3},{6,0},{7,1},{8,14},{9,15},{10,... | collective-permute-start | bytes 196616 | tf_op jit(solution)/shard_map/ppermute | solution.py:68
  124.8 2.6 %collective-permute-start.44 = (bf16[4,64,128]{2,1,0:T(8,128)(2,1)S(1)}, bf16[4,64,128]{2,1,0:T(8,128)(2,1)S(1)}, u32[]{:S(2)}, u32[]{:S(2)}) collective-permute-start(bf16[4,64,128]{2,1,0:T(8,128)(2,1)S(1)} %collective-permute-done.41), channel_id=1, source_target_pairs={{0,2},{1,3},{2,0},{3,1},{4,6},{5,7},{6,4},{7,5},{8,10},{9,11},{10,... | collective-permute-start | bytes 196616 | tf_op jit(solution)/shard_map/ppermute | solution.py:68
  127.3 3.4 %copy-done.1 = bf16[256,128,128]{2,1,0:T(8,128)(2,1)S(1)} copy-done((bf16[256,128,128]{2,1,0:T(8,128)(2,1)S(1)}, bf16[256,128,128]{2,1,0:T(8,128)(2,1)}, u32[]{:S(2)}) %copy-start.1) | copy-done | bytes 8388632
  130.7 2.1 %shard_map.94 = (f32[32,64,128]{2,1,0:T(8,128)S(1)}, bf16[4,2,64,128]{3,2,1,0:T(8,128)(2,1)S(1)}) custom-call(s32[8,384]{1,0:T(8,128)S(1)} %shard_map.86.plan_in, bf16[256,128,128]{2,1,0:T(8,128)(2,1)S(1)} %copy-done.1, bf16[16,64,128]{2,1,0:T(8,128)(2,1)S(1)} %pad_maximum_fusion.4.field), custom_call_target="tpu_custom_call" | custom-call | flops 268435456 | bytes 8388608 | tf_op jit(solution)/shard_map/pallas_call | solution.py:359
  134.1 5.9 %shard_map.95 = (f32[32,64,128]{2,1,0:T(8,128)S(1)}, bf16[4,2,64,128]{3,2,1,0:T(8,128)(2,1)S(1)}, bf16[33,64,128]{2,1,0:T(8,128)(2,1)S(1)}, bf16[16,64,128]{2,1,...) custom-call(s32[8,384]{1,0:T(8,128)S(1)} %shard_map.86.plan_in, ...), custom_call_target="tpu_custom_call", output_to_operand_aliasing={{0}: (2, {}), {1}: (3, {})} | custom-call | flops 1610612736 | bytes 8388608 | tf_op jit(solution)/shard_map/pallas_call | solution.py:359
  140.9 2.0 %collective-permute-start.51 = (bf16[16,64,128]{2,1,0:T(8,128)(2,1)S(1)}, bf16[16,64,128]{2,1,0:T(8,128)(2,1)S(1)}, u32[]{:S(2)}, u32[]{:S(2)}) collective-permute-start(bf16[16,64,128]{2,1,0:T(8,128)(2,1)S(1)} %get-tuple-element.186), channel_id=1, source_target_pairs={{0,16},{1,17},{2,18},{3,19},{4,20},{5,21},{6,22},{7,23},{8,9},{9,8... | collective-permute-start | bytes 786440 | tf_op jit(solution)/shard_map/ppermute | solution.py:68
  143.9 3.5 %collective-permute-start.49 = (bf16[4,64,128]{2,1,0:T(8,128)(2,1)S(1)}, bf16[4,64,128]{2,1,0:T(8,128)(2,1)S(1)}, u32[]{:S(2)}, u32[]{:S(2)}) collective-permute-start(bf16[4,64,128]{2,1,0:T(8,128)(2,1)S(1)} %get-tuple-element.184), channel_id=1, source_target_pairs={{0,2},{1,3},{2,0},{3,1},{4,6},{5,7},{6,4},{7,5},{8,10},{9,11},{10,... | collective-permute-start | bytes 196616 | tf_op jit(solution)/shard_map/ppermute | solution.py:68
  147.4 1.8 %collective-permute-done.47 = bf16[4,64,128]{2,1,0:T(8,128)(2,1)S(1)} collective-permute-done((bf16[4,64,128]{2,1,0:T(8,128)(2,1)S(1)}, bf16[4,64,128]{2,1,0:T(8,128)(2,1)S(1)}, u32[]{:S(2)}, u32[]{:S(2)}) %collective-permute-start.47) | collective-permute-done | bytes 65568 | tf_op jit(solution)/shard_map/ppermute | solution.py:68
  149.2 1.5 shard_map.96
  154.0 1.9 %collective-permute-start.55 = (bf16[4,64,128]{2,1,0:T(8,128)(2,1)S(1)}, bf16[4,64,128]{2,1,0:T(8,128)(2,1)S(1)}, u32[]{:S(2)}, u32[]{:S(2)}) collective-permute-start(bf16[4,64,128]{2,1,0:T(8,128)(2,1)S(1)} %get-tuple-element.198), channel_id=1, source_target_pairs={{0,2},{1,3},{2,0},{3,1},{4,6},{5,7},{6,4},{7,5},{8,10},{9,11},{10,... | collective-permute-start | bytes 196616 | tf_op jit(solution)/shard_map/ppermute | solution.py:68
  156.1 1.5 collective-permute-done.53
  (142 shorter events, 40.6 us)
Async XLA Ops:
  0.6 30.4 %collective-permute-start.5 = (bf16[128,128,128]{2,1,0:T(8,128)(2,1)}, bf16[128,128,128]{2,1,0:T(8,128)(2,1)}, u32[]{:S(2)}, u32[]{:S(2)}) collective-permute-start(bf16[128,128,128]{2,1,0:T(8,128)(2,1)} %first.1), channel_id=1, source_target_pairs={{0,8},{1,9},{2,10},{3,11},{4,12},{5,13},{6,14},{7,15},{8,0},{9,1},... | collective-permute-start | bytes 12582920 | tf_op jit(solution)/shard_map/ppermute | solution.py:68
  8.8 11.9 %collective-permute-start.1 = (bf16[4,80,128]{2,1,0:T(8,128)(2,1)S(1)}, bf16[4,80,128]{2,1,0:T(8,128)(2,1)S(1)}, u32[]{:S(2)}, u32[]{:S(2)}) collective-permute-start(bf16[4,80,128]{2,1,0:T(8,128)(2,1)S(1)} %pad_maximum_fusion.7), channel_id=1, source_target_pairs={{0,6},{1,7},{2,4},{3,5},{4,2},{5,3},{6,0},{7,1},{8,14},{9,15},{10,... | collective-permute-start | bytes 245768 | tf_op jit(solution)/shard_map/ppermute | solution.py:68
  13.8 7.2 %collective-permute-start.2 = (bf16[4,80,128]{2,1,0:T(8,128)(2,1)S(1)}, bf16[4,80,128]{2,1,0:T(8,128)(2,1)S(1)}, u32[]{:S(2)}, u32[]{:S(2)}) collective-permute-start(bf16[4,80,128]{2,1,0:T(8,128)(2,1)S(1)} %pad_maximum_fusion.7), channel_id=1, source_target_pairs={{0,4},{1,5},{2,6},{3,7},{4,0},{5,1},{6,2},{7,3},{8,12},{9,13},{10,... | collective-permute-start | bytes 245768 | tf_op jit(solution)/shard_map/ppermute | solution.py:68
  13.9 7.2 %collective-permute-start.3 = (bf16[4,80,128]{2,1,0:T(8,128)(2,1)S(1)}, bf16[4,80,128]{2,1,0:T(8,128)(2,1)S(1)}, u32[]{:S(2)}, u32[]{:S(2)}) collective-permute-start(bf16[4,80,128]{2,1,0:T(8,128)(2,1)S(1)} %pad_maximum_fusion.7), channel_id=1, source_target_pairs={{0,2},{1,3},{2,0},{3,1},{4,6},{5,7},{6,4},{7,5},{8,10},{9,11},{10,... | collective-permute-start | bytes 245768 | tf_op jit(solution)/shard_map/ppermute | solution.py:68
  14.5 6.6 %collective-permute-start.4 = (bf16[4,80,128]{2,1,0:T(8,128)(2,1)S(1)}, bf16[4,80,128]{2,1,0:T(8,128)(2,1)S(1)}, u32[]{:S(2)}, u32[]{:S(2)}) collective-permute-start(bf16[4,80,128]{2,1,0:T(8,128)(2,1)S(1)} %pad_maximum_fusion.7), channel_id=1, source_target_pairs={{0,17},{1,16},{2,19},{3,18},{4,21},{5,20},{6,23},{7,22},{8,25},{9,... | collective-permute-start | bytes 245768 | tf_op jit(solution)/shard_map/ppermute | solution.py:68
  21.1 6.5 %collective-permute-start.6 = (bf16[4,80,128]{2,1,0:T(8,128)(2,1)S(1)}, bf16[4,80,128]{2,1,0:T(8,128)(2,1)S(1)}, u32[]{:S(2)}, u32[]{:S(2)}) collective-permute-start(bf16[4,80,128]{2,1,0:T(8,128)(2,1)S(1)} %collective-permute-done.4), channel_id=1, source_target_pairs={{0,6},{1,7},{2,4},{3,5},{4,2},{5,3},{6,0},{7,1},{8,14},{9,15},{10,... | collective-permute-start | bytes 245768 | tf_op jit(solution)/shard_map/ppermute | solution.py:68
  24.4 6.5 %collective-permute-start.7 = (bf16[4,80,128]{2,1,0:T(8,128)(2,1)S(1)}, bf16[4,80,128]{2,1,0:T(8,128)(2,1)S(1)}, u32[]{:S(2)}, u32[]{:S(2)}) collective-permute-start(bf16[4,80,128]{2,1,0:T(8,128)(2,1)S(1)} %collective-permute-done.4), channel_id=1, source_target_pairs={{0,4},{1,5},{2,6},{3,7},{4,0},{5,1},{6,2},{7,3},{8,12},{9,13},{10,... | collective-permute-start | bytes 245768 | tf_op jit(solution)/shard_map/ppermute | solution.py:68
  24.4 6.5 %collective-permute-start.8 = (bf16[4,80,128]{2,1,0:T(8,128)(2,1)S(1)}, bf16[4,80,128]{2,1,0:T(8,128)(2,1)S(1)}, u32[]{:S(2)}, u32[]{:S(2)}) collective-permute-start(bf16[4,80,128]{2,1,0:T(8,128)(2,1)S(1)} %collective-permute-done.4), channel_id=1, source_target_pairs={{0,2},{1,3},{2,0},{3,1},{4,6},{5,7},{6,4},{7,5},{8,10},{9,11},{10,... | collective-permute-start | bytes 245768 | tf_op jit(solution)/shard_map/ppermute | solution.py:68
  25.5 12.3 %collective-permute-start.10 = (bf16[16,80,128]{2,1,0:T(8,128)(2,1)S(1)}, bf16[16,80,128]{2,1,0:T(8,128)(2,1)S(1)}, u32[]{:S(2)}, u32[]{:S(2)}) collective-permute-start(bf16[16,80,128]{2,1,0:T(8,128)(2,1)S(1)} %pad_maximum_fusion.field), channel_id=1, source_target_pairs={{0,16},{1,17},{2,18},{3,19},{4,20},{5,21},{6,22},{7,23},{8,9},{9,8... | collective-permute-start | bytes 983048 | tf_op jit(solution)/shard_map/ppermute | solution.py:68
  27.6 10.2 %collective-permute-start.9 = (bf16[16,80,128]{2,1,0:T(8,128)(2,1)S(1)}, bf16[16,80,128]{2,1,0:T(8,128)(2,1)S(1)}, u32[]{:S(2)}, u32[]{:S(2)}) collective-permute-start(bf16[16,80,128]{2,1,0:T(8,128)(2,1)S(1)} %pad_maximum_fusion.field), channel_id=1, source_target_pairs={{0,1},{1,0},{2,3},{3,2},{4,5},{5,4},{6,7},{7,6},{8,24},{9,25},{10,... | collective-permute-start | bytes 983048 | tf_op jit(solution)/shard_map/ppermute | solution.py:68
  43.7 7.8 %collective-permute-start.11 = (bf16[4,64,128]{2,1,0:T(8,128)(2,1)S(1)}, bf16[4,64,128]{2,1,0:T(8,128)(2,1)S(1)}, u32[]{:S(2)}, u32[]{:S(2)}) collective-permute-start(bf16[4,64,128]{2,1,0:T(8,128)(2,1)S(1)} %get-tuple-element.114), channel_id=1, source_target_pairs={{0,6},{1,7},{2,4},{3,5},{4,2},{5,3},{6,0},{7,1},{8,14},{9,15},{10,... | collective-permute-start | bytes 196616 | tf_op jit(solution)/shard_map/ppermute | solution.py:68
  45.9 8.9 %collective-permute-start.14 = (bf16[16,64,128]{2,1,0:T(8,128)(2,1)S(1)}, bf16[16,64,128]{2,1,0:T(8,128)(2,1)S(1)}, u32[]{:S(2)}, u32[]{:S(2)}) collective-permute-start(bf16[16,64,128]{2,1,0:T(8,128)(2,1)S(1)} %get-tuple-element.119), channel_id=1, source_target_pairs={{0,1},{1,0},{2,3},{3,2},{4,5},{5,4},{6,7},{7,6},{8,24},{9,25},{10,... | collective-permute-start | bytes 786440 | tf_op jit(solution)/shard_map/ppermute | solution.py:68
  46.5 8.3 %collective-permute-start.15 = (bf16[16,64,128]{2,1,0:T(8,128)(2,1)S(1)}, bf16[16,64,128]{2,1,0:T(8,128)(2,1)S(1)}, u32[]{:S(2)}, u32[]{:S(2)}) collective-permute-start(bf16[16,64,128]{2,1,0:T(8,128)(2,1)S(1)} %get-tuple-element.120), channel_id=1, source_target_pairs={{0,16},{1,17},{2,18},{3,19},{4,20},{5,21},{6,22},{7,23},{8,9},{9,8... | collective-permute-start | bytes 786440 | tf_op jit(solution)/shard_map/ppermute | solution.py:68
  48.4 5.8 %collective-permute-start.13 = (bf16[4,64,128]{2,1,0:T(8,128)(2,1)S(1)}, bf16[4,64,128]{2,1,0:T(8,128)(2,1)S(1)}, u32[]{:S(2)}, u32[]{:S(2)}) collective-permute-start(bf16[4,64,128]{2,1,0:T(8,128)(2,1)S(1)} %get-tuple-element.118), channel_id=1, source_target_pairs={{0,2},{1,3},{2,0},{3,1},{4,6},{5,7},{6,4},{7,5},{8,10},{9,11},{10,... | collective-permute-start | bytes 196616 | tf_op jit(solution)/shard_map/ppermute | solution.py:68
  55.9 6.8 %collective-permute-start.17 = (bf16[4,64,128]{2,1,0:T(8,128)(2,1)S(1)}, bf16[4,64,128]{2,1,0:T(8,128)(2,1)S(1)}, u32[]{:S(2)}, u32[]{:S(2)}) collective-permute-start(bf16[4,64,128]{2,1,0:T(8,128)(2,1)S(1)} %get-tuple-element.130), channel_id=1, source_target_pairs={{0,6},{1,7},{2,4},{3,5},{4,2},{5,3},{6,0},{7,1},{8,14},{9,15},{10,... | collective-permute-start | bytes 196616 | tf_op jit(solution)/shard_map/ppermute | solution.py:68
  58.3 5.8 %collective-permute-start.18 = (bf16[4,64,128]{2,1,0:T(8,128)(2,1)S(1)}, bf16[4,64,128]{2,1,0:T(8,128)(2,1)S(1)}, u32[]{:S(2)}, u32[]{:S(2)}) collective-permute-start(bf16[4,64,128]{2,1,0:T(8,128)(2,1)S(1)} %get-tuple-element.131), channel_id=1, source_target_pairs={{0,4},{1,5},{2,6},{3,7},{4,0},{5,1},{6,2},{7,3},{8,12},{9,13},{10,... | collective-permute-start | bytes 196616 | tf_op jit(solution)/shard_map/ppermute | solution.py:68
  58.3 5.8 %collective-permute-start.19 = (bf16[4,64,128]{2,1,0:T(8,128)(2,1)S(1)}, bf16[4,64,128]{2,1,0:T(8,128)(2,1)S(1)}, u32[]{:S(2)}, u32[]{:S(2)}) collective-permute-start(bf16[4,64,128]{2,1,0:T(8,128)(2,1)S(1)} %get-tuple-element.132), channel_id=1, source_target_pairs={{0,2},{1,3},{2,0},{3,1},{4,6},{5,7},{6,4},{7,5},{8,10},{9,11},{10,... | collective-permute-start | bytes 196616 | tf_op jit(solution)/shard_map/ppermute | solution.py:68
  64.2 6.9 %collective-permute-start.20 = (bf16[4,64,128]{2,1,0:T(8,128)(2,1)S(1)}, bf16[4,64,128]{2,1,0:T(8,128)(2,1)S(1)}, u32[]{:S(2)}, u32[]{:S(2)}) collective-permute-start(bf16[4,64,128]{2,1,0:T(8,128)(2,1)S(1)} %get-tuple-element.207), channel_id=1, source_target_pairs={{0,6},{1,7},{2,4},{3,5},{4,2},{5,3},{6,0},{7,1},{8,14},{9,15},{10,... | collective-permute-start | bytes 196616 | tf_op jit(solution)/shard_map/ppermute | solution.py:68
  66.2 6.4 %collective-permute-start.21 = (bf16[4,64,128]{2,1,0:T(8,128)(2,1)S(1)}, bf16[4,64,128]{2,1,0:T(8,128)(2,1)S(1)}, u32[]{:S(2)}, u32[]{:S(2)}) collective-permute-start(bf16[4,64,128]{2,1,0:T(8,128)(2,1)S(1)} %get-tuple-element.207), channel_id=1, source_target_pairs={{0,4},{1,5},{2,6},{3,7},{4,0},{5,1},{6,2},{7,3},{8,12},{9,13},{10,... | collective-permute-start | bytes 196616 | tf_op jit(solution)/shard_map/ppermute | solution.py:68
  66.2 6.4 %collective-permute-start.22 = (bf16[4,64,128]{2,1,0:T(8,128)(2,1)S(1)}, bf16[4,64,128]{2,1,0:T(8,128)(2,1)S(1)}, u32[]{:S(2)}, u32[]{:S(2)}) collective-permute-start(bf16[4,64,128]{2,1,0:T(8,128)(2,1)S(1)} %get-tuple-element.207), channel_id=1, source_target_pairs={{0,2},{1,3},{2,0},{3,1},{4,6},{5,7},{6,4},{7,5},{8,10},{9,11},{10,... | collective-permute-start | bytes 196616 | tf_op jit(solution)/shard_map/ppermute | solution.py:68
  73.8 10.5 %collective-permute-start.27 = (bf16[16,64,128]{2,1,0:T(8,128)(2,1)S(1)}, bf16[16,64,128]{2,1,0:T(8,128)(2,1)S(1)}, u32[]{:S(2)}, u32[]{:S(2)}) collective-permute-start(bf16[16,64,128]{2,1,0:T(8,128)(2,1)S(1)} %pad_maximum_fusion.2.field), channel_id=1, source_target_pairs={{0,1},{1,0},{2,3},{3,2},{4,5},{5,4},{6,7},{7,6},{8,24},{9,25},{10,... | collective-permute-start | bytes 786440 | tf_op jit(solution)/shard_map/ppermute | solution.py:68
  74.9 9.5 %collective-permute-start.28 = (bf16[16,64,128]{2,1,0:T(8,128)(2,1)S(1)}, bf16[16,64,128]{2,1,0:T(8,128)(2,1)S(1)}, u32[]{:S(2)}, u32[]{:S(2)}) collective-permute-start(bf16[16,64,128]{2,1,0:T(8,128)(2,1)S(1)} %pad_maximum_fusion.2.field), channel_id=1, source_target_pairs={{0,16},{1,17},{2,18},{3,19},{4,20},{5,21},{6,22},{7,23},{8,9},{9,8... | collective-permute-start | bytes 786440 | tf_op jit(solution)/shard_map/ppermute | solution.py:68
  76.9 6.4 %collective-permute-start.24 = (bf16[4,64,128]{2,1,0:T(8,128)(2,1)S(1)}, bf16[4,64,128]{2,1,0:T(8,128)(2,1)S(1)}, u32[]{:S(2)}, u32[]{:S(2)}) collective-permute-start(bf16[4,64,128]{2,1,0:T(8,128)(2,1)S(1)} %collective-permute-done.23), channel_id=1, source_target_pairs={{0,6},{1,7},{2,4},{3,5},{4,2},{5,3},{6,0},{7,1},{8,14},{9,15},{10,... | collective-permute-start | bytes 196616 | tf_op jit(solution)/shard_map/ppermute | solution.py:68
  78.0 6.3 %collective-permute-start.25 = (bf16[4,64,128]{2,1,0:T(8,128)(2,1)S(1)}, bf16[4,64,128]{2,1,0:T(8,128)(2,1)S(1)}, u32[]{:S(2)}, u32[]{:S(2)}) collective-permute-start(bf16[4,64,128]{2,1,0:T(8,128)(2,1)S(1)} %collective-permute-done.23), channel_id=1, source_target_pairs={{0,4},{1,5},{2,6},{3,7},{4,0},{5,1},{6,2},{7,3},{8,12},{9,13},{10,... | collective-permute-start | bytes 196616 | tf_op jit(solution)/shard_map/ppermute | solution.py:68
  78.3 6.0 %collective-permute-start.26 = (bf16[4,64,128]{2,1,0:T(8,128)(2,1)S(1)}, bf16[4,64,128]{2,1,0:T(8,128)(2,1)S(1)}, u32[]{:S(2)}, u32[]{:S(2)}) collective-permute-start(bf16[4,64,128]{2,1,0:T(8,128)(2,1)S(1)} %collective-permute-done.23), channel_id=1, source_target_pairs={{0,2},{1,3},{2,0},{3,1},{4,6},{5,7},{6,4},{7,5},{8,10},{9,11},{10,... | collective-permute-start | bytes 196616 | tf_op jit(solution)/shard_map/ppermute | solution.py:68
  90.3 9.3 %collective-permute-start.32 = (bf16[16,64,128]{2,1,0:T(8,128)(2,1)S(1)}, bf16[16,64,128]{2,1,0:T(8,128)(2,1)S(1)}, u32[]{:S(2)}, u32[]{:S(2)}) collective-permute-start(bf16[16,64,128]{2,1,0:T(8,128)(2,1)S(1)} %get-tuple-element.152), channel_id=1, source_target_pairs={{0,1},{1,0},{2,3},{3,2},{4,5},{5,4},{6,7},{7,6},{8,24},{9,25},{10,... | collective-permute-start | bytes 786440 | tf_op jit(solution)/shard_map/ppermute | solution.py:68
  91.3 8.3 %collective-permute-start.33 = (bf16[16,64,128]{2,1,0:T(8,128)(2,1)S(1)}, bf16[16,64,128]{2,1,0:T(8,128)(2,1)S(1)}, u32[]{:S(2)}, u32[]{:S(2)}) collective-permute-start(bf16[16,64,128]{2,1,0:T(8,128)(2,1)S(1)} %get-tuple-element.153), channel_id=1, source_target_pairs={{0,16},{1,17},{2,18},{3,19},{4,20},{5,21},{6,22},{7,23},{8,9},{9,8... | collective-permute-start | bytes 786440 | tf_op jit(solution)/shard_map/ppermute | solution.py:68
  91.9 6.2 %collective-permute-start.29 = (bf16[4,64,128]{2,1,0:T(8,128)(2,1)S(1)}, bf16[4,64,128]{2,1,0:T(8,128)(2,1)S(1)}, u32[]{:S(2)}, u32[]{:S(2)}) collective-permute-start(bf16[4,64,128]{2,1,0:T(8,128)(2,1)S(1)} %get-tuple-element.147), channel_id=1, source_target_pairs={{0,6},{1,7},{2,4},{3,5},{4,2},{5,3},{6,0},{7,1},{8,14},{9,15},{10,... | collective-permute-start | bytes 196616 | tf_op jit(solution)/shard_map/ppermute | solution.py:68
  93.4 6.1 %collective-permute-start.30 = (bf16[4,64,128]{2,1,0:T(8,128)(2,1)S(1)}, bf16[4,64,128]{2,1,0:T(8,128)(2,1)S(1)}, u32[]{:S(2)}, u32[]{:S(2)}) collective-permute-start(bf16[4,64,128]{2,1,0:T(8,128)(2,1)S(1)} %get-tuple-element.150), channel_id=1, source_target_pairs={{0,4},{1,5},{2,6},{3,7},{4,0},{5,1},{6,2},{7,3},{8,12},{9,13},{10,... | collective-permute-start | bytes 196616 | tf_op jit(solution)/shard_map/ppermute | solution.py:68
  99.8 6.4 %collective-permute-start.34 = (bf16[4,64,128]{2,1,0:T(8,128)(2,1)S(1)}, bf16[4,64,128]{2,1,0:T(8,128)(2,1)S(1)}, u32[]{:S(2)}, u32[]{:S(2)}) collective-permute-start(bf16[4,64,128]{2,1,0:T(8,128)(2,1)S(1)} %add_convert_fusion.1), channel_id=1, source_target_pairs={{0,17},{1,16},{2,19},{3,18},{4,21},{5,20},{6,23},{7,22},{8,25},{9,... | collective-permute-start | bytes 196616 | tf_op jit(solution)/shard_map/ppermute | solution.py:68
  101.8 6.4 %collective-permute-start.35 = (bf16[4,64,128]{2,1,0:T(8,128)(2,1)S(1)}, bf16[4,64,128]{2,1,0:T(8,128)(2,1)S(1)}, u32[]{:S(2)}, u32[]{:S(2)}) collective-permute-start(bf16[4,64,128]{2,1,0:T(8,128)(2,1)S(1)} %get-tuple-element.163), channel_id=1, source_target_pairs={{0,6},{1,7},{2,4},{3,5},{4,2},{5,3},{6,0},{7,1},{8,14},{9,15},{10,... | collective-permute-start | bytes 196616 | tf_op jit(solution)/shard_map/ppermute | solution.py:68
  103.1 8.2 %collective-permute-start.36 = (bf16[4,64,128]{2,1,0:T(8,128)(2,1)S(1)}, bf16[4,64,128]{2,1,0:T(8,128)(2,1)S(1)}, u32[]{:S(2)}, u32[]{:S(2)}) collective-permute-start(bf16[4,64,128]{2,1,0:T(8,128)(2,1)S(1)} %get-tuple-element.164), channel_id=1, source_target_pairs={{0,4},{1,5},{2,6},{3,7},{4,0},{5,1},{6,2},{7,3},{8,12},{9,13},{10,... | collective-permute-start | bytes 196616 | tf_op jit(solution)/shard_map/ppermute | solution.py:68
  104.3 7.1 %collective-permute-start.37 = (bf16[4,64,128]{2,1,0:T(8,128)(2,1)S(1)}, bf16[4,64,128]{2,1,0:T(8,128)(2,1)S(1)}, u32[]{:S(2)}, u32[]{:S(2)}) collective-permute-start(bf16[4,64,128]{2,1,0:T(8,128)(2,1)S(1)} %get-tuple-element.165), channel_id=1, source_target_pairs={{0,2},{1,3},{2,0},{3,1},{4,6},{5,7},{6,4},{7,5},{8,10},{9,11},{10,... | collective-permute-start | bytes 196616 | tf_op jit(solution)/shard_map/ppermute | solution.py:68
  111.5 6.8 %collective-permute-start.38 = (bf16[4,64,128]{2,1,0:T(8,128)(2,1)S(1)}, bf16[4,64,128]{2,1,0:T(8,128)(2,1)S(1)}, u32[]{:S(2)}, u32[]{:S(2)}) collective-permute-start(bf16[4,64,128]{2,1,0:T(8,128)(2,1)S(1)} %get-tuple-element.202), channel_id=1, source_target_pairs={{0,6},{1,7},{2,4},{3,5},{4,2},{5,3},{6,0},{7,1},{8,14},{9,15},{10,... | collective-permute-start | bytes 196616 | tf_op jit(solution)/shard_map/ppermute | solution.py:68
  112.9 8.2 %collective-permute-start.39 = (bf16[4,64,128]{2,1,0:T(8,128)(2,1)S(1)}, bf16[4,64,128]{2,1,0:T(8,128)(2,1)S(1)}, u32[]{:S(2)}, u32[]{:S(2)}) collective-permute-start(bf16[4,64,128]{2,1,0:T(8,128)(2,1)S(1)} %get-tuple-element.202), channel_id=1, source_target_pairs={{0,4},{1,5},{2,6},{3,7},{4,0},{5,1},{6,2},{7,3},{8,12},{9,13},{10,... | collective-permute-start | bytes 196616 | tf_op jit(solution)/shard_map/ppermute | solution.py:68
  112.9 8.2 %collective-permute-start.40 = (bf16[4,64,128]{2,1,0:T(8,128)(2,1)S(1)}, bf16[4,64,128]{2,1,0:T(8,128)(2,1)S(1)}, u32[]{:S(2)}, u32[]{:S(2)}) collective-permute-start(bf16[4,64,128]{2,1,0:T(8,128)(2,1)S(1)} %get-tuple-element.202), channel_id=1, source_target_pairs={{0,2},{1,3},{2,0},{3,1},{4,6},{5,7},{6,4},{7,5},{8,10},{9,11},{10,... | collective-permute-start | bytes 196616 | tf_op jit(solution)/shard_map/ppermute | solution.py:68
  121.2 11.7 %collective-permute-start.45 = (bf16[16,64,128]{2,1,0:T(8,128)(2,1)S(1)}, bf16[16,64,128]{2,1,0:T(8,128)(2,1)S(1)}, u32[]{:S(2)}, u32[]{:S(2)}) collective-permute-start(bf16[16,64,128]{2,1,0:T(8,128)(2,1)S(1)} %pad_maximum_fusion.4.field), channel_id=1, source_target_pairs={{0,1},{1,0},{2,3},{3,2},{4,5},{5,4},{6,7},{7,6},{8,24},{9,25},{10,... | collective-permute-start | bytes 786440 | tf_op jit(solution)/shard_map/ppermute | solution.py:68
  122.4 10.5 %collective-permute-start.46 = (bf16[16,64,128]{2,1,0:T(8,128)(2,1)S(1)}, bf16[16,64,128]{2,1,0:T(8,128)(2,1)S(1)}, u32[]{:S(2)}, u32[]{:S(2)}) collective-permute-start(bf16[16,64,128]{2,1,0:T(8,128)(2,1)S(1)} %pad_maximum_fusion.4.field), channel_id=1, source_target_pairs={{0,16},{1,17},{2,18},{3,19},{4,20},{5,21},{6,22},{7,23},{8,9},{9,8... | collective-permute-start | bytes 786440 | tf_op jit(solution)/shard_map/ppermute | solution.py:68
  123.0 9.8 %collective-permute-start.42 = (bf16[4,64,128]{2,1,0:T(8,128)(2,1)S(1)}, bf16[4,64,128]{2,1,0:T(8,128)(2,1)S(1)}, u32[]{:S(2)}, u32[]{:S(2)}) collective-permute-start(bf16[4,64,128]{2,1,0:T(8,128)(2,1)S(1)} %collective-permute-done.41), channel_id=1, source_target_pairs={{0,6},{1,7},{2,4},{3,5},{4,2},{5,3},{6,0},{7,1},{8,14},{9,15},{10,... | collective-permute-start | bytes 196616 | tf_op jit(solution)/shard_map/ppermute | solution.py:68
  124.8 8.0 %collective-permute-start.43 = (bf16[4,64,128]{2,1,0:T(8,128)(2,1)S(1)}, bf16[4,64,128]{2,1,0:T(8,128)(2,1)S(1)}, u32[]{:S(2)}, u32[]{:S(2)}) collective-permute-start(bf16[4,64,128]{2,1,0:T(8,128)(2,1)S(1)} %collective-permute-done.41), channel_id=1, source_target_pairs={{0,4},{1,5},{2,6},{3,7},{4,0},{5,1},{6,2},{7,3},{8,12},{9,13},{10,... | collective-permute-start | bytes 196616 | tf_op jit(solution)/shard_map/ppermute | solution.py:68
  124.8 8.0 %collective-permute-start.44 = (bf16[4,64,128]{2,1,0:T(8,128)(2,1)S(1)}, bf16[4,64,128]{2,1,0:T(8,128)(2,1)S(1)}, u32[]{:S(2)}, u32[]{:S(2)}) collective-permute-start(bf16[4,64,128]{2,1,0:T(8,128)(2,1)S(1)} %collective-permute-done.41), channel_id=1, source_target_pairs={{0,2},{1,3},{2,0},{3,1},{4,6},{5,7},{6,4},{7,5},{8,10},{9,11},{10,... | collective-permute-start | bytes 196616 | tf_op jit(solution)/shard_map/ppermute | solution.py:68
  140.0 10.7 %collective-permute-start.50 = (bf16[16,64,128]{2,1,0:T(8,128)(2,1)S(1)}, bf16[16,64,128]{2,1,0:T(8,128)(2,1)S(1)}, u32[]{:S(2)}, u32[]{:S(2)}) collective-permute-start(bf16[16,64,128]{2,1,0:T(8,128)(2,1)S(1)} %get-tuple-element.185), channel_id=1, source_target_pairs={{0,1},{1,0},{2,3},{3,2},{4,5},{5,4},{6,7},{7,6},{8,24},{9,25},{10,... | collective-permute-start | bytes 786440 | tf_op jit(solution)/shard_map/ppermute | solution.py:68
  140.9 9.8 %collective-permute-start.51 = (bf16[16,64,128]{2,1,0:T(8,128)(2,1)S(1)}, bf16[16,64,128]{2,1,0:T(8,128)(2,1)S(1)}, u32[]{:S(2)}, u32[]{:S(2)}) collective-permute-start(bf16[16,64,128]{2,1,0:T(8,128)(2,1)S(1)} %get-tuple-element.186), channel_id=1, source_target_pairs={{0,16},{1,17},{2,18},{3,19},{4,20},{5,21},{6,22},{7,23},{8,9},{9,8... | collective-permute-start | bytes 786440 | tf_op jit(solution)/shard_map/ppermute | solution.py:68
  142.9 6.3 %collective-permute-start.47 = (bf16[4,64,128]{2,1,0:T(8,128)(2,1)S(1)}, bf16[4,64,128]{2,1,0:T(8,128)(2,1)S(1)}, u32[]{:S(2)}, u32[]{:S(2)}) collective-permute-start(bf16[4,64,128]{2,1,0:T(8,128)(2,1)S(1)} %get-tuple-element.180), channel_id=1, source_target_pairs={{0,6},{1,7},{2,4},{3,5},{4,2},{5,3},{6,0},{7,1},{8,14},{9,15},{10,... | collective-permute-start | bytes 196616 | tf_op jit(solution)/shard_map/ppermute | solution.py:68
  143.8 6.8 %collective-permute-start.48 = (bf16[4,64,128]{2,1,0:T(8,128)(2,1)S(1)}, bf16[4,64,128]{2,1,0:T(8,128)(2,1)S(1)}, u32[]{:S(2)}, u32[]{:S(2)}) collective-permute-start(bf16[4,64,128]{2,1,0:T(8,128)(2,1)S(1)} %get-tuple-element.183), channel_id=1, source_target_pairs={{0,4},{1,5},{2,6},{3,7},{4,0},{5,1},{6,2},{7,3},{8,12},{9,13},{10,... | collective-permute-start | bytes 196616 | tf_op jit(solution)/shard_map/ppermute | solution.py:68
  143.9 6.8 %collective-permute-start.49 = (bf16[4,64,128]{2,1,0:T(8,128)(2,1)S(1)}, bf16[4,64,128]{2,1,0:T(8,128)(2,1)S(1)}, u32[]{:S(2)}, u32[]{:S(2)}) collective-permute-start(bf16[4,64,128]{2,1,0:T(8,128)(2,1)S(1)} %get-tuple-element.184), channel_id=1, source_target_pairs={{0,2},{1,3},{2,0},{3,1},{4,6},{5,7},{6,4},{7,5},{8,10},{9,11},{10,... | collective-permute-start | bytes 196616 | tf_op jit(solution)/shard_map/ppermute | solution.py:68
  151.5 6.1 %collective-permute-start.53 = (bf16[4,64,128]{2,1,0:T(8,128)(2,1)S(1)}, bf16[4,64,128]{2,1,0:T(8,128)(2,1)S(1)}, u32[]{:S(2)}, u32[]{:S(2)}) collective-permute-start(bf16[4,64,128]{2,1,0:T(8,128)(2,1)S(1)} %get-tuple-element.196), channel_id=1, source_target_pairs={{0,6},{1,7},{2,4},{3,5},{4,2},{5,3},{6,0},{7,1},{8,14},{9,15},{10,... | collective-permute-start | bytes 196616 | tf_op jit(solution)/shard_map/ppermute | solution.py:68
  152.9 6.1 %collective-permute-start.54 = (bf16[4,64,128]{2,1,0:T(8,128)(2,1)S(1)}, bf16[4,64,128]{2,1,0:T(8,128)(2,1)S(1)}, u32[]{:S(2)}, u32[]{:S(2)}) collective-permute-start(bf16[4,64,128]{2,1,0:T(8,128)(2,1)S(1)} %get-tuple-element.197), channel_id=1, source_target_pairs={{0,4},{1,5},{2,6},{3,7},{4,0},{5,1},{6,2},{7,3},{8,12},{9,13},{10,... | collective-permute-start | bytes 196616 | tf_op jit(solution)/shard_map/ppermute | solution.py:68
  (13 other events, 114.4 us)
where the time goes:
time: 162 us
  starting transfers between devices  80.5 us (50%)
  waiting for transfers between devices  32.7 us (20%)
  Pallas kernels  32 us (20%)
  local copies, waits for them, and re-layouts  9.23 us (6%)
  other arithmetic  5.66 us (3%)
  between operations  1.64 us (1%)
    ppermute x57, starting transfers between devices, send(): return lax.ppermute(block, BOTH, route)  80.5 us
    ppermute x57, waiting for transfers between devices, send(): return lax.ppermute(block, BOTH, route)  32.7 us
    pallas_call x9, Pallas kernels, call(): pl.pallas_call(kernel, out_shape=outs, in_specs=[place[kind] for kind in...  28.2 us
    unnamed x10, local copies, waits for them, and re-layouts  6.95 us
  transfers between devices with their start and end apart: 57, of which 22 were waited for; matrix products, arithmetic and copies ran while one was open for 4% of the time, Pallas kernels for 9%

commit v1 on v0

--- a/solution.py
+++ b/solution.py
@@ -11,7 +11,7 @@
 PT_DEV = 16
 ITERS = 3
 CORES = 2
-UNROLL = 8
+UNROLL = 16
 AREAS = 2
 NEAR = 2 * AREAS
 
@@ -328,6 +328,8 @@
     copy.start()
     assemble(pieces, field)
     total[...] = jnp.zeros_like(total)
+    acc[...] = part[...]
+    sides[...] = sides_in[...]
     points = acc.shape[0]
     low[points] = jnp.zeros(low.shape[1:], jnp.bfloat16)
     copy.wait()
@@ -463,16 +465,15 @@
     names = jnp.pad(names, ((0, 0), (0, width * params - names.shape[1])))
     extra = jnp.concatenate([prior_weight, names.reshape(3 * width, params)])
     extra = jnp.pad(extra, ((0, -extra.shape[0] % 16), (0, 0))).reshape(2, -1, params)
-    pack = jnp.concatenate([half(turned, 1 - core), extra], axis=1)
+    pack = lax.optimization_barrier(jnp.concatenate([half(turned, 1 - core), extra], axis=1))
     other_tiles = grid.swap(jac_tiles)
     theirs = grid.swap(pack)
     right_side = in_order(core, half(turned, core), theirs[:, :rows], 0)
-    theirs = theirs[:, rows:].reshape(-1, params)
-    weights = in_order(core, prior_weight, theirs[:2], 0)
-    names = theirs[2 : 2 + 3 * width].reshape(3, -1)[:, : tile_pose.shape[0]].astype(jnp.int32)
-    indices = jnp.stack([tile_pose, tile_point, tile_valid])
-    shift = jnp.array([[0], [PT_DEV], [0]], jnp.int32)
-    indices = jnp.concatenate([indices, names + shift], axis=1)
+    notes = [v[:, rows:].reshape(-1, params) for v in (pack, theirs)]
+    weights = in_order(core, notes[0][:2], notes[1][:2], 0)
+    names = [v[2 : 2 + 3 * width].reshape(3, -1)[:, : tile_pose.shape[0]] for v in notes]
+    shift = jnp.array([[0.0], [PT_DEV], [0.0]], jnp.float32)
+    indices = jnp.concatenate([names[0], names[1] + shift], axis=1).astype(jnp.int32)
     near = []
     for home in homes:
         near += grid.spot(2 * jnp.maximum(home - 1, 0), place)

time: 162 us -> 158 us (0.975)
  Pallas kernels: 32 us -> 26 us
  other arithmetic: 5.66 us -> 3.56 us
  waiting for transfers between devices: 32.7 us -> 34.5 us
    pallas_call x9, Pallas kernels: 28.2 us -> 22.1 us  [call(): pl.pallas_call(kernel, out_shape=outs, in_specs=[place[kind] for kind in...]
    ppermute x57, waiting for transfers between devices: 32.7 us -> 34.5 us  [send(): return lax.ppermute(block, BOTH, route)]
    ppermute x57, starting transfers between devices: 80.5 us -> 82.1 us  [send(): return lax.ppermute(block, BOTH, route)]
  transfers between devices with their start and end apart: 57 -> 57, of which waited for: 22 -> 22; matrix products, arithmetic and copies ran while one was open for 4% -> 3% of each run, Pallas kernels for 9% -> 9%
where the time goes in v1:
time: 158 us; the launch traced here: 157 us
  starting transfers between devices  82.1 us (52%)
  waiting for transfers between devices  34.5 us (22%)
  Pallas kernels  26 us (16%)
  local copies, waits for them, and re-layouts  9.51 us (6%)
  other arithmetic  3.56 us (2%)
  between operations  1.64 us (1%)
    ppermute x57, starting transfers between devices, send(): return lax.ppermute(block, BOTH, route)  82.1 us
    ppermute x57, waiting for transfers between devices, send(): return lax.ppermute(block, BOTH, route)  34.5 us
    pallas_call x9, Pallas kernels, call(): pl.pallas_call(kernel, out_shape=outs, in_specs=[place[kind] for kind in...  22.1 us
    unnamed x10, local copies, waits for them, and re-layouts  7.23 us
  transfers between devices with their start and end apart: 57, of which 22 were waited for; matrix products, arithmetic and copies ran while one was open for 3% of the time, Pallas kernels for 9%

profile of v1, /device:TPU:0, one launch (start us, length us, event | category | flops | bytes accessed | tf_op | source)
XLA Modules:
  0.0 157.3 jit_solution(8017354107118734662)
XLA Ops:
  4.4 3.6 %collective-permute-done = f32[2,72,128]{2,1,0:T(8,128)S(1)} collective-permute-done((f32[2,72,128]{2,1,0:T(8,128)S(1)}, f32[2,72,128]{2,1,0:T(8,128)S(1)}, u32[]{:S(2)}, u32[]{:S(2)}) %collective-permute-start) | collective-permute-done | bytes 73760 | tf_op jit(solution)/shard_map/ppermute | solution.py:68
  8.1 5.0 %collective-permute-start.1 = (bf16[4,80,128]{2,1,0:T(8,128)(2,1)S(1)}, bf16[4,80,128]{2,1,0:T(8,128)(2,1)S(1)}, u32[]{:S(2)}, u32[]{:S(2)}) collective-permute-start(bf16[4,80,128]{2,1,0:T(8,128)(2,1)S(1)} %pad_maximum_fusion.7), channel_id=1, source_target_pairs={{0,6},{1,7},{2,4},{3,5},{4,2},{5,3},{6,0},{7,1},{8,14},{9,15},{10,... | collective-permute-start | bytes 245768 | tf_op jit(solution)/shard_map/ppermute | solution.py:68
  13.8 2.6 %collective-permute-start.4 = (bf16[4,80,128]{2,1,0:T(8,128)(2,1)S(1)}, bf16[4,80,128]{2,1,0:T(8,128)(2,1)S(1)}, u32[]{:S(2)}, u32[]{:S(2)}) collective-permute-start(bf16[4,80,128]{2,1,0:T(8,128)(2,1)S(1)} %pad_maximum_fusion.7), channel_id=1, source_target_pairs={{0,17},{1,16},{2,19},{3,18},{4,21},{5,20},{6,23},{7,22},{8,25},{9,... | collective-permute-start | bytes 245768 | tf_op jit(solution)/shard_map/ppermute | solution.py:68
  18.6 1.7 %collective-permute-done.2 = bf16[4,80,128]{2,1,0:T(8,128)(2,1)S(1)} collective-permute-done((bf16[4,80,128]{2,1,0:T(8,128)(2,1)S(1)}, bf16[4,80,128]{2,1,0:T(8,128)(2,1)S(1)}, u32[]{:S(2)}, u32[]{:S(2)}) %collective-permute-start.2) | collective-permute-done | bytes 81952 | tf_op jit(solution)/shard_map/ppermute | solution.py:68
  20.4 2.5 %collective-permute-start.6 = (bf16[4,80,128]{2,1,0:T(8,128)(2,1)S(1)}, bf16[4,80,128]{2,1,0:T(8,128)(2,1)S(1)}, u32[]{:S(2)}, u32[]{:S(2)}) collective-permute-start(bf16[4,80,128]{2,1,0:T(8,128)(2,1)S(1)} %collective-permute-done.4), channel_id=1, source_target_pairs={{0,6},{1,7},{2,4},{3,5},{4,2},{5,3},{6,0},{7,1},{8,14},{9,15},{10,... | collective-permute-start | bytes 245768 | tf_op jit(solution)/shard_map/ppermute | solution.py:68
  22.9 1.9 %collective-permute-start.8 = (bf16[4,80,128]{2,1,0:T(8,128)(2,1)S(1)}, bf16[4,80,128]{2,1,0:T(8,128)(2,1)S(1)}, u32[]{:S(2)}, u32[]{:S(2)}) collective-permute-start(bf16[4,80,128]{2,1,0:T(8,128)(2,1)S(1)} %collective-permute-done.4), channel_id=1, source_target_pairs={{0,2},{1,3},{2,0},{3,1},{4,6},{5,7},{6,4},{7,5},{8,10},{9,11},{10,... | collective-permute-start | bytes 245768 | tf_op jit(solution)/shard_map/ppermute | solution.py:68
  28.4 1.9 %collective-permute-done.7 = bf16[4,80,128]{2,1,0:T(8,128)(2,1)S(1)} collective-permute-done((bf16[4,80,128]{2,1,0:T(8,128)(2,1)S(1)}, bf16[4,80,128]{2,1,0:T(8,128)(2,1)S(1)}, u32[]{:S(2)}, u32[]{:S(2)}) %collective-permute-start.7) | collective-permute-done | bytes 81952 | tf_op jit(solution)/shard_map/ppermute | solution.py:68
  30.4 2.2 %copy-done.3 = bf16[128,128,128]{2,1,0:T(8,128)(2,1)S(1)} copy-done((bf16[128,128,128]{2,1,0:T(8,128)(2,1)S(1)}, bf16[128,128,128]{2,1,0:T(8,128)(2,1)}, u32[]{:S(2)}) %copy-start.3) | copy-done | bytes 4194328
  32.5 2.5 %shard_map.87.tiles = bf16[256,128,128]{2,1,0:T(8,128)(2,1)S(1)} custom-call(bf16[128,128,128]{2,1,0:T(8,128)(2,1)S(1)} %copy-done.3, bf16[128,128,128]{2,1,0:T(8,128)(2,1)} %collective-permute-done.5.second), custom_call_target="tpu_custom_call" | custom-call | tf_op jit(solution)/shard_map/pallas_call | solution.py:245
  35.0 1.7 %shard_map.88 = (f32[32,64,128]{2,1,0:T(8,128)S(1)}, bf16[4,2,80,128]{3,2,1,0:T(8,128)(2,1)S(1)}) custom-call(s32[8,384]{1,0:T(8,128)S(1)} %shard_map.86.plan_in, bf16[256,128,128]{2,1,0:T(8,128)(2,1)S(1)} %shard_map.87.tiles, bf16[16,80,128]{2,1,0:T(8,128)(2,1)S(1)} %pad_maximum_fusion.field), custom_call_target="tpu_custom_call" | custom-call | flops 268435456 | bytes 8388608 | tf_op jit(solution)/shard_map/pallas_call | solution.py:361
  36.8 4.1 %shard_map.89 = (f32[32,64,128]{2,1,0:T(8,128)S(1)}, bf16[4,2,80,128]{3,2,1,0:T(8,128)(2,1)S(1)}, bf16[33,64,128]{2,1,0:T(8,128)(2,1)S(1)}, bf16[16,64,128]{2,1,...) custom-call(s32[8,384]{1,0:T(8,128)S(1)} %shard_map.86.plan_in, ...), custom_call_target="tpu_custom_call", output_to_operand_aliasing={{0}: (2, {}), {1}: (3, {})} | custom-call | flops 1610612736 | bytes 8388608 | tf_op jit(solution)/shard_map/pallas_call | solution.py:361
  40.9 2.6 %collective-permute-start.11 = (bf16[4,64,128]{2,1,0:T(8,128)(2,1)S(1)}, bf16[4,64,128]{2,1,0:T(8,128)(2,1)S(1)}, u32[]{:S(2)}, u32[]{:S(2)}) collective-permute-start(bf16[4,64,128]{2,1,0:T(8,128)(2,1)S(1)} %get-tuple-element.114), channel_id=1, source_target_pairs={{0,6},{1,7},{2,4},{3,5},{4,2},{5,3},{6,0},{7,1},{8,14},{9,15},{10,... | collective-permute-start | bytes 196616 | tf_op jit(solution)/shard_map/ppermute | solution.py:68
  46.4 2.8 %collective-permute-start.13 = (bf16[4,64,128]{2,1,0:T(8,128)(2,1)S(1)}, bf16[4,64,128]{2,1,0:T(8,128)(2,1)S(1)}, u32[]{:S(2)}, u32[]{:S(2)}) collective-permute-start(bf16[4,64,128]{2,1,0:T(8,128)(2,1)S(1)} %get-tuple-element.118), channel_id=1, source_target_pairs={{0,2},{1,3},{2,0},{3,1},{4,6},{5,7},{6,4},{7,5},{8,10},{9,11},{10,... | collective-permute-start | bytes 196616 | tf_op jit(solution)/shard_map/ppermute | solution.py:68
  52.2 2.2 %collective-permute-start.16 = (bf16[4,64,128]{2,1,0:T(8,128)(2,1)S(1)}, bf16[4,64,128]{2,1,0:T(8,128)(2,1)S(1)}, u32[]{:S(2)}, u32[]{:S(2)}) collective-permute-start(bf16[4,64,128]{2,1,0:T(8,128)(2,1)S(1)} %add_convert_fusion.2), channel_id=1, source_target_pairs={{0,17},{1,16},{2,19},{3,18},{4,21},{5,20},{6,23},{7,22},{8,25},{9,... | collective-permute-start | bytes 196616 | tf_op jit(solution)/shard_map/ppermute | solution.py:68
  55.8 3.0 %collective-permute-start.19 = (bf16[4,64,128]{2,1,0:T(8,128)(2,1)S(1)}, bf16[4,64,128]{2,1,0:T(8,128)(2,1)S(1)}, u32[]{:S(2)}, u32[]{:S(2)}) collective-permute-start(bf16[4,64,128]{2,1,0:T(8,128)(2,1)S(1)} %get-tuple-element.132), channel_id=1, source_target_pairs={{0,2},{1,3},{2,0},{3,1},{4,6},{5,7},{6,4},{7,5},{8,10},{9,11},{10,... | collective-permute-start | bytes 196616 | tf_op jit(solution)/shard_map/ppermute | solution.py:68
  58.9 2.4 %collective-permute-done.17 = bf16[4,64,128]{2,1,0:T(8,128)(2,1)S(1)} collective-permute-done((bf16[4,64,128]{2,1,0:T(8,128)(2,1)S(1)}, bf16[4,64,128]{2,1,0:T(8,128)(2,1)S(1)}, u32[]{:S(2)}, u32[]{:S(2)}) %collective-permute-start.17) | collective-permute-done | bytes 65568 | tf_op jit(solution)/shard_map/ppermute | solution.py:68
  62.3 1.6 collective-permute-start.20
  64.7 2.0 %collective-permute-start.22 = (bf16[4,64,128]{2,1,0:T(8,128)(2,1)S(1)}, bf16[4,64,128]{2,1,0:T(8,128)(2,1)S(1)}, u32[]{:S(2)}, u32[]{:S(2)}) collective-permute-start(bf16[4,64,128]{2,1,0:T(8,128)(2,1)S(1)} %get-tuple-element.207), channel_id=1, source_target_pairs={{0,2},{1,3},{2,0},{3,1},{4,6},{5,7},{6,4},{7,5},{8,10},{9,11},{10,... | collective-permute-start | bytes 196616 | tf_op jit(solution)/shard_map/ppermute | solution.py:68
  70.1 1.8 %collective-permute-done.23 = bf16[4,64,128]{2,1,0:T(8,128)(2,1)S(1)} collective-permute-done((bf16[4,64,128]{2,1,0:T(8,128)(2,1)S(1)}, bf16[4,64,128]{2,1,0:T(8,128)(2,1)S(1)}, u32[]{:S(2)}, u32[]{:S(2)}) %collective-permute-start.23) | collective-permute-done | bytes 65568 | tf_op jit(solution)/shard_map/ppermute | solution.py:68
  74.0 2.2 %collective-permute-start.24 = (bf16[4,64,128]{2,1,0:T(8,128)(2,1)S(1)}, bf16[4,64,128]{2,1,0:T(8,128)(2,1)S(1)}, u32[]{:S(2)}, u32[]{:S(2)}) collective-permute-start(bf16[4,64,128]{2,1,0:T(8,128)(2,1)S(1)} %collective-permute-done.23), channel_id=1, source_target_pairs={{0,6},{1,7},{2,4},{3,5},{4,2},{5,3},{6,0},{7,1},{8,14},{9,15},{10,... | collective-permute-start | bytes 196616 | tf_op jit(solution)/shard_map/ppermute | solution.py:68
  76.1 2.2 %collective-permute-start.26 = (bf16[4,64,128]{2,1,0:T(8,128)(2,1)S(1)}, bf16[4,64,128]{2,1,0:T(8,128)(2,1)S(1)}, u32[]{:S(2)}, u32[]{:S(2)}) collective-permute-start(bf16[4,64,128]{2,1,0:T(8,128)(2,1)S(1)} %collective-permute-done.23), channel_id=1, source_target_pairs={{0,2},{1,3},{2,0},{3,1},{4,6},{5,7},{6,4},{7,5},{8,10},{9,11},{10,... | collective-permute-start | bytes 196616 | tf_op jit(solution)/shard_map/ppermute | solution.py:68
  78.4 1.8 %shard_map.91 = (f32[32,64,128]{2,1,0:T(8,128)S(1)}, bf16[4,2,64,128]{3,2,1,0:T(8,128)(2,1)S(1)}) custom-call(s32[8,384]{1,0:T(8,128)S(1)} %shard_map.86.plan_in, bf16[256,128,128]{2,1,0:T(8,128)(2,1)S(1)} %shard_map.87.tiles, bf16[16,64,128]{2,1,0:T(8,128)(2,1)S(1)} %pad_maximum_fusion.2.field), custom_call_target="tpu_custom_call" | custom-call | flops 268435456 | bytes 8388608 | tf_op jit(solution)/shard_map/pallas_call | solution.py:361
  81.5 4.1 %shard_map.92 = (f32[32,64,128]{2,1,0:T(8,128)S(1)}, bf16[4,2,64,128]{3,2,1,0:T(8,128)(2,1)S(1)}, bf16[33,64,128]{2,1,0:T(8,128)(2,1)S(1)}, bf16[16,64,128]{2,1,...) custom-call(s32[8,384]{1,0:T(8,128)S(1)} %shard_map.86.plan_in, ...), custom_call_target="tpu_custom_call", output_to_operand_aliasing={{0}: (2, {}), {1}: (3, {})} | custom-call | flops 1610612736 | bytes 8388608 | tf_op jit(solution)/shard_map/pallas_call | solution.py:361
  85.7 2.2 %collective-permute-start.32 = (bf16[16,64,128]{2,1,0:T(8,128)(2,1)S(1)}, bf16[16,64,128]{2,1,0:T(8,128)(2,1)S(1)}, u32[]{:S(2)}, u32[]{:S(2)}) collective-permute-start(bf16[16,64,128]{2,1,0:T(8,128)(2,1)S(1)} %get-tuple-element.152), channel_id=1, source_target_pairs={{0,1},{1,0},{2,3},{3,2},{4,5},{5,4},{6,7},{7,6},{8,24},{9,25},{10,... | collective-permute-start | bytes 786440 | tf_op jit(solution)/shard_map/ppermute | solution.py:68
  89.7 1.6 %collective-permute-start.30 = (bf16[4,64,128]{2,1,0:T(8,128)(2,1)S(1)}, bf16[4,64,128]{2,1,0:T(8,128)(2,1)S(1)}, u32[]{:S(2)}, u32[]{:S(2)}) collective-permute-start(bf16[4,64,128]{2,1,0:T(8,128)(2,1)S(1)} %get-tuple-element.150), channel_id=1, source_target_pairs={{0,4},{1,5},{2,6},{3,7},{4,0},{5,1},{6,2},{7,3},{8,12},{9,13},{10,... | collective-permute-start | bytes 196616 | tf_op jit(solution)/shard_map/ppermute | solution.py:68
  91.2 1.8 %collective-permute-start.31 = (bf16[4,64,128]{2,1,0:T(8,128)(2,1)S(1)}, bf16[4,64,128]{2,1,0:T(8,128)(2,1)S(1)}, u32[]{:S(2)}, u32[]{:S(2)}) collective-permute-start(bf16[4,64,128]{2,1,0:T(8,128)(2,1)S(1)} %get-tuple-element.151), channel_id=1, source_target_pairs={{0,2},{1,3},{2,0},{3,1},{4,6},{5,7},{6,4},{7,5},{8,10},{9,11},{10,... | collective-permute-start | bytes 196616 | tf_op jit(solution)/shard_map/ppermute | solution.py:68
  93.0 1.7 %collective-permute-done.29 = bf16[4,64,128]{2,1,0:T(8,128)(2,1)S(1)} collective-permute-done((bf16[4,64,128]{2,1,0:T(8,128)(2,1)S(1)}, bf16[4,64,128]{2,1,0:T(8,128)(2,1)S(1)}, u32[]{:S(2)}, u32[]{:S(2)}) %collective-permute-start.29) | collective-permute-done | bytes 65568 | tf_op jit(solution)/shard_map/ppermute | solution.py:68
  96.5 1.6 collective-permute-start.34
  98.0 2.1 %collective-permute-start.35 = (bf16[4,64,128]{2,1,0:T(8,128)(2,1)S(1)}, bf16[4,64,128]{2,1,0:T(8,128)(2,1)S(1)}, u32[]{:S(2)}, u32[]{:S(2)}) collective-permute-start(bf16[4,64,128]{2,1,0:T(8,128)(2,1)S(1)} %get-tuple-element.163), channel_id=1, source_target_pairs={{0,6},{1,7},{2,4},{3,5},{4,2},{5,3},{6,0},{7,1},{8,14},{9,15},{10,... | collective-permute-start | bytes 196616 | tf_op jit(solution)/shard_map/ppermute | solution.py:68
  100.1 2.3 %collective-permute-start.37 = (bf16[4,64,128]{2,1,0:T(8,128)(2,1)S(1)}, bf16[4,64,128]{2,1,0:T(8,128)(2,1)S(1)}, u32[]{:S(2)}, u32[]{:S(2)}) collective-permute-start(bf16[4,64,128]{2,1,0:T(8,128)(2,1)S(1)} %get-tuple-element.165), channel_id=1, source_target_pairs={{0,2},{1,3},{2,0},{3,1},{4,6},{5,7},{6,4},{7,5},{8,10},{9,11},{10,... | collective-permute-start | bytes 196616 | tf_op jit(solution)/shard_map/ppermute | solution.py:68
  102.4 2.1 %collective-permute-done.35 = bf16[4,64,128]{2,1,0:T(8,128)(2,1)S(1)} collective-permute-done((bf16[4,64,128]{2,1,0:T(8,128)(2,1)S(1)}, bf16[4,64,128]{2,1,0:T(8,128)(2,1)S(1)}, u32[]{:S(2)}, u32[]{:S(2)}) %collective-permute-start.35) | collective-permute-done | bytes 65568 | tf_op jit(solution)/shard_map/ppermute | solution.py:68
  104.5 3.0 %collective-permute-done.36 = bf16[4,64,128]{2,1,0:T(8,128)(2,1)S(1)} collective-permute-done((bf16[4,64,128]{2,1,0:T(8,128)(2,1)S(1)}, bf16[4,64,128]{2,1,0:T(8,128)(2,1)S(1)}, u32[]{:S(2)}, u32[]{:S(2)}) %collective-permute-start.36) | collective-permute-done | bytes 65568 | tf_op jit(solution)/shard_map/ppermute | solution.py:68
  107.7 2.5 %collective-permute-start.38 = (bf16[4,64,128]{2,1,0:T(8,128)(2,1)S(1)}, bf16[4,64,128]{2,1,0:T(8,128)(2,1)S(1)}, u32[]{:S(2)}, u32[]{:S(2)}) collective-permute-start(bf16[4,64,128]{2,1,0:T(8,128)(2,1)S(1)} %get-tuple-element.202), channel_id=1, source_target_pairs={{0,6},{1,7},{2,4},{3,5},{4,2},{5,3},{6,0},{7,1},{8,14},{9,15},{10,... | collective-permute-start | bytes 196616 | tf_op jit(solution)/shard_map/ppermute | solution.py:68
  110.1 2.0 %collective-permute-start.40 = (bf16[4,64,128]{2,1,0:T(8,128)(2,1)S(1)}, bf16[4,64,128]{2,1,0:T(8,128)(2,1)S(1)}, u32[]{:S(2)}, u32[]{:S(2)}) collective-permute-start(bf16[4,64,128]{2,1,0:T(8,128)(2,1)S(1)} %get-tuple-element.202), channel_id=1, source_target_pairs={{0,2},{1,3},{2,0},{3,1},{4,6},{5,7},{6,4},{7,5},{8,10},{9,11},{10,... | collective-permute-start | bytes 196616 | tf_op jit(solution)/shard_map/ppermute | solution.py:68
  114.0 3.3 %collective-permute-done.39 = bf16[4,64,128]{2,1,0:T(8,128)(2,1)S(1)} collective-permute-done((bf16[4,64,128]{2,1,0:T(8,128)(2,1)S(1)}, bf16[4,64,128]{2,1,0:T(8,128)(2,1)S(1)}, u32[]{:S(2)}, u32[]{:S(2)}) %collective-permute-start.39) | collective-permute-done | bytes 65568 | tf_op jit(solution)/shard_map/ppermute | solution.py:68
  119.4 1.9 %collective-permute-start.42 = (bf16[4,64,128]{2,1,0:T(8,128)(2,1)S(1)}, bf16[4,64,128]{2,1,0:T(8,128)(2,1)S(1)}, u32[]{:S(2)}, u32[]{:S(2)}) collective-permute-start(bf16[4,64,128]{2,1,0:T(8,128)(2,1)S(1)} %collective-permute-done.41), channel_id=1, source_target_pairs={{0,6},{1,7},{2,4},{3,5},{4,2},{5,3},{6,0},{7,1},{8,14},{9,15},{10,... | collective-permute-start | bytes 196616 | tf_op jit(solution)/shard_map/ppermute | solution.py:68
  121.3 2.5 %collective-permute-start.44 = (bf16[4,64,128]{2,1,0:T(8,128)(2,1)S(1)}, bf16[4,64,128]{2,1,0:T(8,128)(2,1)S(1)}, u32[]{:S(2)}, u32[]{:S(2)}) collective-permute-start(bf16[4,64,128]{2,1,0:T(8,128)(2,1)S(1)} %collective-permute-done.41), channel_id=1, source_target_pairs={{0,2},{1,3},{2,0},{3,1},{4,6},{5,7},{6,4},{7,5},{8,10},{9,11},{10,... | collective-permute-start | bytes 196616 | tf_op jit(solution)/shard_map/ppermute | solution.py:68
  123.8 3.4 %copy-done.1 = bf16[256,128,128]{2,1,0:T(8,128)(2,1)S(1)} copy-done((bf16[256,128,128]{2,1,0:T(8,128)(2,1)S(1)}, bf16[256,128,128]{2,1,0:T(8,128)(2,1)}, u32[]{:S(2)}) %copy-start.1) | copy-done | bytes 8388632
  127.2 1.8 %shard_map.94 = (f32[32,64,128]{2,1,0:T(8,128)S(1)}, bf16[4,2,64,128]{3,2,1,0:T(8,128)(2,1)S(1)}) custom-call(s32[8,384]{1,0:T(8,128)S(1)} %shard_map.86.plan_in, bf16[256,128,128]{2,1,0:T(8,128)(2,1)S(1)} %copy-done.1, bf16[16,64,128]{2,1,0:T(8,128)(2,1)S(1)} %pad_maximum_fusion.4.field), custom_call_target="tpu_custom_call" | custom-call | flops 268435456 | bytes 8388608 | tf_op jit(solution)/shard_map/pallas_call | solution.py:361
  130.5 4.3 %shard_map.95 = (f32[32,64,128]{2,1,0:T(8,128)S(1)}, bf16[4,2,64,128]{3,2,1,0:T(8,128)(2,1)S(1)}, bf16[33,64,128]{2,1,0:T(8,128)(2,1)S(1)}, bf16[16,64,128]{2,1,...) custom-call(s32[8,384]{1,0:T(8,128)S(1)} %shard_map.86.plan_in, ...), custom_call_target="tpu_custom_call", output_to_operand_aliasing={{0}: (2, {}), {1}: (3, {})} | custom-call | flops 1610612736 | bytes 8388608 | tf_op jit(solution)/shard_map/pallas_call | solution.py:361
  134.9 2.1 %collective-permute-start.50 = (bf16[16,64,128]{2,1,0:T(8,128)(2,1)S(1)}, bf16[16,64,128]{2,1,0:T(8,128)(2,1)S(1)}, u32[]{:S(2)}, u32[]{:S(2)}) collective-permute-start(bf16[16,64,128]{2,1,0:T(8,128)(2,1)S(1)} %get-tuple-element.185), channel_id=1, source_target_pairs={{0,1},{1,0},{2,3},{3,2},{4,5},{5,4},{6,7},{7,6},{8,24},{9,25},{10,... | collective-permute-start | bytes 786440 | tf_op jit(solution)/shard_map/ppermute | solution.py:68
  137.9 1.9 %collective-permute-start.47 = (bf16[4,64,128]{2,1,0:T(8,128)(2,1)S(1)}, bf16[4,64,128]{2,1,0:T(8,128)(2,1)S(1)}, u32[]{:S(2)}, u32[]{:S(2)}) collective-permute-start(bf16[4,64,128]{2,1,0:T(8,128)(2,1)S(1)} %get-tuple-element.180), channel_id=1, source_target_pairs={{0,6},{1,7},{2,4},{3,5},{4,2},{5,3},{6,0},{7,1},{8,14},{9,15},{10,... | collective-permute-start | bytes 196616 | tf_op jit(solution)/shard_map/ppermute | solution.py:68
  139.8 2.5 %collective-permute-start.49 = (bf16[4,64,128]{2,1,0:T(8,128)(2,1)S(1)}, bf16[4,64,128]{2,1,0:T(8,128)(2,1)S(1)}, u32[]{:S(2)}, u32[]{:S(2)}) collective-permute-start(bf16[4,64,128]{2,1,0:T(8,128)(2,1)S(1)} %get-tuple-element.184), channel_id=1, source_target_pairs={{0,2},{1,3},{2,0},{3,1},{4,6},{5,7},{6,4},{7,5},{8,10},{9,11},{10,... | collective-permute-start | bytes 196616 | tf_op jit(solution)/shard_map/ppermute | solution.py:68
  142.3 1.6 %collective-permute-done.47 = bf16[4,64,128]{2,1,0:T(8,128)(2,1)S(1)} collective-permute-done((bf16[4,64,128]{2,1,0:T(8,128)(2,1)S(1)}, bf16[4,64,128]{2,1,0:T(8,128)(2,1)S(1)}, u32[]{:S(2)}, u32[]{:S(2)}) %collective-permute-start.47) | collective-permute-done | bytes 65568 | tf_op jit(solution)/shard_map/ppermute | solution.py:68
  146.7 2.4 %collective-permute-start.53 = (bf16[4,64,128]{2,1,0:T(8,128)(2,1)S(1)}, bf16[4,64,128]{2,1,0:T(8,128)(2,1)S(1)}, u32[]{:S(2)}, u32[]{:S(2)}) collective-permute-start(bf16[4,64,128]{2,1,0:T(8,128)(2,1)S(1)} %get-tuple-element.196), channel_id=1, source_target_pairs={{0,6},{1,7},{2,4},{3,5},{4,2},{5,3},{6,0},{7,1},{8,14},{9,15},{10,... | collective-permute-start | bytes 196616 | tf_op jit(solution)/shard_map/ppermute | solution.py:68
  149.1 2.0 %collective-permute-start.55 = (bf16[4,64,128]{2,1,0:T(8,128)(2,1)S(1)}, bf16[4,64,128]{2,1,0:T(8,128)(2,1)S(1)}, u32[]{:S(2)}, u32[]{:S(2)}) collective-permute-start(bf16[4,64,128]{2,1,0:T(8,128)(2,1)S(1)} %get-tuple-element.198), channel_id=1, source_target_pairs={{0,2},{1,3},{2,0},{3,1},{4,6},{5,7},{6,4},{7,5},{8,10},{9,11},{10,... | collective-permute-start | bytes 196616 | tf_op jit(solution)/shard_map/ppermute | solution.py:68
  151.1 1.6 %collective-permute-done.53 = bf16[4,64,128]{2,1,0:T(8,128)(2,1)S(1)} collective-permute-done((bf16[4,64,128]{2,1,0:T(8,128)(2,1)S(1)}, bf16[4,64,128]{2,1,0:T(8,128)(2,1)S(1)}, u32[]{:S(2)}, u32[]{:S(2)}) %collective-permute-start.53) | collective-permute-done | bytes 65568 | tf_op jit(solution)/shard_map/ppermute | solution.py:68
  152.7 1.8 %collective-permute-done.54 = bf16[4,64,128]{2,1,0:T(8,128)(2,1)S(1)} collective-permute-done((bf16[4,64,128]{2,1,0:T(8,128)(2,1)S(1)}, bf16[4,64,128]{2,1,0:T(8,128)(2,1)S(1)}, u32[]{:S(2)}, u32[]{:S(2)}) %collective-permute-start.54) | collective-permute-done | bytes 65568 | tf_op jit(solution)/shard_map/ppermute | solution.py:68
  (144 shorter events, 41.3 us)
Async XLA Ops:
  0.6 29.7 %collective-permute-start.5 = (bf16[128,128,128]{2,1,0:T(8,128)(2,1)}, bf16[128,128,128]{2,1,0:T(8,128)(2,1)}, u32[]{:S(2)}, u32[]{:S(2)}) collective-permute-start(bf16[128,128,128]{2,1,0:T(8,128)(2,1)} %first.1), channel_id=1, source_target_pairs={{0,8},{1,9},{2,10},{3,11},{4,12},{5,13},{6,14},{7,15},{8,0},{9,1},... | collective-permute-start | bytes 12582920 | tf_op jit(solution)/shard_map/ppermute | solution.py:68
  8.1 10.5 %collective-permute-start.1 = (bf16[4,80,128]{2,1,0:T(8,128)(2,1)S(1)}, bf16[4,80,128]{2,1,0:T(8,128)(2,1)S(1)}, u32[]{:S(2)}, u32[]{:S(2)}) collective-permute-start(bf16[4,80,128]{2,1,0:T(8,128)(2,1)S(1)} %pad_maximum_fusion.7), channel_id=1, source_target_pairs={{0,6},{1,7},{2,4},{3,5},{4,2},{5,3},{6,0},{7,1},{8,14},{9,15},{10,... | collective-permute-start | bytes 245768 | tf_op jit(solution)/shard_map/ppermute | solution.py:68
  13.2 7.2 %collective-permute-start.2 = (bf16[4,80,128]{2,1,0:T(8,128)(2,1)S(1)}, bf16[4,80,128]{2,1,0:T(8,128)(2,1)S(1)}, u32[]{:S(2)}, u32[]{:S(2)}) collective-permute-start(bf16[4,80,128]{2,1,0:T(8,128)(2,1)S(1)} %pad_maximum_fusion.7), channel_id=1, source_target_pairs={{0,4},{1,5},{2,6},{3,7},{4,0},{5,1},{6,2},{7,3},{8,12},{9,13},{10,... | collective-permute-start | bytes 245768 | tf_op jit(solution)/shard_map/ppermute | solution.py:68
  13.2 7.2 %collective-permute-start.3 = (bf16[4,80,128]{2,1,0:T(8,128)(2,1)S(1)}, bf16[4,80,128]{2,1,0:T(8,128)(2,1)S(1)}, u32[]{:S(2)}, u32[]{:S(2)}) collective-permute-start(bf16[4,80,128]{2,1,0:T(8,128)(2,1)S(1)} %pad_maximum_fusion.7), channel_id=1, source_target_pairs={{0,2},{1,3},{2,0},{3,1},{4,6},{5,7},{6,4},{7,5},{8,10},{9,11},{10,... | collective-permute-start | bytes 245768 | tf_op jit(solution)/shard_map/ppermute | solution.py:68
  13.8 6.6 %collective-permute-start.4 = (bf16[4,80,128]{2,1,0:T(8,128)(2,1)S(1)}, bf16[4,80,128]{2,1,0:T(8,128)(2,1)S(1)}, u32[]{:S(2)}, u32[]{:S(2)}) collective-permute-start(bf16[4,80,128]{2,1,0:T(8,128)(2,1)S(1)} %pad_maximum_fusion.7), channel_id=1, source_target_pairs={{0,17},{1,16},{2,19},{3,18},{4,21},{5,20},{6,23},{7,22},{8,25},{9,... | collective-permute-start | bytes 245768 | tf_op jit(solution)/shard_map/ppermute | solution.py:68
  20.4 6.5 %collective-permute-start.6 = (bf16[4,80,128]{2,1,0:T(8,128)(2,1)S(1)}, bf16[4,80,128]{2,1,0:T(8,128)(2,1)S(1)}, u32[]{:S(2)}, u32[]{:S(2)}) collective-permute-start(bf16[4,80,128]{2,1,0:T(8,128)(2,1)S(1)} %collective-permute-done.4), channel_id=1, source_target_pairs={{0,6},{1,7},{2,4},{3,5},{4,2},{5,3},{6,0},{7,1},{8,14},{9,15},{10,... | collective-permute-start | bytes 245768 | tf_op jit(solution)/shard_map/ppermute | solution.py:68
  22.9 7.4 %collective-permute-start.7 = (bf16[4,80,128]{2,1,0:T(8,128)(2,1)S(1)}, bf16[4,80,128]{2,1,0:T(8,128)(2,1)S(1)}, u32[]{:S(2)}, u32[]{:S(2)}) collective-permute-start(bf16[4,80,128]{2,1,0:T(8,128)(2,1)S(1)} %collective-permute-done.4), channel_id=1, source_target_pairs={{0,4},{1,5},{2,6},{3,7},{4,0},{5,1},{6,2},{7,3},{8,12},{9,13},{10,... | collective-permute-start | bytes 245768 | tf_op jit(solution)/shard_map/ppermute | solution.py:68
  22.9 7.4 %collective-permute-start.8 = (bf16[4,80,128]{2,1,0:T(8,128)(2,1)S(1)}, bf16[4,80,128]{2,1,0:T(8,128)(2,1)S(1)}, u32[]{:S(2)}, u32[]{:S(2)}) collective-permute-start(bf16[4,80,128]{2,1,0:T(8,128)(2,1)S(1)} %collective-permute-done.4), channel_id=1, source_target_pairs={{0,2},{1,3},{2,0},{3,1},{4,6},{5,7},{6,4},{7,5},{8,10},{9,11},{10,... | collective-permute-start | bytes 245768 | tf_op jit(solution)/shard_map/ppermute | solution.py:68
  24.8 12.0 %collective-permute-start.10 = (bf16[16,80,128]{2,1,0:T(8,128)(2,1)S(1)}, bf16[16,80,128]{2,1,0:T(8,128)(2,1)S(1)}, u32[]{:S(2)}, u32[]{:S(2)}) collective-permute-start(bf16[16,80,128]{2,1,0:T(8,128)(2,1)S(1)} %pad_maximum_fusion.field), channel_id=1, source_target_pairs={{0,16},{1,17},{2,18},{3,19},{4,20},{5,21},{6,22},{7,23},{8,9},{9,8... | collective-permute-start | bytes 983048 | tf_op jit(solution)/shard_map/ppermute | solution.py:68
  26.9 9.9 %collective-permute-start.9 = (bf16[16,80,128]{2,1,0:T(8,128)(2,1)S(1)}, bf16[16,80,128]{2,1,0:T(8,128)(2,1)S(1)}, u32[]{:S(2)}, u32[]{:S(2)}) collective-permute-start(bf16[16,80,128]{2,1,0:T(8,128)(2,1)S(1)} %pad_maximum_fusion.field), channel_id=1, source_target_pairs={{0,1},{1,0},{2,3},{3,2},{4,5},{5,4},{6,7},{7,6},{8,24},{9,25},{10,... | collective-permute-start | bytes 983048 | tf_op jit(solution)/shard_map/ppermute | solution.py:68
  40.9 8.4 %collective-permute-start.11 = (bf16[4,64,128]{2,1,0:T(8,128)(2,1)S(1)}, bf16[4,64,128]{2,1,0:T(8,128)(2,1)S(1)}, u32[]{:S(2)}, u32[]{:S(2)}) collective-permute-start(bf16[4,64,128]{2,1,0:T(8,128)(2,1)S(1)} %get-tuple-element.114), channel_id=1, source_target_pairs={{0,6},{1,7},{2,4},{3,5},{4,2},{5,3},{6,0},{7,1},{8,14},{9,15},{10,... | collective-permute-start | bytes 196616 | tf_op jit(solution)/shard_map/ppermute | solution.py:68
  43.6 8.5 %collective-permute-start.14 = (bf16[16,64,128]{2,1,0:T(8,128)(2,1)S(1)}, bf16[16,64,128]{2,1,0:T(8,128)(2,1)S(1)}, u32[]{:S(2)}, u32[]{:S(2)}) collective-permute-start(bf16[16,64,128]{2,1,0:T(8,128)(2,1)S(1)} %get-tuple-element.119), channel_id=1, source_target_pairs={{0,1},{1,0},{2,3},{3,2},{4,5},{5,4},{6,7},{7,6},{8,24},{9,25},{10,... | collective-permute-start | bytes 786440 | tf_op jit(solution)/shard_map/ppermute | solution.py:68
  45.1 7.0 %collective-permute-start.15 = (bf16[16,64,128]{2,1,0:T(8,128)(2,1)S(1)}, bf16[16,64,128]{2,1,0:T(8,128)(2,1)S(1)}, u32[]{:S(2)}, u32[]{:S(2)}) collective-permute-start(bf16[16,64,128]{2,1,0:T(8,128)(2,1)S(1)} %get-tuple-element.120), channel_id=1, source_target_pairs={{0,16},{1,17},{2,18},{3,19},{4,20},{5,21},{6,22},{7,23},{8,9},{9,8... | collective-permute-start | bytes 786440 | tf_op jit(solution)/shard_map/ppermute | solution.py:68
  46.1 5.7 %collective-permute-start.12 = (bf16[4,64,128]{2,1,0:T(8,128)(2,1)S(1)}, bf16[4,64,128]{2,1,0:T(8,128)(2,1)S(1)}, u32[]{:S(2)}, u32[]{:S(2)}) collective-permute-start(bf16[4,64,128]{2,1,0:T(8,128)(2,1)S(1)} %get-tuple-element.117), channel_id=1, source_target_pairs={{0,4},{1,5},{2,6},{3,7},{4,0},{5,1},{6,2},{7,3},{8,12},{9,13},{10,... | collective-permute-start | bytes 196616 | tf_op jit(solution)/shard_map/ppermute | solution.py:68
  46.4 5.6 %collective-permute-start.13 = (bf16[4,64,128]{2,1,0:T(8,128)(2,1)S(1)}, bf16[4,64,128]{2,1,0:T(8,128)(2,1)S(1)}, u32[]{:S(2)}, u32[]{:S(2)}) collective-permute-start(bf16[4,64,128]{2,1,0:T(8,128)(2,1)S(1)} %get-tuple-element.118), channel_id=1, source_target_pairs={{0,2},{1,3},{2,0},{3,1},{4,6},{5,7},{6,4},{7,5},{8,10},{9,11},{10,... | collective-permute-start | bytes 196616 | tf_op jit(solution)/shard_map/ppermute | solution.py:68
  52.2 6.6 %collective-permute-start.16 = (bf16[4,64,128]{2,1,0:T(8,128)(2,1)S(1)}, bf16[4,64,128]{2,1,0:T(8,128)(2,1)S(1)}, u32[]{:S(2)}, u32[]{:S(2)}) collective-permute-start(bf16[4,64,128]{2,1,0:T(8,128)(2,1)S(1)} %add_convert_fusion.2), channel_id=1, source_target_pairs={{0,17},{1,16},{2,19},{3,18},{4,21},{5,20},{6,23},{7,22},{8,25},{9,... | collective-permute-start | bytes 196616 | tf_op jit(solution)/shard_map/ppermute | solution.py:68
  54.4 6.8 %collective-permute-start.17 = (bf16[4,64,128]{2,1,0:T(8,128)(2,1)S(1)}, bf16[4,64,128]{2,1,0:T(8,128)(2,1)S(1)}, u32[]{:S(2)}, u32[]{:S(2)}) collective-permute-start(bf16[4,64,128]{2,1,0:T(8,128)(2,1)S(1)} %get-tuple-element.130), channel_id=1, source_target_pairs={{0,6},{1,7},{2,4},{3,5},{4,2},{5,3},{6,0},{7,1},{8,14},{9,15},{10,... | collective-permute-start | bytes 196616 | tf_op jit(solution)/shard_map/ppermute | solution.py:68
  55.8 6.4 %collective-permute-start.18 = (bf16[4,64,128]{2,1,0:T(8,128)(2,1)S(1)}, bf16[4,64,128]{2,1,0:T(8,128)(2,1)S(1)}, u32[]{:S(2)}, u32[]{:S(2)}) collective-permute-start(bf16[4,64,128]{2,1,0:T(8,128)(2,1)S(1)} %get-tuple-element.131), channel_id=1, source_target_pairs={{0,4},{1,5},{2,6},{3,7},{4,0},{5,1},{6,2},{7,3},{8,12},{9,13},{10,... | collective-permute-start | bytes 196616 | tf_op jit(solution)/shard_map/ppermute | solution.py:68
  55.8 6.4 %collective-permute-start.19 = (bf16[4,64,128]{2,1,0:T(8,128)(2,1)S(1)}, bf16[4,64,128]{2,1,0:T(8,128)(2,1)S(1)}, u32[]{:S(2)}, u32[]{:S(2)}) collective-permute-start(bf16[4,64,128]{2,1,0:T(8,128)(2,1)S(1)} %get-tuple-element.132), channel_id=1, source_target_pairs={{0,2},{1,3},{2,0},{3,1},{4,6},{5,7},{6,4},{7,5},{8,10},{9,11},{10,... | collective-permute-start | bytes 196616 | tf_op jit(solution)/shard_map/ppermute | solution.py:68
  62.3 6.4 %collective-permute-start.20 = (bf16[4,64,128]{2,1,0:T(8,128)(2,1)S(1)}, bf16[4,64,128]{2,1,0:T(8,128)(2,1)S(1)}, u32[]{:S(2)}, u32[]{:S(2)}) collective-permute-start(bf16[4,64,128]{2,1,0:T(8,128)(2,1)S(1)} %get-tuple-element.207), channel_id=1, source_target_pairs={{0,6},{1,7},{2,4},{3,5},{4,2},{5,3},{6,0},{7,1},{8,14},{9,15},{10,... | collective-permute-start | bytes 196616 | tf_op jit(solution)/shard_map/ppermute | solution.py:68
  63.9 6.2 %collective-permute-start.21 = (bf16[4,64,128]{2,1,0:T(8,128)(2,1)S(1)}, bf16[4,64,128]{2,1,0:T(8,128)(2,1)S(1)}, u32[]{:S(2)}, u32[]{:S(2)}) collective-permute-start(bf16[4,64,128]{2,1,0:T(8,128)(2,1)S(1)} %get-tuple-element.207), channel_id=1, source_target_pairs={{0,4},{1,5},{2,6},{3,7},{4,0},{5,1},{6,2},{7,3},{8,12},{9,13},{10,... | collective-permute-start | bytes 196616 | tf_op jit(solution)/shard_map/ppermute | solution.py:68
  71.9 9.6 %collective-permute-start.27 = (bf16[16,64,128]{2,1,0:T(8,128)(2,1)S(1)}, bf16[16,64,128]{2,1,0:T(8,128)(2,1)S(1)}, u32[]{:S(2)}, u32[]{:S(2)}) collective-permute-start(bf16[16,64,128]{2,1,0:T(8,128)(2,1)S(1)} %pad_maximum_fusion.2.field), channel_id=1, source_target_pairs={{0,1},{1,0},{2,3},{3,2},{4,5},{5,4},{6,7},{7,6},{8,24},{9,25},{10,... | collective-permute-start | bytes 786440 | tf_op jit(solution)/shard_map/ppermute | solution.py:68
  73.3 8.2 %collective-permute-start.28 = (bf16[16,64,128]{2,1,0:T(8,128)(2,1)S(1)}, bf16[16,64,128]{2,1,0:T(8,128)(2,1)S(1)}, u32[]{:S(2)}, u32[]{:S(2)}) collective-permute-start(bf16[16,64,128]{2,1,0:T(8,128)(2,1)S(1)} %pad_maximum_fusion.2.field), channel_id=1, source_target_pairs={{0,16},{1,17},{2,18},{3,19},{4,20},{5,21},{6,22},{7,23},{8,9},{9,8... | collective-permute-start | bytes 786440 | tf_op jit(solution)/shard_map/ppermute | solution.py:68
  74.0 6.2 %collective-permute-start.24 = (bf16[4,64,128]{2,1,0:T(8,128)(2,1)S(1)}, bf16[4,64,128]{2,1,0:T(8,128)(2,1)S(1)}, u32[]{:S(2)}, u32[]{:S(2)}) collective-permute-start(bf16[4,64,128]{2,1,0:T(8,128)(2,1)S(1)} %collective-permute-done.23), channel_id=1, source_target_pairs={{0,6},{1,7},{2,4},{3,5},{4,2},{5,3},{6,0},{7,1},{8,14},{9,15},{10,... | collective-permute-start | bytes 196616 | tf_op jit(solution)/shard_map/ppermute | solution.py:68
  85.7 10.6 %collective-permute-start.32 = (bf16[16,64,128]{2,1,0:T(8,128)(2,1)S(1)}, bf16[16,64,128]{2,1,0:T(8,128)(2,1)S(1)}, u32[]{:S(2)}, u32[]{:S(2)}) collective-permute-start(bf16[16,64,128]{2,1,0:T(8,128)(2,1)S(1)} %get-tuple-element.152), channel_id=1, source_target_pairs={{0,1},{1,0},{2,3},{3,2},{4,5},{5,4},{6,7},{7,6},{8,24},{9,25},{10,... | collective-permute-start | bytes 786440 | tf_op jit(solution)/shard_map/ppermute | solution.py:68
  87.9 8.4 %collective-permute-start.33 = (bf16[16,64,128]{2,1,0:T(8,128)(2,1)S(1)}, bf16[16,64,128]{2,1,0:T(8,128)(2,1)S(1)}, u32[]{:S(2)}, u32[]{:S(2)}) collective-permute-start(bf16[16,64,128]{2,1,0:T(8,128)(2,1)S(1)} %get-tuple-element.153), channel_id=1, source_target_pairs={{0,16},{1,17},{2,18},{3,19},{4,20},{5,21},{6,22},{7,23},{8,9},{9,8... | collective-permute-start | bytes 786440 | tf_op jit(solution)/shard_map/ppermute | solution.py:68
  88.5 6.2 %collective-permute-start.29 = (bf16[4,64,128]{2,1,0:T(8,128)(2,1)S(1)}, bf16[4,64,128]{2,1,0:T(8,128)(2,1)S(1)}, u32[]{:S(2)}, u32[]{:S(2)}) collective-permute-start(bf16[4,64,128]{2,1,0:T(8,128)(2,1)S(1)} %get-tuple-element.147), channel_id=1, source_target_pairs={{0,6},{1,7},{2,4},{3,5},{4,2},{5,3},{6,0},{7,1},{8,14},{9,15},{10,... | collective-permute-start | bytes 196616 | tf_op jit(solution)/shard_map/ppermute | solution.py:68
  89.7 6.6 %collective-permute-start.30 = (bf16[4,64,128]{2,1,0:T(8,128)(2,1)S(1)}, bf16[4,64,128]{2,1,0:T(8,128)(2,1)S(1)}, u32[]{:S(2)}, u32[]{:S(2)}) collective-permute-start(bf16[4,64,128]{2,1,0:T(8,128)(2,1)S(1)} %get-tuple-element.150), channel_id=1, source_target_pairs={{0,4},{1,5},{2,6},{3,7},{4,0},{5,1},{6,2},{7,3},{8,12},{9,13},{10,... | collective-permute-start | bytes 196616 | tf_op jit(solution)/shard_map/ppermute | solution.py:68
  96.5 6.0 %collective-permute-start.34 = (bf16[4,64,128]{2,1,0:T(8,128)(2,1)S(1)}, bf16[4,64,128]{2,1,0:T(8,128)(2,1)S(1)}, u32[]{:S(2)}, u32[]{:S(2)}) collective-permute-start(bf16[4,64,128]{2,1,0:T(8,128)(2,1)S(1)} %add_convert_fusion.1), channel_id=1, source_target_pairs={{0,17},{1,16},{2,19},{3,18},{4,21},{5,20},{6,23},{7,22},{8,25},{9,... | collective-permute-start | bytes 196616 | tf_op jit(solution)/shard_map/ppermute | solution.py:68
  98.0 6.5 %collective-permute-start.35 = (bf16[4,64,128]{2,1,0:T(8,128)(2,1)S(1)}, bf16[4,64,128]{2,1,0:T(8,128)(2,1)S(1)}, u32[]{:S(2)}, u32[]{:S(2)}) collective-permute-start(bf16[4,64,128]{2,1,0:T(8,128)(2,1)S(1)} %get-tuple-element.163), channel_id=1, source_target_pairs={{0,6},{1,7},{2,4},{3,5},{4,2},{5,3},{6,0},{7,1},{8,14},{9,15},{10,... | collective-permute-start | bytes 196616 | tf_op jit(solution)/shard_map/ppermute | solution.py:68
  100.1 7.4 %collective-permute-start.36 = (bf16[4,64,128]{2,1,0:T(8,128)(2,1)S(1)}, bf16[4,64,128]{2,1,0:T(8,128)(2,1)S(1)}, u32[]{:S(2)}, u32[]{:S(2)}) collective-permute-start(bf16[4,64,128]{2,1,0:T(8,128)(2,1)S(1)} %get-tuple-element.164), channel_id=1, source_target_pairs={{0,4},{1,5},{2,6},{3,7},{4,0},{5,1},{6,2},{7,3},{8,12},{9,13},{10,... | collective-permute-start | bytes 196616 | tf_op jit(solution)/shard_map/ppermute | solution.py:68
  100.1 7.4 %collective-permute-start.37 = (bf16[4,64,128]{2,1,0:T(8,128)(2,1)S(1)}, bf16[4,64,128]{2,1,0:T(8,128)(2,1)S(1)}, u32[]{:S(2)}, u32[]{:S(2)}) collective-permute-start(bf16[4,64,128]{2,1,0:T(8,128)(2,1)S(1)} %get-tuple-element.165), channel_id=1, source_target_pairs={{0,2},{1,3},{2,0},{3,1},{4,6},{5,7},{6,4},{7,5},{8,10},{9,11},{10,... | collective-permute-start | bytes 196616 | tf_op jit(solution)/shard_map/ppermute | solution.py:68
  107.7 6.4 %collective-permute-start.38 = (bf16[4,64,128]{2,1,0:T(8,128)(2,1)S(1)}, bf16[4,64,128]{2,1,0:T(8,128)(2,1)S(1)}, u32[]{:S(2)}, u32[]{:S(2)}) collective-permute-start(bf16[4,64,128]{2,1,0:T(8,128)(2,1)S(1)} %get-tuple-element.202), channel_id=1, source_target_pairs={{0,6},{1,7},{2,4},{3,5},{4,2},{5,3},{6,0},{7,1},{8,14},{9,15},{10,... | collective-permute-start | bytes 196616 | tf_op jit(solution)/shard_map/ppermute | solution.py:68
  110.1 7.2 %collective-permute-start.39 = (bf16[4,64,128]{2,1,0:T(8,128)(2,1)S(1)}, bf16[4,64,128]{2,1,0:T(8,128)(2,1)S(1)}, u32[]{:S(2)}, u32[]{:S(2)}) collective-permute-start(bf16[4,64,128]{2,1,0:T(8,128)(2,1)S(1)} %get-tuple-element.202), channel_id=1, source_target_pairs={{0,4},{1,5},{2,6},{3,7},{4,0},{5,1},{6,2},{7,3},{8,12},{9,13},{10,... | collective-permute-start | bytes 196616 | tf_op jit(solution)/shard_map/ppermute | solution.py:68
  110.1 7.2 %collective-permute-start.40 = (bf16[4,64,128]{2,1,0:T(8,128)(2,1)S(1)}, bf16[4,64,128]{2,1,0:T(8,128)(2,1)S(1)}, u32[]{:S(2)}, u32[]{:S(2)}) collective-permute-start(bf16[4,64,128]{2,1,0:T(8,128)(2,1)S(1)} %get-tuple-element.202), channel_id=1, source_target_pairs={{0,2},{1,3},{2,0},{3,1},{4,6},{5,7},{6,4},{7,5},{8,10},{9,11},{10,... | collective-permute-start | bytes 196616 | tf_op jit(solution)/shard_map/ppermute | solution.py:68
  117.4 11.7 %collective-permute-start.45 = (bf16[16,64,128]{2,1,0:T(8,128)(2,1)S(1)}, bf16[16,64,128]{2,1,0:T(8,128)(2,1)S(1)}, u32[]{:S(2)}, u32[]{:S(2)}) collective-permute-start(bf16[16,64,128]{2,1,0:T(8,128)(2,1)S(1)} %pad_maximum_fusion.4.field), channel_id=1, source_target_pairs={{0,1},{1,0},{2,3},{3,2},{4,5},{5,4},{6,7},{7,6},{8,24},{9,25},{10,... | collective-permute-start | bytes 786440 | tf_op jit(solution)/shard_map/ppermute | solution.py:68
  118.7 10.4 %collective-permute-start.46 = (bf16[16,64,128]{2,1,0:T(8,128)(2,1)S(1)}, bf16[16,64,128]{2,1,0:T(8,128)(2,1)S(1)}, u32[]{:S(2)}, u32[]{:S(2)}) collective-permute-start(bf16[16,64,128]{2,1,0:T(8,128)(2,1)S(1)} %pad_maximum_fusion.4.field), channel_id=1, source_target_pairs={{0,16},{1,17},{2,18},{3,19},{4,20},{5,21},{6,22},{7,23},{8,9},{9,8... | collective-permute-start | bytes 786440 | tf_op jit(solution)/shard_map/ppermute | solution.py:68
  119.4 9.6 %collective-permute-start.42 = (bf16[4,64,128]{2,1,0:T(8,128)(2,1)S(1)}, bf16[4,64,128]{2,1,0:T(8,128)(2,1)S(1)}, u32[]{:S(2)}, u32[]{:S(2)}) collective-permute-start(bf16[4,64,128]{2,1,0:T(8,128)(2,1)S(1)} %collective-permute-done.41), channel_id=1, source_target_pairs={{0,6},{1,7},{2,4},{3,5},{4,2},{5,3},{6,0},{7,1},{8,14},{9,15},{10,... | collective-permute-start | bytes 196616 | tf_op jit(solution)/shard_map/ppermute | solution.py:68
  121.3 7.6 %collective-permute-start.43 = (bf16[4,64,128]{2,1,0:T(8,128)(2,1)S(1)}, bf16[4,64,128]{2,1,0:T(8,128)(2,1)S(1)}, u32[]{:S(2)}, u32[]{:S(2)}) collective-permute-start(bf16[4,64,128]{2,1,0:T(8,128)(2,1)S(1)} %collective-permute-done.41), channel_id=1, source_target_pairs={{0,4},{1,5},{2,6},{3,7},{4,0},{5,1},{6,2},{7,3},{8,12},{9,13},{10,... | collective-permute-start | bytes 196616 | tf_op jit(solution)/shard_map/ppermute | solution.py:68
  121.3 7.6 %collective-permute-start.44 = (bf16[4,64,128]{2,1,0:T(8,128)(2,1)S(1)}, bf16[4,64,128]{2,1,0:T(8,128)(2,1)S(1)}, u32[]{:S(2)}, u32[]{:S(2)}) collective-permute-start(bf16[4,64,128]{2,1,0:T(8,128)(2,1)S(1)} %collective-permute-done.41), channel_id=1, source_target_pairs={{0,2},{1,3},{2,0},{3,1},{4,6},{5,7},{6,4},{7,5},{8,10},{9,11},{10,... | collective-permute-start | bytes 196616 | tf_op jit(solution)/shard_map/ppermute | solution.py:68
  134.9 10.6 %collective-permute-start.50 = (bf16[16,64,128]{2,1,0:T(8,128)(2,1)S(1)}, bf16[16,64,128]{2,1,0:T(8,128)(2,1)S(1)}, u32[]{:S(2)}, u32[]{:S(2)}) collective-permute-start(bf16[16,64,128]{2,1,0:T(8,128)(2,1)S(1)} %get-tuple-element.185), channel_id=1, source_target_pairs={{0,1},{1,0},{2,3},{3,2},{4,5},{5,4},{6,7},{7,6},{8,24},{9,25},{10,... | collective-permute-start | bytes 786440 | tf_op jit(solution)/shard_map/ppermute | solution.py:68
  137.0 8.5 %collective-permute-start.51 = (bf16[16,64,128]{2,1,0:T(8,128)(2,1)S(1)}, bf16[16,64,128]{2,1,0:T(8,128)(2,1)S(1)}, u32[]{:S(2)}, u32[]{:S(2)}) collective-permute-start(bf16[16,64,128]{2,1,0:T(8,128)(2,1)S(1)} %get-tuple-element.186), channel_id=1, source_target_pairs={{0,16},{1,17},{2,18},{3,19},{4,20},{5,21},{6,22},{7,23},{8,9},{9,8... | collective-permute-start | bytes 786440 | tf_op jit(solution)/shard_map/ppermute | solution.py:68
  137.9 6.1 %collective-permute-start.47 = (bf16[4,64,128]{2,1,0:T(8,128)(2,1)S(1)}, bf16[4,64,128]{2,1,0:T(8,128)(2,1)S(1)}, u32[]{:S(2)}, u32[]{:S(2)}) collective-permute-start(bf16[4,64,128]{2,1,0:T(8,128)(2,1)S(1)} %get-tuple-element.180), channel_id=1, source_target_pairs={{0,6},{1,7},{2,4},{3,5},{4,2},{5,3},{6,0},{7,1},{8,14},{9,15},{10,... | collective-permute-start | bytes 196616 | tf_op jit(solution)/shard_map/ppermute | solution.py:68
  139.8 5.6 %collective-permute-start.48 = (bf16[4,64,128]{2,1,0:T(8,128)(2,1)S(1)}, bf16[4,64,128]{2,1,0:T(8,128)(2,1)S(1)}, u32[]{:S(2)}, u32[]{:S(2)}) collective-permute-start(bf16[4,64,128]{2,1,0:T(8,128)(2,1)S(1)} %get-tuple-element.183), channel_id=1, source_target_pairs={{0,4},{1,5},{2,6},{3,7},{4,0},{5,1},{6,2},{7,3},{8,12},{9,13},{10,... | collective-permute-start | bytes 196616 | tf_op jit(solution)/shard_map/ppermute | solution.py:68
  139.8 5.6 %collective-permute-start.49 = (bf16[4,64,128]{2,1,0:T(8,128)(2,1)S(1)}, bf16[4,64,128]{2,1,0:T(8,128)(2,1)S(1)}, u32[]{:S(2)}, u32[]{:S(2)}) collective-permute-start(bf16[4,64,128]{2,1,0:T(8,128)(2,1)S(1)} %get-tuple-element.184), channel_id=1, source_target_pairs={{0,2},{1,3},{2,0},{3,1},{4,6},{5,7},{6,4},{7,5},{8,10},{9,11},{10,... | collective-permute-start | bytes 196616 | tf_op jit(solution)/shard_map/ppermute | solution.py:68
  146.7 6.1 %collective-permute-start.53 = (bf16[4,64,128]{2,1,0:T(8,128)(2,1)S(1)}, bf16[4,64,128]{2,1,0:T(8,128)(2,1)S(1)}, u32[]{:S(2)}, u32[]{:S(2)}) collective-permute-start(bf16[4,64,128]{2,1,0:T(8,128)(2,1)S(1)} %get-tuple-element.196), channel_id=1, source_target_pairs={{0,6},{1,7},{2,4},{3,5},{4,2},{5,3},{6,0},{7,1},{8,14},{9,15},{10,... | collective-permute-start | bytes 196616 | tf_op jit(solution)/shard_map/ppermute | solution.py:68
  149.1 5.5 %collective-permute-start.54 = (bf16[4,64,128]{2,1,0:T(8,128)(2,1)S(1)}, bf16[4,64,128]{2,1,0:T(8,128)(2,1)S(1)}, u32[]{:S(2)}, u32[]{:S(2)}) collective-permute-start(bf16[4,64,128]{2,1,0:T(8,128)(2,1)S(1)} %get-tuple-element.197), channel_id=1, source_target_pairs={{0,4},{1,5},{2,6},{3,7},{4,0},{5,1},{6,2},{7,3},{8,12},{9,13},{10,... | collective-permute-start | bytes 196616 | tf_op jit(solution)/shard_map/ppermute | solution.py:68
  149.1 5.5 %collective-permute-start.55 = (bf16[4,64,128]{2,1,0:T(8,128)(2,1)S(1)}, bf16[4,64,128]{2,1,0:T(8,128)(2,1)S(1)}, u32[]{:S(2)}, u32[]{:S(2)}) collective-permute-start(bf16[4,64,128]{2,1,0:T(8,128)(2,1)S(1)} %get-tuple-element.198), channel_id=1, source_target_pairs={{0,2},{1,3},{2,0},{3,1},{4,6},{5,7},{6,4},{7,5},{8,10},{9,11},{10,... | collective-permute-start | bytes 196616 | tf_op jit(solution)/shard_map/ppermute | solution.py:68
  (13 other events, 111.3 us)

commit v2 on v1

--- a/solution.py
+++ b/solution.py
@@ -74,25 +74,27 @@
         return self.send(block, "core", 1)
 
 
-def along_z(grid, block):
+def along_z(grid, block, beside=None):
     depth = grid.sizes["z"]
     moved = [grid.send(block, "z", r) for r in range(1, depth)]
-    return jnp.concatenate([block] + moved[::-1])
+    if beside is not None:
+        moved[-1], beside = lax.optimization_barrier((moved[-1], beside))
+    return jnp.concatenate([block] + moved[::-1]), beside
 
 
 def gather_field(grid, low, plan, load):
     wide = grid.sizes["y"]
-    base = along_z(grid, low)
     if wide == 2:
-        corner = grid.send(low, BOTH_AXES, 1)
+        base, corner = along_z(grid, low, grid.send(low, BOTH_AXES, 1))
         base, corner, plan = lax.optimization_barrier((base, corner, plan))
         tiles = load()
         sums = base_product(plan, tiles, base)
         over = [grid.send(base, axes, 1) for axes in (ONE, TWO)]
-        far = along_z(grid, corner)
+        far, _ = along_z(grid, corner)
         far, *sums = lax.optimization_barrier((far, *sums))
         pieces = [*over, far]
     else:
+        base, _ = along_z(grid, low)
         base, plan = lax.optimization_barrier((base, plan))
         tiles = load()
         sums = base_product(plan, tiles, base)
@@ -115,7 +117,7 @@
     def widen(v):
         return v.astype(jnp.float32)
 
-    diagonal = 0.0
+    diagonal = jnp.zeros((), jnp.float32)
     if wide == 2:
         one, two, here, *parts = rest
         one, two, *parts = lax.optimization_barrier((one, two, *parts))
@@ -137,10 +139,13 @@
     parts = [narrow(base[depth - r]) for r in order]
     if corner is not None:
         *parts, corner = lax.optimization_barrier((*parts, corner))
-        diagonal = widen(grid.send(corner, BOTH_AXES, 1))
-    gram = base[0] + diagonal
-    for r, part in zip(order, parts):
-        gram = gram + widen(grid.send(part, "z", r))
+        diagonal = grid.send(corner, BOTH_AXES, 1)
+    parts = [grid.send(part, "z", r) for r, part in zip(order, parts)]
+    if corner is not None:
+        parts[0], diagonal = lax.optimization_barrier((parts[0], diagonal))
+    gram = base[0] + widen(diagonal)
+    for part in parts:
+        gram = gram + widen(part)
     return gram
 
 

time: 158 us -> 157 us (level)
  starting transfers between devices: 82.1 us -> 74.8 us
  waiting for transfers between devices: 34.5 us -> 39.3 us
  Pallas kernels: 26 us -> 28.3 us
    ppermute x57, starting transfers between devices: 82.1 us -> 74.8 us  [send(): return lax.ppermute(block, BOTH, route)]
    ppermute x57, waiting for transfers between devices: 34.5 us -> 39.3 us  [send(): return lax.ppermute(block, BOTH, route)]
    pallas_call x9, Pallas kernels: 22.1 us -> 24.5 us  [call(): pl.pallas_call(kernel, out_shape=outs, in_specs=[place[kind] for kind in...]
  transfers between devices with their start and end apart: 57 -> 57, of which waited for: 22 -> 29; matrix products, arithmetic and copies ran while one was open for 3% -> 3% of each run, Pallas kernels for 9% -> 9%
where the time goes in v2:
time: 157 us
  starting transfers between devices  74.8 us (48%)
  waiting for transfers between devices  39.3 us (25%)
  Pallas kernels  28.3 us (18%)
  local copies, waits for them, and re-layouts  9.51 us (6%)
  other arithmetic  3.56 us (2%)
  between operations  1.59 us (1%)
    ppermute x57, starting transfers between devices, send(): return lax.ppermute(block, BOTH, route)  74.8 us
    ppermute x57, waiting for transfers between devices, send(): return lax.ppermute(block, BOTH, route)  39.3 us
    pallas_call x9, Pallas kernels, call(): pl.pallas_call(kernel, out_shape=outs, in_specs=[place[kind] for kind in...  24.5 us
    unnamed x10, local copies, waits for them, and re-layouts  7.23 us
  transfers between devices with their start and end apart: 57, of which 29 were waited for; matrix products, arithmetic and copies ran while one was open for 3% of the time, Pallas kernels for 9%

profile of v2, /device:TPU:0, one launch (start us, length us, event | category | flops | bytes accessed | tf_op | source)
XLA Modules:
  0.0 157.2 jit_solution(15098314119948836998)
XLA Ops:
  4.4 3.6 %collective-permute-done = f32[2,72,128]{2,1,0:T(8,128)S(1)} collective-permute-done((f32[2,72,128]{2,1,0:T(8,128)S(1)}, f32[2,72,128]{2,1,0:T(8,128)S(1)}, u32[]{:S(2)}, u32[]{:S(2)}) %collective-permute-start) | collective-permute-done | bytes 73760 | tf_op jit(solution)/shard_map/ppermute | solution.py:68
  8.1 5.0 %collective-permute-start.1 = (bf16[4,80,128]{2,1,0:T(8,128)(2,1)S(1)}, bf16[4,80,128]{2,1,0:T(8,128)(2,1)S(1)}, u32[]{:S(2)}, u32[]{:S(2)}) collective-permute-start(bf16[4,80,128]{2,1,0:T(8,128)(2,1)S(1)} %pad_maximum_fusion.7), channel_id=1, source_target_pairs={{0,6},{1,7},{2,4},{3,5},{4,2},{5,3},{6,0},{7,1},{8,14},{9,15},{10,... | collective-permute-start | bytes 245768 | tf_op jit(solution)/shard_map/ppermute | solution.py:68
  13.2 2.4 %collective-permute-start.2 = (bf16[4,80,128]{2,1,0:T(8,128)(2,1)S(1)}, bf16[4,80,128]{2,1,0:T(8,128)(2,1)S(1)}, u32[]{:S(2)}, u32[]{:S(2)}) collective-permute-start(bf16[4,80,128]{2,1,0:T(8,128)(2,1)S(1)} %pad_maximum_fusion.7), channel_id=1, source_target_pairs={{0,17},{1,16},{2,19},{3,18},{4,21},{5,20},{6,23},{7,22},{8,25},{9,... | collective-permute-start | bytes 245768 | tf_op jit(solution)/shard_map/ppermute | solution.py:68
  18.6 2.7 %collective-permute-done.3 = bf16[4,80,128]{2,1,0:T(8,128)(2,1)S(1)} collective-permute-done((bf16[4,80,128]{2,1,0:T(8,128)(2,1)S(1)}, bf16[4,80,128]{2,1,0:T(8,128)(2,1)S(1)}, u32[]{:S(2)}, u32[]{:S(2)}) %collective-permute-start.3) | collective-permute-done | bytes 81952 | tf_op jit(solution)/shard_map/ppermute | solution.py:68
  21.4 2.0 %collective-permute-start.6 = (bf16[4,80,128]{2,1,0:T(8,128)(2,1)S(1)}, bf16[4,80,128]{2,1,0:T(8,128)(2,1)S(1)}, u32[]{:S(2)}, u32[]{:S(2)}) collective-permute-start(bf16[4,80,128]{2,1,0:T(8,128)(2,1)S(1)} %collective-permute-done.2), channel_id=1, source_target_pairs={{0,6},{1,7},{2,4},{3,5},{4,2},{5,3},{6,0},{7,1},{8,14},{9,15},{10,... | collective-permute-start | bytes 245768 | tf_op jit(solution)/shard_map/ppermute | solution.py:68
  23.3 2.5 %collective-permute-start.8 = (bf16[4,80,128]{2,1,0:T(8,128)(2,1)S(1)}, bf16[4,80,128]{2,1,0:T(8,128)(2,1)S(1)}, u32[]{:S(2)}, u32[]{:S(2)}) collective-permute-start(bf16[4,80,128]{2,1,0:T(8,128)(2,1)S(1)} %collective-permute-done.2), channel_id=1, source_target_pairs={{0,2},{1,3},{2,0},{3,1},{4,6},{5,7},{6,4},{7,5},{8,10},{9,11},{10,... | collective-permute-start | bytes 245768 | tf_op jit(solution)/shard_map/ppermute | solution.py:68
  26.5 2.2 %collective-permute-done.6 = bf16[4,80,128]{2,1,0:T(8,128)(2,1)S(1)} collective-permute-done((bf16[4,80,128]{2,1,0:T(8,128)(2,1)S(1)}, bf16[4,80,128]{2,1,0:T(8,128)(2,1)S(1)}, u32[]{:S(2)}, u32[]{:S(2)}) %collective-permute-start.6) | collective-permute-done | bytes 81952 | tf_op jit(solution)/shard_map/ppermute | solution.py:68
  28.7 2.1 %collective-permute-done.7 = bf16[4,80,128]{2,1,0:T(8,128)(2,1)S(1)} collective-permute-done((bf16[4,80,128]{2,1,0:T(8,128)(2,1)S(1)}, bf16[4,80,128]{2,1,0:T(8,128)(2,1)S(1)}, u32[]{:S(2)}, u32[]{:S(2)}) %collective-permute-start.7) | collective-permute-done | bytes 81952 | tf_op jit(solution)/shard_map/ppermute | solution.py:68
  30.9 2.2 %copy-done.3 = bf16[128,128,128]{2,1,0:T(8,128)(2,1)S(1)} copy-done((bf16[128,128,128]{2,1,0:T(8,128)(2,1)S(1)}, bf16[128,128,128]{2,1,0:T(8,128)(2,1)}, u32[]{:S(2)}) %copy-start.3) | copy-done | bytes 4194328
  33.1 2.5 %shard_map.87.tiles = bf16[256,128,128]{2,1,0:T(8,128)(2,1)S(1)} custom-call(bf16[128,128,128]{2,1,0:T(8,128)(2,1)S(1)} %copy-done.3, bf16[128,128,128]{2,1,0:T(8,128)(2,1)} %collective-permute-done.5.second), custom_call_target="tpu_custom_call" | custom-call | tf_op jit(solution)/shard_map/pallas_call | solution.py:250
  35.6 1.7 %shard_map.88 = (f32[32,64,128]{2,1,0:T(8,128)S(1)}, bf16[4,2,80,128]{3,2,1,0:T(8,128)(2,1)S(1)}) custom-call(s32[8,384]{1,0:T(8,128)S(1)} %shard_map.86.plan_in, bf16[256,128,128]{2,1,0:T(8,128)(2,1)S(1)} %shard_map.87.tiles, bf16[16,80,128]{2,1,0:T(8,128)(2,1)S(1)} %pad_maximum_fusion.field), custom_call_target="tpu_custom_call" | custom-call | flops 268435456 | bytes 8388608 | tf_op jit(solution)/shard_map/pallas_call | solution.py:366
  37.3 4.9 %shard_map.89 = (f32[32,64,128]{2,1,0:T(8,128)S(1)}, bf16[4,2,80,128]{3,2,1,0:T(8,128)(2,1)S(1)}, bf16[33,64,128]{2,1,0:T(8,128)(2,1)S(1)}, bf16[16,64,128]{2,1,...) custom-call(s32[8,384]{1,0:T(8,128)S(1)} %shard_map.86.plan_in, ...), custom_call_target="tpu_custom_call", output_to_operand_aliasing={{0}: (2, {}), {1}: (3, {})} | custom-call | flops 1610612736 | bytes 8388608 | tf_op jit(solution)/shard_map/pallas_call | solution.py:366
  42.2 1.7 %collective-permute-start.11 = (bf16[4,64,128]{2,1,0:T(8,128)(2,1)S(1)}, bf16[4,64,128]{2,1,0:T(8,128)(2,1)S(1)}, u32[]{:S(2)}, u32[]{:S(2)}) collective-permute-start(bf16[4,64,128]{2,1,0:T(8,128)(2,1)S(1)} %get-tuple-element.128), channel_id=1, source_target_pairs={{0,6},{1,7},{2,4},{3,5},{4,2},{5,3},{6,0},{7,1},{8,14},{9,15},{10,... | collective-permute-start | bytes 196616 | tf_op jit(solution)/shard_map/ppermute | solution.py:68
  46.6 1.8 %collective-permute-start.13 = (bf16[4,64,128]{2,1,0:T(8,128)(2,1)S(1)}, bf16[4,64,128]{2,1,0:T(8,128)(2,1)S(1)}, u32[]{:S(2)}, u32[]{:S(2)}) collective-permute-start(bf16[4,64,128]{2,1,0:T(8,128)(2,1)S(1)} %get-tuple-element.132), channel_id=1, source_target_pairs={{0,2},{1,3},{2,0},{3,1},{4,6},{5,7},{6,4},{7,5},{8,10},{9,11},{10,... | collective-permute-start | bytes 196616 | tf_op jit(solution)/shard_map/ppermute | solution.py:68
  50.4 1.4 collective-permute-done.12
  53.2 1.4 collective-permute-start.16
  56.2 2.4 %collective-permute-start.19 = (bf16[4,64,128]{2,1,0:T(8,128)(2,1)S(1)}, bf16[4,64,128]{2,1,0:T(8,128)(2,1)S(1)}, u32[]{:S(2)}, u32[]{:S(2)}) collective-permute-start(bf16[4,64,128]{2,1,0:T(8,128)(2,1)S(1)} %get-tuple-element.148), channel_id=1, source_target_pairs={{0,2},{1,3},{2,0},{3,1},{4,6},{5,7},{6,4},{7,5},{8,10},{9,11},{10,... | collective-permute-start | bytes 196616 | tf_op jit(solution)/shard_map/ppermute | solution.py:68
  60.0 1.9 %collective-permute-done.18 = bf16[4,64,128]{2,1,0:T(8,128)(2,1)S(1)} collective-permute-done((bf16[4,64,128]{2,1,0:T(8,128)(2,1)S(1)}, bf16[4,64,128]{2,1,0:T(8,128)(2,1)S(1)}, u32[]{:S(2)}, u32[]{:S(2)}) %collective-permute-start.18) | collective-permute-done | bytes 65568 | tf_op jit(solution)/shard_map/ppermute | solution.py:68
  62.0 1.6 %collective-permute-start.20 = (bf16[4,64,128]{2,1,0:T(8,128)(2,1)S(1)}, bf16[4,64,128]{2,1,0:T(8,128)(2,1)S(1)}, u32[]{:S(2)}, u32[]{:S(2)}) collective-permute-start(bf16[4,64,128]{2,1,0:T(8,128)(2,1)S(1)} %get-tuple-element.231), channel_id=1, source_target_pairs={{0,6},{1,7},{2,4},{3,5},{4,2},{5,3},{6,0},{7,1},{8,14},{9,15},{10,... | collective-permute-start | bytes 196616 | tf_op jit(solution)/shard_map/ppermute | solution.py:68
  63.6 2.2 %collective-permute-start.21 = (bf16[4,64,128]{2,1,0:T(8,128)(2,1)S(1)}, bf16[4,64,128]{2,1,0:T(8,128)(2,1)S(1)}, u32[]{:S(2)}, u32[]{:S(2)}) collective-permute-start(bf16[4,64,128]{2,1,0:T(8,128)(2,1)S(1)} %get-tuple-element.231), channel_id=1, source_target_pairs={{0,17},{1,16},{2,19},{3,18},{4,21},{5,20},{6,23},{7,22},{8,25},{9,... | collective-permute-start | bytes 196616 | tf_op jit(solution)/shard_map/ppermute | solution.py:68
  66.5 1.6 %collective-permute-start.23 = (bf16[4,64,128]{2,1,0:T(8,128)(2,1)S(1)}, bf16[4,64,128]{2,1,0:T(8,128)(2,1)S(1)}, u32[]{:S(2)}, u32[]{:S(2)}) collective-permute-start(bf16[4,64,128]{2,1,0:T(8,128)(2,1)S(1)} %get-tuple-element.231), channel_id=1, source_target_pairs={{0,2},{1,3},{2,0},{3,1},{4,6},{5,7},{6,4},{7,5},{8,10},{9,11},{10,... | collective-permute-start | bytes 196616 | tf_op jit(solution)/shard_map/ppermute | solution.py:68
  68.8 2.3 %collective-permute-done.22 = bf16[4,64,128]{2,1,0:T(8,128)(2,1)S(1)} collective-permute-done((bf16[4,64,128]{2,1,0:T(8,128)(2,1)S(1)}, bf16[4,64,128]{2,1,0:T(8,128)(2,1)S(1)}, u32[]{:S(2)}, u32[]{:S(2)}) %collective-permute-start.22) | collective-permute-done | bytes 65568 | tf_op jit(solution)/shard_map/ppermute | solution.py:68
  73.1 2.1 %collective-permute-start.24 = (bf16[4,64,128]{2,1,0:T(8,128)(2,1)S(1)}, bf16[4,64,128]{2,1,0:T(8,128)(2,1)S(1)}, u32[]{:S(2)}, u32[]{:S(2)}) collective-permute-start(bf16[4,64,128]{2,1,0:T(8,128)(2,1)S(1)} %collective-permute-done.21), channel_id=1, source_target_pairs={{0,6},{1,7},{2,4},{3,5},{4,2},{5,3},{6,0},{7,1},{8,14},{9,15},{10,... | collective-permute-start | bytes 196616 | tf_op jit(solution)/shard_map/ppermute | solution.py:68
  75.8 1.7 %collective-permute-start.26 = (bf16[4,64,128]{2,1,0:T(8,128)(2,1)S(1)}, bf16[4,64,128]{2,1,0:T(8,128)(2,1)S(1)}, u32[]{:S(2)}, u32[]{:S(2)}) collective-permute-start(bf16[4,64,128]{2,1,0:T(8,128)(2,1)S(1)} %collective-permute-done.21), channel_id=1, source_target_pairs={{0,2},{1,3},{2,0},{3,1},{4,6},{5,7},{6,4},{7,5},{8,10},{9,11},{10,... | collective-permute-start | bytes 196616 | tf_op jit(solution)/shard_map/ppermute | solution.py:68
  77.5 1.8 %shard_map.91 = (f32[32,64,128]{2,1,0:T(8,128)S(1)}, bf16[4,2,64,128]{3,2,1,0:T(8,128)(2,1)S(1)}) custom-call(s32[8,384]{1,0:T(8,128)S(1)} %shard_map.86.plan_in, bf16[256,128,128]{2,1,0:T(8,128)(2,1)S(1)} %shard_map.87.tiles, bf16[16,64,128]{2,1,0:T(8,128)(2,1)S(1)} %pad_maximum_fusion.2.field), custom_call_target="tpu_custom_call" | custom-call | flops 268435456 | bytes 8388608 | tf_op jit(solution)/shard_map/pallas_call | solution.py:366
  80.8 4.9 %shard_map.92 = (f32[32,64,128]{2,1,0:T(8,128)S(1)}, bf16[4,2,64,128]{3,2,1,0:T(8,128)(2,1)S(1)}, bf16[33,64,128]{2,1,0:T(8,128)(2,1)S(1)}, bf16[16,64,128]{2,1,...) custom-call(s32[8,384]{1,0:T(8,128)S(1)} %shard_map.86.plan_in, ...), custom_call_target="tpu_custom_call", output_to_operand_aliasing={{0}: (2, {}), {1}: (3, {})} | custom-call | flops 1610612736 | bytes 8388608 | tf_op jit(solution)/shard_map/pallas_call | solution.py:366
  87.5 2.7 %collective-permute-start.29 = (bf16[4,64,128]{2,1,0:T(8,128)(2,1)S(1)}, bf16[4,64,128]{2,1,0:T(8,128)(2,1)S(1)}, u32[]{:S(2)}, u32[]{:S(2)}) collective-permute-start(bf16[4,64,128]{2,1,0:T(8,128)(2,1)S(1)} %get-tuple-element.165), channel_id=1, source_target_pairs={{0,6},{1,7},{2,4},{3,5},{4,2},{5,3},{6,0},{7,1},{8,14},{9,15},{10,... | collective-permute-start | bytes 196616 | tf_op jit(solution)/shard_map/ppermute | solution.py:68
  92.0 1.7 %collective-permute-done.29 = bf16[4,64,128]{2,1,0:T(8,128)(2,1)S(1)} collective-permute-done((bf16[4,64,128]{2,1,0:T(8,128)(2,1)S(1)}, bf16[4,64,128]{2,1,0:T(8,128)(2,1)S(1)}, u32[]{:S(2)}, u32[]{:S(2)}) %collective-permute-start.29) | collective-permute-done | bytes 65568 | tf_op jit(solution)/shard_map/ppermute | solution.py:68
  93.7 1.4 shard_map.93
  95.1 1.7 %collective-permute-done.30 = bf16[4,64,128]{2,1,0:T(8,128)(2,1)S(1)} collective-permute-done((bf16[4,64,128]{2,1,0:T(8,128)(2,1)S(1)}, bf16[4,64,128]{2,1,0:T(8,128)(2,1)S(1)}, u32[]{:S(2)}, u32[]{:S(2)}) %collective-permute-start.30) | collective-permute-done | bytes 65568 | tf_op jit(solution)/shard_map/ppermute | solution.py:68
  97.0 3.1 %collective-permute-start.34 = (bf16[4,64,128]{2,1,0:T(8,128)(2,1)S(1)}, bf16[4,64,128]{2,1,0:T(8,128)(2,1)S(1)}, u32[]{:S(2)}, u32[]{:S(2)}) collective-permute-start(bf16[4,64,128]{2,1,0:T(8,128)(2,1)S(1)} %get-tuple-element.180), channel_id=1, source_target_pairs={{0,6},{1,7},{2,4},{3,5},{4,2},{5,3},{6,0},{7,1},{8,14},{9,15},{10,... | collective-permute-start | bytes 196616 | tf_op jit(solution)/shard_map/ppermute | solution.py:68
  100.1 3.5 %collective-permute-start.37 = (bf16[4,64,128]{2,1,0:T(8,128)(2,1)S(1)}, bf16[4,64,128]{2,1,0:T(8,128)(2,1)S(1)}, u32[]{:S(2)}, u32[]{:S(2)}) collective-permute-start(bf16[4,64,128]{2,1,0:T(8,128)(2,1)S(1)} %get-tuple-element.185), channel_id=1, source_target_pairs={{0,2},{1,3},{2,0},{3,1},{4,6},{5,7},{6,4},{7,5},{8,10},{9,11},{10,... | collective-permute-start | bytes 196616 | tf_op jit(solution)/shard_map/ppermute | solution.py:68
  103.6 1.7 %collective-permute-done.35 = bf16[4,64,128]{2,1,0:T(8,128)(2,1)S(1)} collective-permute-done((bf16[4,64,128]{2,1,0:T(8,128)(2,1)S(1)}, bf16[4,64,128]{2,1,0:T(8,128)(2,1)S(1)}, u32[]{:S(2)}, u32[]{:S(2)}) %collective-permute-start.35) | collective-permute-done | bytes 65568 | tf_op jit(solution)/shard_map/ppermute | solution.py:68
  105.3 1.5 collective-permute-done.36
  107.3 1.9 %collective-permute-start.38 = (bf16[4,64,128]{2,1,0:T(8,128)(2,1)S(1)}, bf16[4,64,128]{2,1,0:T(8,128)(2,1)S(1)}, u32[]{:S(2)}, u32[]{:S(2)}) collective-permute-start(bf16[4,64,128]{2,1,0:T(8,128)(2,1)S(1)} %get-tuple-element.226), channel_id=1, source_target_pairs={{0,6},{1,7},{2,4},{3,5},{4,2},{5,3},{6,0},{7,1},{8,14},{9,15},{10,... | collective-permute-start | bytes 196616 | tf_op jit(solution)/shard_map/ppermute | solution.py:68
  109.2 2.0 %collective-permute-start.39 = (bf16[4,64,128]{2,1,0:T(8,128)(2,1)S(1)}, bf16[4,64,128]{2,1,0:T(8,128)(2,1)S(1)}, u32[]{:S(2)}, u32[]{:S(2)}) collective-permute-start(bf16[4,64,128]{2,1,0:T(8,128)(2,1)S(1)} %get-tuple-element.226), channel_id=1, source_target_pairs={{0,17},{1,16},{2,19},{3,18},{4,21},{5,20},{6,23},{7,22},{8,25},{9,... | collective-permute-start | bytes 196616 | tf_op jit(solution)/shard_map/ppermute | solution.py:68
  111.2 2.1 %collective-permute-start.41 = (bf16[4,64,128]{2,1,0:T(8,128)(2,1)S(1)}, bf16[4,64,128]{2,1,0:T(8,128)(2,1)S(1)}, u32[]{:S(2)}, u32[]{:S(2)}) collective-permute-start(bf16[4,64,128]{2,1,0:T(8,128)(2,1)S(1)} %get-tuple-element.226), channel_id=1, source_target_pairs={{0,2},{1,3},{2,0},{3,1},{4,6},{5,7},{6,4},{7,5},{8,10},{9,11},{10,... | collective-permute-start | bytes 196616 | tf_op jit(solution)/shard_map/ppermute | solution.py:68
  114.4 2.3 %collective-permute-done.40 = bf16[4,64,128]{2,1,0:T(8,128)(2,1)S(1)} collective-permute-done((bf16[4,64,128]{2,1,0:T(8,128)(2,1)S(1)}, bf16[4,64,128]{2,1,0:T(8,128)(2,1)S(1)}, u32[]{:S(2)}, u32[]{:S(2)}) %collective-permute-start.40) | collective-permute-done | bytes 65568 | tf_op jit(solution)/shard_map/ppermute | solution.py:68
  119.1 2.2 %collective-permute-start.42 = (bf16[4,64,128]{2,1,0:T(8,128)(2,1)S(1)}, bf16[4,64,128]{2,1,0:T(8,128)(2,1)S(1)}, u32[]{:S(2)}, u32[]{:S(2)}) collective-permute-start(bf16[4,64,128]{2,1,0:T(8,128)(2,1)S(1)} %collective-permute-done.39), channel_id=1, source_target_pairs={{0,6},{1,7},{2,4},{3,5},{4,2},{5,3},{6,0},{7,1},{8,14},{9,15},{10,... | collective-permute-start | bytes 196616 | tf_op jit(solution)/shard_map/ppermute | solution.py:68
  121.3 2.2 %collective-permute-start.44 = (bf16[4,64,128]{2,1,0:T(8,128)(2,1)S(1)}, bf16[4,64,128]{2,1,0:T(8,128)(2,1)S(1)}, u32[]{:S(2)}, u32[]{:S(2)}) collective-permute-start(bf16[4,64,128]{2,1,0:T(8,128)(2,1)S(1)} %collective-permute-done.39), channel_id=1, source_target_pairs={{0,2},{1,3},{2,0},{3,1},{4,6},{5,7},{6,4},{7,5},{8,10},{9,11},{10,... | collective-permute-start | bytes 196616 | tf_op jit(solution)/shard_map/ppermute | solution.py:68
  123.5 3.4 %copy-done.1 = bf16[256,128,128]{2,1,0:T(8,128)(2,1)S(1)} copy-done((bf16[256,128,128]{2,1,0:T(8,128)(2,1)S(1)}, bf16[256,128,128]{2,1,0:T(8,128)(2,1)}, u32[]{:S(2)}) %copy-start.1) | copy-done | bytes 8388632
  126.9 1.8 %shard_map.94 = (f32[32,64,128]{2,1,0:T(8,128)S(1)}, bf16[4,2,64,128]{3,2,1,0:T(8,128)(2,1)S(1)}) custom-call(s32[8,384]{1,0:T(8,128)S(1)} %shard_map.86.plan_in, bf16[256,128,128]{2,1,0:T(8,128)(2,1)S(1)} %copy-done.1, bf16[16,64,128]{2,1,0:T(8,128)(2,1)S(1)} %pad_maximum_fusion.4.field), custom_call_target="tpu_custom_call" | custom-call | flops 268435456 | bytes 8388608 | tf_op jit(solution)/shard_map/pallas_call | solution.py:366
  128.8 1.5 copy-done.2
  130.3 5.1 %shard_map.95 = (f32[32,64,128]{2,1,0:T(8,128)S(1)}, bf16[4,2,64,128]{3,2,1,0:T(8,128)(2,1)S(1)}, bf16[33,64,128]{2,1,0:T(8,128)(2,1)S(1)}, bf16[16,64,128]{2,1,...) custom-call(s32[8,384]{1,0:T(8,128)S(1)} %shard_map.86.plan_in, ...), custom_call_target="tpu_custom_call", output_to_operand_aliasing={{0}: (2, {}), {1}: (3, {})} | custom-call | flops 1610612736 | bytes 8388608 | tf_op jit(solution)/shard_map/pallas_call | solution.py:366
  136.4 3.2 %collective-permute-start.47 = (bf16[4,64,128]{2,1,0:T(8,128)(2,1)S(1)}, bf16[4,64,128]{2,1,0:T(8,128)(2,1)S(1)}, u32[]{:S(2)}, u32[]{:S(2)}) collective-permute-start(bf16[4,64,128]{2,1,0:T(8,128)(2,1)S(1)} %get-tuple-element.202), channel_id=1, source_target_pairs={{0,6},{1,7},{2,4},{3,5},{4,2},{5,3},{6,0},{7,1},{8,14},{9,15},{10,... | collective-permute-start | bytes 196616 | tf_op jit(solution)/shard_map/ppermute | solution.py:68
  140.9 1.6 %collective-permute-done.47 = bf16[4,64,128]{2,1,0:T(8,128)(2,1)S(1)} collective-permute-done((bf16[4,64,128]{2,1,0:T(8,128)(2,1)S(1)}, bf16[4,64,128]{2,1,0:T(8,128)(2,1)S(1)}, u32[]{:S(2)}, u32[]{:S(2)}) %collective-permute-start.47) | collective-permute-done | bytes 65568 | tf_op jit(solution)/shard_map/ppermute | solution.py:68
  145.0 2.5 %collective-permute-start.52 = (bf16[4,64,128]{2,1,0:T(8,128)(2,1)S(1)}, bf16[4,64,128]{2,1,0:T(8,128)(2,1)S(1)}, u32[]{:S(2)}, u32[]{:S(2)}) collective-permute-start(bf16[4,64,128]{2,1,0:T(8,128)(2,1)S(1)} %get-tuple-element.217), channel_id=1, source_target_pairs={{0,6},{1,7},{2,4},{3,5},{4,2},{5,3},{6,0},{7,1},{8,14},{9,15},{10,... | collective-permute-start | bytes 196616 | tf_op jit(solution)/shard_map/ppermute | solution.py:68
  149.4 1.8 %collective-permute-start.55 = (bf16[4,64,128]{2,1,0:T(8,128)(2,1)S(1)}, bf16[4,64,128]{2,1,0:T(8,128)(2,1)S(1)}, u32[]{:S(2)}, u32[]{:S(2)}) collective-permute-start(bf16[4,64,128]{2,1,0:T(8,128)(2,1)S(1)} %get-tuple-element.222), channel_id=1, source_target_pairs={{0,2},{1,3},{2,0},{3,1},{4,6},{5,7},{6,4},{7,5},{8,10},{9,11},{10,... | collective-permute-start | bytes 196616 | tf_op jit(solution)/shard_map/ppermute | solution.py:68
  (144 shorter events, 42.1 us)
Async XLA Ops:
  0.6 30.2 %collective-permute-start.5 = (bf16[128,128,128]{2,1,0:T(8,128)(2,1)}, bf16[128,128,128]{2,1,0:T(8,128)(2,1)}, u32[]{:S(2)}, u32[]{:S(2)}) collective-permute-start(bf16[128,128,128]{2,1,0:T(8,128)(2,1)} %first.1), channel_id=1, source_target_pairs={{0,8},{1,9},{2,10},{3,11},{4,12},{5,13},{6,14},{7,15},{8,0},{9,1},... | collective-permute-start | bytes 12582920 | tf_op jit(solution)/shard_map/ppermute | solution.py:68
  8.1 10.5 %collective-permute-start.1 = (bf16[4,80,128]{2,1,0:T(8,128)(2,1)S(1)}, bf16[4,80,128]{2,1,0:T(8,128)(2,1)S(1)}, u32[]{:S(2)}, u32[]{:S(2)}) collective-permute-start(bf16[4,80,128]{2,1,0:T(8,128)(2,1)S(1)} %pad_maximum_fusion.7), channel_id=1, source_target_pairs={{0,6},{1,7},{2,4},{3,5},{4,2},{5,3},{6,0},{7,1},{8,14},{9,15},{10,... | collective-permute-start | bytes 245768 | tf_op jit(solution)/shard_map/ppermute | solution.py:68
  13.2 5.4 %collective-permute-start.2 = (bf16[4,80,128]{2,1,0:T(8,128)(2,1)S(1)}, bf16[4,80,128]{2,1,0:T(8,128)(2,1)S(1)}, u32[]{:S(2)}, u32[]{:S(2)}) collective-permute-start(bf16[4,80,128]{2,1,0:T(8,128)(2,1)S(1)} %pad_maximum_fusion.7), channel_id=1, source_target_pairs={{0,17},{1,16},{2,19},{3,18},{4,21},{5,20},{6,23},{7,22},{8,25},{9,... | collective-permute-start | bytes 245768 | tf_op jit(solution)/shard_map/ppermute | solution.py:68
  15.6 5.7 %collective-permute-start.3 = (bf16[4,80,128]{2,1,0:T(8,128)(2,1)S(1)}, bf16[4,80,128]{2,1,0:T(8,128)(2,1)S(1)}, u32[]{:S(2)}, u32[]{:S(2)}) collective-permute-start(bf16[4,80,128]{2,1,0:T(8,128)(2,1)S(1)} %pad_maximum_fusion.7), channel_id=1, source_target_pairs={{0,4},{1,5},{2,6},{3,7},{4,0},{5,1},{6,2},{7,3},{8,12},{9,13},{10,... | collective-permute-start | bytes 245768 | tf_op jit(solution)/shard_map/ppermute | solution.py:68
  15.6 5.7 %collective-permute-start.4 = (bf16[4,80,128]{2,1,0:T(8,128)(2,1)S(1)}, bf16[4,80,128]{2,1,0:T(8,128)(2,1)S(1)}, u32[]{:S(2)}, u32[]{:S(2)}) collective-permute-start(bf16[4,80,128]{2,1,0:T(8,128)(2,1)S(1)} %pad_maximum_fusion.7), channel_id=1, source_target_pairs={{0,2},{1,3},{2,0},{3,1},{4,6},{5,7},{6,4},{7,5},{8,10},{9,11},{10,... | collective-permute-start | bytes 245768 | tf_op jit(solution)/shard_map/ppermute | solution.py:68
  21.4 7.3 %collective-permute-start.6 = (bf16[4,80,128]{2,1,0:T(8,128)(2,1)S(1)}, bf16[4,80,128]{2,1,0:T(8,128)(2,1)S(1)}, u32[]{:S(2)}, u32[]{:S(2)}) collective-permute-start(bf16[4,80,128]{2,1,0:T(8,128)(2,1)S(1)} %collective-permute-done.2), channel_id=1, source_target_pairs={{0,6},{1,7},{2,4},{3,5},{4,2},{5,3},{6,0},{7,1},{8,14},{9,15},{10,... | collective-permute-start | bytes 245768 | tf_op jit(solution)/shard_map/ppermute | solution.py:68
  23.3 7.5 %collective-permute-start.7 = (bf16[4,80,128]{2,1,0:T(8,128)(2,1)S(1)}, bf16[4,80,128]{2,1,0:T(8,128)(2,1)S(1)}, u32[]{:S(2)}, u32[]{:S(2)}) collective-permute-start(bf16[4,80,128]{2,1,0:T(8,128)(2,1)S(1)} %collective-permute-done.2), channel_id=1, source_target_pairs={{0,4},{1,5},{2,6},{3,7},{4,0},{5,1},{6,2},{7,3},{8,12},{9,13},{10,... | collective-permute-start | bytes 245768 | tf_op jit(solution)/shard_map/ppermute | solution.py:68
  23.3 7.5 %collective-permute-start.8 = (bf16[4,80,128]{2,1,0:T(8,128)(2,1)S(1)}, bf16[4,80,128]{2,1,0:T(8,128)(2,1)S(1)}, u32[]{:S(2)}, u32[]{:S(2)}) collective-permute-start(bf16[4,80,128]{2,1,0:T(8,128)(2,1)S(1)} %collective-permute-done.2), channel_id=1, source_target_pairs={{0,2},{1,3},{2,0},{3,1},{4,6},{5,7},{6,4},{7,5},{8,10},{9,11},{10,... | collective-permute-start | bytes 245768 | tf_op jit(solution)/shard_map/ppermute | solution.py:68
  25.8 11.5 %collective-permute-start.10 = (bf16[16,80,128]{2,1,0:T(8,128)(2,1)S(1)}, bf16[16,80,128]{2,1,0:T(8,128)(2,1)S(1)}, u32[]{:S(2)}, u32[]{:S(2)}) collective-permute-start(bf16[16,80,128]{2,1,0:T(8,128)(2,1)S(1)} %pad_maximum_fusion.field), channel_id=1, source_target_pairs={{0,16},{1,17},{2,18},{3,19},{4,20},{5,21},{6,22},{7,23},{8,9},{9,8... | collective-permute-start | bytes 983048 | tf_op jit(solution)/shard_map/ppermute | solution.py:68
  28.7 8.7 %collective-permute-start.9 = (bf16[16,80,128]{2,1,0:T(8,128)(2,1)S(1)}, bf16[16,80,128]{2,1,0:T(8,128)(2,1)S(1)}, u32[]{:S(2)}, u32[]{:S(2)}) collective-permute-start(bf16[16,80,128]{2,1,0:T(8,128)(2,1)S(1)} %pad_maximum_fusion.field), channel_id=1, source_target_pairs={{0,1},{1,0},{2,3},{3,2},{4,5},{5,4},{6,7},{7,6},{8,24},{9,25},{10,... | collective-permute-start | bytes 983048 | tf_op jit(solution)/shard_map/ppermute | solution.py:68
  42.2 6.7 %collective-permute-start.11 = (bf16[4,64,128]{2,1,0:T(8,128)(2,1)S(1)}, bf16[4,64,128]{2,1,0:T(8,128)(2,1)S(1)}, u32[]{:S(2)}, u32[]{:S(2)}) collective-permute-start(bf16[4,64,128]{2,1,0:T(8,128)(2,1)S(1)} %get-tuple-element.128), channel_id=1, source_target_pairs={{0,6},{1,7},{2,4},{3,5},{4,2},{5,3},{6,0},{7,1},{8,14},{9,15},{10,... | collective-permute-start | bytes 196616 | tf_op jit(solution)/shard_map/ppermute | solution.py:68
  44.0 9.1 %collective-permute-start.14 = (bf16[16,64,128]{2,1,0:T(8,128)(2,1)S(1)}, bf16[16,64,128]{2,1,0:T(8,128)(2,1)S(1)}, u32[]{:S(2)}, u32[]{:S(2)}) collective-permute-start(bf16[16,64,128]{2,1,0:T(8,128)(2,1)S(1)} %get-tuple-element.133), channel_id=1, source_target_pairs={{0,1},{1,0},{2,3},{3,2},{4,5},{5,4},{6,7},{7,6},{8,24},{9,25},{10,... | collective-permute-start | bytes 786440 | tf_op jit(solution)/shard_map/ppermute | solution.py:68
  45.3 7.8 %collective-permute-start.15 = (bf16[16,64,128]{2,1,0:T(8,128)(2,1)S(1)}, bf16[16,64,128]{2,1,0:T(8,128)(2,1)S(1)}, u32[]{:S(2)}, u32[]{:S(2)}) collective-permute-start(bf16[16,64,128]{2,1,0:T(8,128)(2,1)S(1)} %get-tuple-element.134), channel_id=1, source_target_pairs={{0,16},{1,17},{2,18},{3,19},{4,20},{5,21},{6,22},{7,23},{8,9},{9,8... | collective-permute-start | bytes 786440 | tf_op jit(solution)/shard_map/ppermute | solution.py:68
  46.6 5.2 %collective-permute-start.12 = (bf16[4,64,128]{2,1,0:T(8,128)(2,1)S(1)}, bf16[4,64,128]{2,1,0:T(8,128)(2,1)S(1)}, u32[]{:S(2)}, u32[]{:S(2)}) collective-permute-start(bf16[4,64,128]{2,1,0:T(8,128)(2,1)S(1)} %get-tuple-element.131), channel_id=1, source_target_pairs={{0,4},{1,5},{2,6},{3,7},{4,0},{5,1},{6,2},{7,3},{8,12},{9,13},{10,... | collective-permute-start | bytes 196616 | tf_op jit(solution)/shard_map/ppermute | solution.py:68
  46.6 5.3 %collective-permute-start.13 = (bf16[4,64,128]{2,1,0:T(8,128)(2,1)S(1)}, bf16[4,64,128]{2,1,0:T(8,128)(2,1)S(1)}, u32[]{:S(2)}, u32[]{:S(2)}) collective-permute-start(bf16[4,64,128]{2,1,0:T(8,128)(2,1)S(1)} %get-tuple-element.132), channel_id=1, source_target_pairs={{0,2},{1,3},{2,0},{3,1},{4,6},{5,7},{6,4},{7,5},{8,10},{9,11},{10,... | collective-permute-start | bytes 196616 | tf_op jit(solution)/shard_map/ppermute | solution.py:68
  53.2 6.8 %collective-permute-start.16 = (bf16[4,64,128]{2,1,0:T(8,128)(2,1)S(1)}, bf16[4,64,128]{2,1,0:T(8,128)(2,1)S(1)}, u32[]{:S(2)}, u32[]{:S(2)}) collective-permute-start(bf16[4,64,128]{2,1,0:T(8,128)(2,1)S(1)} %get-tuple-element.143), channel_id=1, source_target_pairs={{0,6},{1,7},{2,4},{3,5},{4,2},{5,3},{6,0},{7,1},{8,14},{9,15},{10,... | collective-permute-start | bytes 196616 | tf_op jit(solution)/shard_map/ppermute | solution.py:68
  54.6 5.4 %collective-permute-start.17 = (bf16[4,64,128]{2,1,0:T(8,128)(2,1)S(1)}, bf16[4,64,128]{2,1,0:T(8,128)(2,1)S(1)}, u32[]{:S(2)}, u32[]{:S(2)}) collective-permute-start(bf16[4,64,128]{2,1,0:T(8,128)(2,1)S(1)} %add_convert_fusion.2), channel_id=1, source_target_pairs={{0,17},{1,16},{2,19},{3,18},{4,21},{5,20},{6,23},{7,22},{8,25},{9,... | collective-permute-start | bytes 196616 | tf_op jit(solution)/shard_map/ppermute | solution.py:68
  55.8 6.1 %collective-permute-start.18 = (bf16[4,64,128]{2,1,0:T(8,128)(2,1)S(1)}, bf16[4,64,128]{2,1,0:T(8,128)(2,1)S(1)}, u32[]{:S(2)}, u32[]{:S(2)}) collective-permute-start(bf16[4,64,128]{2,1,0:T(8,128)(2,1)S(1)} %get-tuple-element.147), channel_id=1, source_target_pairs={{0,4},{1,5},{2,6},{3,7},{4,0},{5,1},{6,2},{7,3},{8,12},{9,13},{10,... | collective-permute-start | bytes 196616 | tf_op jit(solution)/shard_map/ppermute | solution.py:68
  56.2 5.7 %collective-permute-start.19 = (bf16[4,64,128]{2,1,0:T(8,128)(2,1)S(1)}, bf16[4,64,128]{2,1,0:T(8,128)(2,1)S(1)}, u32[]{:S(2)}, u32[]{:S(2)}) collective-permute-start(bf16[4,64,128]{2,1,0:T(8,128)(2,1)S(1)} %get-tuple-element.148), channel_id=1, source_target_pairs={{0,2},{1,3},{2,0},{3,1},{4,6},{5,7},{6,4},{7,5},{8,10},{9,11},{10,... | collective-permute-start | bytes 196616 | tf_op jit(solution)/shard_map/ppermute | solution.py:68
  62.0 6.2 %collective-permute-start.20 = (bf16[4,64,128]{2,1,0:T(8,128)(2,1)S(1)}, bf16[4,64,128]{2,1,0:T(8,128)(2,1)S(1)}, u32[]{:S(2)}, u32[]{:S(2)}) collective-permute-start(bf16[4,64,128]{2,1,0:T(8,128)(2,1)S(1)} %get-tuple-element.231), channel_id=1, source_target_pairs={{0,6},{1,7},{2,4},{3,5},{4,2},{5,3},{6,0},{7,1},{8,14},{9,15},{10,... | collective-permute-start | bytes 196616 | tf_op jit(solution)/shard_map/ppermute | solution.py:68
  63.6 5.2 %collective-permute-start.21 = (bf16[4,64,128]{2,1,0:T(8,128)(2,1)S(1)}, bf16[4,64,128]{2,1,0:T(8,128)(2,1)S(1)}, u32[]{:S(2)}, u32[]{:S(2)}) collective-permute-start(bf16[4,64,128]{2,1,0:T(8,128)(2,1)S(1)} %get-tuple-element.231), channel_id=1, source_target_pairs={{0,17},{1,16},{2,19},{3,18},{4,21},{5,20},{6,23},{7,22},{8,25},{9,... | collective-permute-start | bytes 196616 | tf_op jit(solution)/shard_map/ppermute | solution.py:68
  65.8 5.3 %collective-permute-start.22 = (bf16[4,64,128]{2,1,0:T(8,128)(2,1)S(1)}, bf16[4,64,128]{2,1,0:T(8,128)(2,1)S(1)}, u32[]{:S(2)}, u32[]{:S(2)}) collective-permute-start(bf16[4,64,128]{2,1,0:T(8,128)(2,1)S(1)} %get-tuple-element.231), channel_id=1, source_target_pairs={{0,4},{1,5},{2,6},{3,7},{4,0},{5,1},{6,2},{7,3},{8,12},{9,13},{10,... | collective-permute-start | bytes 196616 | tf_op jit(solution)/shard_map/ppermute | solution.py:68
  71.6 9.2 %collective-permute-start.27 = (bf16[16,64,128]{2,1,0:T(8,128)(2,1)S(1)}, bf16[16,64,128]{2,1,0:T(8,128)(2,1)S(1)}, u32[]{:S(2)}, u32[]{:S(2)}) collective-permute-start(bf16[16,64,128]{2,1,0:T(8,128)(2,1)S(1)} %pad_maximum_fusion.2.field), channel_id=1, source_target_pairs={{0,1},{1,0},{2,3},{3,2},{4,5},{5,4},{6,7},{7,6},{8,24},{9,25},{10,... | collective-permute-start | bytes 786440 | tf_op jit(solution)/shard_map/ppermute | solution.py:68
  72.7 8.2 %collective-permute-start.28 = (bf16[16,64,128]{2,1,0:T(8,128)(2,1)S(1)}, bf16[16,64,128]{2,1,0:T(8,128)(2,1)S(1)}, u32[]{:S(2)}, u32[]{:S(2)}) collective-permute-start(bf16[16,64,128]{2,1,0:T(8,128)(2,1)S(1)} %pad_maximum_fusion.2.field), channel_id=1, source_target_pairs={{0,16},{1,17},{2,18},{3,19},{4,20},{5,21},{6,22},{7,23},{8,9},{9,8... | collective-permute-start | bytes 786440 | tf_op jit(solution)/shard_map/ppermute | solution.py:68
  73.1 6.2 %collective-permute-start.24 = (bf16[4,64,128]{2,1,0:T(8,128)(2,1)S(1)}, bf16[4,64,128]{2,1,0:T(8,128)(2,1)S(1)}, u32[]{:S(2)}, u32[]{:S(2)}) collective-permute-start(bf16[4,64,128]{2,1,0:T(8,128)(2,1)S(1)} %collective-permute-done.21), channel_id=1, source_target_pairs={{0,6},{1,7},{2,4},{3,5},{4,2},{5,3},{6,0},{7,1},{8,14},{9,15},{10,... | collective-permute-start | bytes 196616 | tf_op jit(solution)/shard_map/ppermute | solution.py:68
  75.1 5.5 %collective-permute-start.25 = (bf16[4,64,128]{2,1,0:T(8,128)(2,1)S(1)}, bf16[4,64,128]{2,1,0:T(8,128)(2,1)S(1)}, u32[]{:S(2)}, u32[]{:S(2)}) collective-permute-start(bf16[4,64,128]{2,1,0:T(8,128)(2,1)S(1)} %collective-permute-done.21), channel_id=1, source_target_pairs={{0,4},{1,5},{2,6},{3,7},{4,0},{5,1},{6,2},{7,3},{8,12},{9,13},{10,... | collective-permute-start | bytes 196616 | tf_op jit(solution)/shard_map/ppermute | solution.py:68
  85.8 11.0 %collective-permute-start.32 = (bf16[16,64,128]{2,1,0:T(8,128)(2,1)S(1)}, bf16[16,64,128]{2,1,0:T(8,128)(2,1)S(1)}, u32[]{:S(2)}, u32[]{:S(2)}) collective-permute-start(bf16[16,64,128]{2,1,0:T(8,128)(2,1)S(1)} %get-tuple-element.170), channel_id=1, source_target_pairs={{0,1},{1,0},{2,3},{3,2},{4,5},{5,4},{6,7},{7,6},{8,24},{9,25},{10,... | collective-permute-start | bytes 786440 | tf_op jit(solution)/shard_map/ppermute | solution.py:68
  86.6 10.2 %collective-permute-start.33 = (bf16[16,64,128]{2,1,0:T(8,128)(2,1)S(1)}, bf16[16,64,128]{2,1,0:T(8,128)(2,1)S(1)}, u32[]{:S(2)}, u32[]{:S(2)}) collective-permute-start(bf16[16,64,128]{2,1,0:T(8,128)(2,1)S(1)} %get-tuple-element.171), channel_id=1, source_target_pairs={{0,16},{1,17},{2,18},{3,19},{4,20},{5,21},{6,22},{7,23},{8,9},{9,8... | collective-permute-start | bytes 786440 | tf_op jit(solution)/shard_map/ppermute | solution.py:68
  87.5 6.2 %collective-permute-start.29 = (bf16[4,64,128]{2,1,0:T(8,128)(2,1)S(1)}, bf16[4,64,128]{2,1,0:T(8,128)(2,1)S(1)}, u32[]{:S(2)}, u32[]{:S(2)}) collective-permute-start(bf16[4,64,128]{2,1,0:T(8,128)(2,1)S(1)} %get-tuple-element.165), channel_id=1, source_target_pairs={{0,6},{1,7},{2,4},{3,5},{4,2},{5,3},{6,0},{7,1},{8,14},{9,15},{10,... | collective-permute-start | bytes 196616 | tf_op jit(solution)/shard_map/ppermute | solution.py:68
  90.2 6.6 %collective-permute-start.30 = (bf16[4,64,128]{2,1,0:T(8,128)(2,1)S(1)}, bf16[4,64,128]{2,1,0:T(8,128)(2,1)S(1)}, u32[]{:S(2)}, u32[]{:S(2)}) collective-permute-start(bf16[4,64,128]{2,1,0:T(8,128)(2,1)S(1)} %get-tuple-element.168), channel_id=1, source_target_pairs={{0,4},{1,5},{2,6},{3,7},{4,0},{5,1},{6,2},{7,3},{8,12},{9,13},{10,... | collective-permute-start | bytes 196616 | tf_op jit(solution)/shard_map/ppermute | solution.py:68
  91.0 5.8 %collective-permute-start.31 = (bf16[4,64,128]{2,1,0:T(8,128)(2,1)S(1)}, bf16[4,64,128]{2,1,0:T(8,128)(2,1)S(1)}, u32[]{:S(2)}, u32[]{:S(2)}) collective-permute-start(bf16[4,64,128]{2,1,0:T(8,128)(2,1)S(1)} %get-tuple-element.169), channel_id=1, source_target_pairs={{0,2},{1,3},{2,0},{3,1},{4,6},{5,7},{6,4},{7,5},{8,10},{9,11},{10,... | collective-permute-start | bytes 196616 | tf_op jit(solution)/shard_map/ppermute | solution.py:68
  97.0 6.6 %collective-permute-start.34 = (bf16[4,64,128]{2,1,0:T(8,128)(2,1)S(1)}, bf16[4,64,128]{2,1,0:T(8,128)(2,1)S(1)}, u32[]{:S(2)}, u32[]{:S(2)}) collective-permute-start(bf16[4,64,128]{2,1,0:T(8,128)(2,1)S(1)} %get-tuple-element.180), channel_id=1, source_target_pairs={{0,6},{1,7},{2,4},{3,5},{4,2},{5,3},{6,0},{7,1},{8,14},{9,15},{10,... | collective-permute-start | bytes 196616 | tf_op jit(solution)/shard_map/ppermute | solution.py:68
  100.1 5.2 %collective-permute-start.35 = (bf16[4,64,128]{2,1,0:T(8,128)(2,1)S(1)}, bf16[4,64,128]{2,1,0:T(8,128)(2,1)S(1)}, u32[]{:S(2)}, u32[]{:S(2)}) collective-permute-start(bf16[4,64,128]{2,1,0:T(8,128)(2,1)S(1)} %add_convert_fusion.1), channel_id=1, source_target_pairs={{0,17},{1,16},{2,19},{3,18},{4,21},{5,20},{6,23},{7,22},{8,25},{9,... | collective-permute-start | bytes 196616 | tf_op jit(solution)/shard_map/ppermute | solution.py:68
  100.1 6.7 %collective-permute-start.36 = (bf16[4,64,128]{2,1,0:T(8,128)(2,1)S(1)}, bf16[4,64,128]{2,1,0:T(8,128)(2,1)S(1)}, u32[]{:S(2)}, u32[]{:S(2)}) collective-permute-start(bf16[4,64,128]{2,1,0:T(8,128)(2,1)S(1)} %get-tuple-element.184), channel_id=1, source_target_pairs={{0,4},{1,5},{2,6},{3,7},{4,0},{5,1},{6,2},{7,3},{8,12},{9,13},{10,... | collective-permute-start | bytes 196616 | tf_op jit(solution)/shard_map/ppermute | solution.py:68
  100.1 7.0 %collective-permute-start.37 = (bf16[4,64,128]{2,1,0:T(8,128)(2,1)S(1)}, bf16[4,64,128]{2,1,0:T(8,128)(2,1)S(1)}, u32[]{:S(2)}, u32[]{:S(2)}) collective-permute-start(bf16[4,64,128]{2,1,0:T(8,128)(2,1)S(1)} %get-tuple-element.185), channel_id=1, source_target_pairs={{0,2},{1,3},{2,0},{3,1},{4,6},{5,7},{6,4},{7,5},{8,10},{9,11},{10,... | collective-permute-start | bytes 196616 | tf_op jit(solution)/shard_map/ppermute | solution.py:68
  107.3 6.8 %collective-permute-start.38 = (bf16[4,64,128]{2,1,0:T(8,128)(2,1)S(1)}, bf16[4,64,128]{2,1,0:T(8,128)(2,1)S(1)}, u32[]{:S(2)}, u32[]{:S(2)}) collective-permute-start(bf16[4,64,128]{2,1,0:T(8,128)(2,1)S(1)} %get-tuple-element.226), channel_id=1, source_target_pairs={{0,6},{1,7},{2,4},{3,5},{4,2},{5,3},{6,0},{7,1},{8,14},{9,15},{10,... | collective-permute-start | bytes 196616 | tf_op jit(solution)/shard_map/ppermute | solution.py:68
  111.2 5.5 %collective-permute-start.40 = (bf16[4,64,128]{2,1,0:T(8,128)(2,1)S(1)}, bf16[4,64,128]{2,1,0:T(8,128)(2,1)S(1)}, u32[]{:S(2)}, u32[]{:S(2)}) collective-permute-start(bf16[4,64,128]{2,1,0:T(8,128)(2,1)S(1)} %get-tuple-element.226), channel_id=1, source_target_pairs={{0,4},{1,5},{2,6},{3,7},{4,0},{5,1},{6,2},{7,3},{8,12},{9,13},{10,... | collective-permute-start | bytes 196616 | tf_op jit(solution)/shard_map/ppermute | solution.py:68
  111.2 5.5 %collective-permute-start.41 = (bf16[4,64,128]{2,1,0:T(8,128)(2,1)S(1)}, bf16[4,64,128]{2,1,0:T(8,128)(2,1)S(1)}, u32[]{:S(2)}, u32[]{:S(2)}) collective-permute-start(bf16[4,64,128]{2,1,0:T(8,128)(2,1)S(1)} %get-tuple-element.226), channel_id=1, source_target_pairs={{0,2},{1,3},{2,0},{3,1},{4,6},{5,7},{6,4},{7,5},{8,10},{9,11},{10,... | collective-permute-start | bytes 196616 | tf_op jit(solution)/shard_map/ppermute | solution.py:68
  116.7 12.1 %collective-permute-start.45 = (bf16[16,64,128]{2,1,0:T(8,128)(2,1)S(1)}, bf16[16,64,128]{2,1,0:T(8,128)(2,1)S(1)}, u32[]{:S(2)}, u32[]{:S(2)}) collective-permute-start(bf16[16,64,128]{2,1,0:T(8,128)(2,1)S(1)} %pad_maximum_fusion.4.field), channel_id=1, source_target_pairs={{0,1},{1,0},{2,3},{3,2},{4,5},{5,4},{6,7},{7,6},{8,24},{9,25},{10,... | collective-permute-start | bytes 786440 | tf_op jit(solution)/shard_map/ppermute | solution.py:68
  117.9 10.8 %collective-permute-start.46 = (bf16[16,64,128]{2,1,0:T(8,128)(2,1)S(1)}, bf16[16,64,128]{2,1,0:T(8,128)(2,1)S(1)}, u32[]{:S(2)}, u32[]{:S(2)}) collective-permute-start(bf16[16,64,128]{2,1,0:T(8,128)(2,1)S(1)} %pad_maximum_fusion.4.field), channel_id=1, source_target_pairs={{0,16},{1,17},{2,18},{3,19},{4,20},{5,21},{6,22},{7,23},{8,9},{9,8... | collective-permute-start | bytes 786440 | tf_op jit(solution)/shard_map/ppermute | solution.py:68
  119.1 9.6 %collective-permute-start.42 = (bf16[4,64,128]{2,1,0:T(8,128)(2,1)S(1)}, bf16[4,64,128]{2,1,0:T(8,128)(2,1)S(1)}, u32[]{:S(2)}, u32[]{:S(2)}) collective-permute-start(bf16[4,64,128]{2,1,0:T(8,128)(2,1)S(1)} %collective-permute-done.39), channel_id=1, source_target_pairs={{0,6},{1,7},{2,4},{3,5},{4,2},{5,3},{6,0},{7,1},{8,14},{9,15},{10,... | collective-permute-start | bytes 196616 | tf_op jit(solution)/shard_map/ppermute | solution.py:68
  121.3 7.4 %collective-permute-start.43 = (bf16[4,64,128]{2,1,0:T(8,128)(2,1)S(1)}, bf16[4,64,128]{2,1,0:T(8,128)(2,1)S(1)}, u32[]{:S(2)}, u32[]{:S(2)}) collective-permute-start(bf16[4,64,128]{2,1,0:T(8,128)(2,1)S(1)} %collective-permute-done.39), channel_id=1, source_target_pairs={{0,4},{1,5},{2,6},{3,7},{4,0},{5,1},{6,2},{7,3},{8,12},{9,13},{10,... | collective-permute-start | bytes 196616 | tf_op jit(solution)/shard_map/ppermute | solution.py:68
  121.3 7.4 %collective-permute-start.44 = (bf16[4,64,128]{2,1,0:T(8,128)(2,1)S(1)}, bf16[4,64,128]{2,1,0:T(8,128)(2,1)S(1)}, u32[]{:S(2)}, u32[]{:S(2)}) collective-permute-start(bf16[4,64,128]{2,1,0:T(8,128)(2,1)S(1)} %collective-permute-done.39), channel_id=1, source_target_pairs={{0,2},{1,3},{2,0},{3,1},{4,6},{5,7},{6,4},{7,5},{8,10},{9,11},{10,... | collective-permute-start | bytes 196616 | tf_op jit(solution)/shard_map/ppermute | solution.py:68
  135.4 9.4 %collective-permute-start.50 = (bf16[16,64,128]{2,1,0:T(8,128)(2,1)S(1)}, bf16[16,64,128]{2,1,0:T(8,128)(2,1)S(1)}, u32[]{:S(2)}, u32[]{:S(2)}) collective-permute-start(bf16[16,64,128]{2,1,0:T(8,128)(2,1)S(1)} %get-tuple-element.207), channel_id=1, source_target_pairs={{0,1},{1,0},{2,3},{3,2},{4,5},{5,4},{6,7},{7,6},{8,24},{9,25},{10,... | collective-permute-start | bytes 786440 | tf_op jit(solution)/shard_map/ppermute | solution.py:68
  136.1 8.7 %collective-permute-start.51 = (bf16[16,64,128]{2,1,0:T(8,128)(2,1)S(1)}, bf16[16,64,128]{2,1,0:T(8,128)(2,1)S(1)}, u32[]{:S(2)}, u32[]{:S(2)}) collective-permute-start(bf16[16,64,128]{2,1,0:T(8,128)(2,1)S(1)} %get-tuple-element.208), channel_id=1, source_target_pairs={{0,16},{1,17},{2,18},{3,19},{4,20},{5,21},{6,22},{7,23},{8,9},{9,8... | collective-permute-start | bytes 786440 | tf_op jit(solution)/shard_map/ppermute | solution.py:68
  136.4 6.1 %collective-permute-start.47 = (bf16[4,64,128]{2,1,0:T(8,128)(2,1)S(1)}, bf16[4,64,128]{2,1,0:T(8,128)(2,1)S(1)}, u32[]{:S(2)}, u32[]{:S(2)}) collective-permute-start(bf16[4,64,128]{2,1,0:T(8,128)(2,1)S(1)} %get-tuple-element.202), channel_id=1, source_target_pairs={{0,6},{1,7},{2,4},{3,5},{4,2},{5,3},{6,0},{7,1},{8,14},{9,15},{10,... | collective-permute-start | bytes 196616 | tf_op jit(solution)/shard_map/ppermute | solution.py:68
  145.0 6.3 %collective-permute-start.52 = (bf16[4,64,128]{2,1,0:T(8,128)(2,1)S(1)}, bf16[4,64,128]{2,1,0:T(8,128)(2,1)S(1)}, u32[]{:S(2)}, u32[]{:S(2)}) collective-permute-start(bf16[4,64,128]{2,1,0:T(8,128)(2,1)S(1)} %get-tuple-element.217), channel_id=1, source_target_pairs={{0,6},{1,7},{2,4},{3,5},{4,2},{5,3},{6,0},{7,1},{8,14},{9,15},{10,... | collective-permute-start | bytes 196616 | tf_op jit(solution)/shard_map/ppermute | solution.py:68
  148.3 5.6 %collective-permute-start.54 = (bf16[4,64,128]{2,1,0:T(8,128)(2,1)S(1)}, bf16[4,64,128]{2,1,0:T(8,128)(2,1)S(1)}, u32[]{:S(2)}, u32[]{:S(2)}) collective-permute-start(bf16[4,64,128]{2,1,0:T(8,128)(2,1)S(1)} %get-tuple-element.221), channel_id=1, source_target_pairs={{0,4},{1,5},{2,6},{3,7},{4,0},{5,1},{6,2},{7,3},{8,12},{9,13},{10,... | collective-permute-start | bytes 196616 | tf_op jit(solution)/shard_map/ppermute | solution.py:68
  (13 other events, 108.6 us)
